TPU v7x, 32 devices: a whole 2x2x4 slice. The times are simulated.
32 devices in a mesh: clips: 16 (over z, y, x), tm: 2 (over core).
Axes of the slice: x: 2, y: 2, z: 4, core: 2. Of those that a mesh axis runs over, the one named last changes fastest.
Arguments:
- tokens: bfloat16 [100352, 384], P(('clips', 'tm')), may hold values from -6 to 6
- frame_clip: int32 [512], P('clips'), may hold values from 0 to 47, as said below
- ln1_gain: bfloat16 [384], replicated, may hold values from 0.25 to 1.75
- ln1_bias: bfloat16 [384], replicated, may hold values from -1 to 1
- w_qkv: bfloat16 [384, 1152], replicated, may hold values from -0.4375 to 0.4375
- qv_bias: bfloat16 [2, 384], replicated, may hold values from -1 to 1
- w_out: bfloat16 [384, 384], replicated, may hold values from -1.75 to 1.75
- b_out: bfloat16 [384], replicated, may hold values from -1 to 1
- ln2_gain: bfloat16 [384], replicated, may hold values from 0.25 to 1.75
- ln2_bias: bfloat16 [384], replicated, may hold values from -1 to 1
- w_fc1: bfloat16 [384, 1536], replicated, may hold values from -0.3125 to 0.3125
- b_fc1: bfloat16 [1536], replicated, may hold values from -1.5 to 1.5
- w_fc2: bfloat16 [1536, 384], replicated, may hold values from -0.3125 to 0.3125
- b_fc2: bfloat16 [384], replicated, may hold values from -1 to 1
- cotangent: bfloat16 [100352, 384], P(('clips', 'tm')), may hold values from -6 to 6
Outputs:
- block_out: bfloat16 [100352, 384], P(('clips', 'tm'))
- input_grad: float32 [100352, 384], P(('clips', 'tm'))
- grad_ln1_gain: float32 [384], replicated
- grad_ln1_bias: float32 [384], replicated
- grad_w_qkv: float32 [384, 1152], replicated
- grad_qv_bias: float32 [2, 384], replicated
- grad_w_out: float32 [384, 384], replicated
- grad_b_out: float32 [384], replicated
- grad_ln2_gain: float32 [384], replicated
- grad_ln2_bias: float32 [384], replicated
- grad_w_fc1: float32 [384, 1536], replicated
- grad_b_fc1: float32 [1536], replicated
- grad_w_fc2: float32 [1536, 384], replicated
- grad_b_fc2: float32 [384], replicated
Inputs may be any that keep to these rules, and one draw needn't show every extreme that they name: `frame_clip`: clip numbers never fall along the frames; frames of different groups of 32 frames carry different numbers; in every group one clip runs from inside its first 16 frames into its last 16 frames.
All inputs are finite; a program needn't handle non-finite values.
Results may differ from a plain program's by a relative error of at most 0.012.
The roundings to bfloat16 on the way count: a program that leaves them out, or rounds other values in their place, can miss the bound.
Values may be sent and summed in bfloat16 or wider, within the bound.
A program may use at most 192 MiB of HBM per device.

v0:
```python
import math

import jax
import jax.numpy as jnp
from jax import lax
from jax.sharding import PartitionSpec as P

HEADS = 6
FRAME = 196


norm_eps = 1e-06
masked_score = -1e30


def padded(x, sides, width):
    for axis, dim in sides:
        count, length = (lax.axis_size(axis), x.shape[dim])
        up = [(i, (i + 1) % count) for i in range(count - 1)]
        down = [(j, i) for i, j in up]
        last = lax.slice_in_dim(x, length - width, length, axis=dim)
        leading = lax.slice_in_dim(x, 0, width, axis=dim)
        before = lax.ppermute(last, axis, up)
        after = lax.ppermute(leading, axis, down)
        x = jnp.concatenate([before, x, after], axis=dim)
    return x


def norm_forward(values, gain_vec, shift_vec):
    row_mean = jnp.mean(values, axis=-1, keepdims=True)
    centred = values - row_mean
    variance = jnp.mean(centred * centred, axis=-1, keepdims=True)
    inverse = lax.rsqrt(variance + norm_eps)
    normed = centred * inverse
    return (normed * gain_vec + shift_vec, normed, inverse)


def norm_backward(upstream, normed, inverse, gain_vec):
    scaled = upstream * gain_vec
    scaled_mean = jnp.mean(scaled, axis=-1, keepdims=True)
    along_mean = jnp.mean(scaled * normed, axis=-1, keepdims=True)
    back_grad = inverse * (scaled - scaled_mean - normed * along_mean)
    return (back_grad, jnp.sum(upstream * normed, axis=0), jnp.sum(upstream, axis=0))


def cross(left_arr, right_arr):
    return lax.dot_general(
        left_arr, right_arr, (((0,), (0,)), ((), ())), preferred_element_type=jnp.float32
    )


def back_through(upstream, weight):
    return lax.dot_general(
        upstream, weight, (((1,), (1,)), ((), ())), preferred_element_type=jnp.float32
    )


def frame_windows(extended, start_frame, frame_count):
    window = lax.dynamic_slice_in_dim(extended, start_frame, frame_count + 2, 0)
    return jnp.concatenate([window[:-2], window[1:-1], window[2:]], axis=1)


def head_split(values):
    return values.reshape(values.shape[0], values.shape[1], HEADS, values.shape[2] // HEADS)


def block_scores(query_heads, key_heads, allowed):
    score_scale = 1.0 / math.sqrt(query_heads.shape[3])
    scores = (
        jnp.einsum("bihd,bjhd->bhij", query_heads, key_heads, preferred_element_type=jnp.float32)
        * score_scale
    )
    return (jnp.where(allowed[:, None, None, :], scores, masked_score), score_scale)


def per_device(
    tokens,
    frame_clip,
    ln1_gain,
    ln1_bias,
    w_qkv,
    qv_bias,
    w_out,
    b_out,
    ln2_gain,
    ln2_bias,
    w_fc1,
    b_fc1,
    w_fc2,
    b_fc2,
    cotangent,
):
    tok_count, feat_width = tokens.shape
    frames = tok_count // FRAME
    per_block = math.gcd(frames, 4)
    n_blocks = frames // per_block
    inputs = tokens.astype(jnp.float32)
    gain_one = ln1_gain.astype(jnp.float32)
    shift_one = ln1_bias.astype(jnp.float32)
    gain_two = ln2_gain.astype(jnp.float32)
    shift_two = ln2_bias.astype(jnp.float32)
    bias_qkv = jnp.concatenate(
        [
            qv_bias[0].astype(jnp.float32),
            jnp.zeros((feat_width,), jnp.float32),
            qv_bias[1].astype(jnp.float32),
        ]
    )
    bias_out = b_out.astype(jnp.float32)
    bias_up = b_fc1.astype(jnp.float32)
    bias_down = b_fc2.astype(jnp.float32)
    tm_index = lax.axis_index("tm")
    edge_ids = jnp.full((1,), -1, jnp.int32)
    padded_ids = jnp.concatenate([edge_ids, frame_clip, edge_ids])
    ext_ids = lax.dynamic_slice_in_dim(padded_ids, tm_index * frames, frames + 2)
    own_ids = ext_ids[1:-1]
    frame_ok = jnp.stack(
        [ext_ids[:-2] == own_ids, own_ids == own_ids, ext_ids[2:] == own_ids], axis=1
    )
    key_ok = jnp.repeat(frame_ok, FRAME, axis=1)
    attn_in, attn_hat, attn_inv = norm_forward(inputs, gain_one, shift_one)
    attn_in_bf = attn_in.astype(jnp.bfloat16)
    qkv_bf = (jnp.dot(attn_in_bf, w_qkv, preferred_element_type=jnp.float32) + bias_qkv).astype(
        jnp.bfloat16
    )
    attn_in_bf, attn_hat, attn_inv, qkv_bf = (
        attn_in_bf,
        attn_hat,
        attn_inv,
        qkv_bf.reshape(frames, FRAME, 3 * feat_width),
    )
    kv_ext = padded(qkv_bf[..., feat_width:], (("tm", 0),), 1)
    attend_queries = qkv_bf[..., :feat_width]

    def one_block(block_idx):
        block_start = block_idx * per_block
        q_blk = head_split(lax.dynamic_slice_in_dim(attend_queries, block_start, per_block, 0))
        kv_blk = frame_windows(kv_ext, block_start, per_block)
        ok_blk = lax.dynamic_slice_in_dim(key_ok, block_start, per_block, 0)
        scores, score_scale = block_scores(q_blk, head_split(kv_blk[..., :feat_width]), ok_blk)
        row_max = jnp.max(scores, axis=-1, keepdims=True)
        powered = jnp.exp(scores - row_max)
        row_total = jnp.sum(powered, axis=-1, keepdims=True)
        prob_bf = (powered / row_total).astype(jnp.bfloat16)
        attended = jnp.einsum(
            "bhij,bjhd->bihd",
            prob_bf,
            head_split(kv_blk[..., feat_width:]),
            preferred_element_type=jnp.float32,
        )
        return (
            attended.reshape(per_block, FRAME, feat_width),
            (row_max + jnp.log(row_total))[..., 0],
        )

    attended, attend_log_sums = lax.map(one_block, jnp.arange(n_blocks))
    attended, log_sums = (
        attended.reshape(frames, FRAME, feat_width),
        attend_log_sums.reshape(frames, HEADS, FRAME),
    )
    attended_bf = attended.astype(jnp.bfloat16).reshape(tok_count, feat_width)
    resid = inputs + jnp.dot(attended_bf, w_out, preferred_element_type=jnp.float32) + bias_out
    mlp_in, mlp_hat, mlp_inv = norm_forward(resid, gain_two, shift_two)
    mlp_in_bf = mlp_in.astype(jnp.bfloat16)
    pre_act = jnp.dot(mlp_in_bf, w_fc1, preferred_element_type=jnp.float32) + bias_up
    attended_bf, resid, mlp_in_bf, mlp_hat, mlp_inv, pre_act = (
        attended_bf,
        resid,
        mlp_in_bf,
        mlp_hat,
        mlp_inv,
        pre_act,
    )
    hidden_bf = jax.nn.gelu(pre_act, approximate=False).astype(jnp.bfloat16)
    block_out = (
        resid + jnp.dot(hidden_bf, w_fc2, preferred_element_type=jnp.float32) + bias_down
    ).astype(jnp.bfloat16)
    grad_out = cotangent.astype(jnp.float32)
    g_b_fc2 = jnp.sum(grad_out, axis=0)
    g_w_fc2 = cross(hidden_bf, cotangent)
    grad_hidden = back_through(cotangent, w_fc2)
    cumulative = 0.5 * (1.0 + lax.erf(pre_act / math.sqrt(2.0)))
    density = jnp.exp(-0.5 * pre_act * pre_act) / math.sqrt(2.0 * math.pi)
    grad_pre_bf = (grad_hidden * (cumulative + pre_act * density)).astype(jnp.bfloat16)
    g_b_fc1 = jnp.sum(grad_pre_bf, axis=0, dtype=jnp.float32)
    g_w_fc1 = cross(mlp_in_bf, grad_pre_bf)
    back_mlp, g_ln2_gain, g_ln2_bias = norm_backward(
        back_through(grad_pre_bf, w_fc1), mlp_hat, mlp_inv, gain_two
    )
    grad_resid = grad_out + back_mlp
    grad_branch_bf = grad_resid.astype(jnp.bfloat16)
    g_b_out = jnp.sum(grad_branch_bf, axis=0, dtype=jnp.float32)
    g_w_out = cross(attended_bf, grad_branch_bf)
    grad_att_bf = (
        back_through(grad_branch_bf, w_out).astype(jnp.bfloat16).reshape(frames, FRAME, feat_width)
    )
    queries = qkv_bf[..., :feat_width]

    def back_block(grad_acc, block_idx):
        block_start = block_idx * per_block
        q_blk = head_split(lax.dynamic_slice_in_dim(queries, block_start, per_block, 0))
        kv_blk = frame_windows(kv_ext, block_start, per_block)
        ok_blk = lax.dynamic_slice_in_dim(key_ok, block_start, per_block, 0)
        sums_blk = lax.dynamic_slice_in_dim(log_sums, block_start, per_block, 0)
        grad_heads = head_split(lax.dynamic_slice_in_dim(grad_att_bf, block_start, per_block, 0))
        key_heads = head_split(kv_blk[..., :feat_width])
        value_heads = head_split(kv_blk[..., feat_width:])
        scores, score_scale = block_scores(q_blk, key_heads, ok_blk)
        prob_vals = jnp.exp(scores - sums_blk[..., None])
        grad_probs = jnp.einsum(
            "bihd,bjhd->bhij", grad_heads, value_heads, preferred_element_type=jnp.float32
        )
        grad_values = jnp.einsum(
            "bhij,bihd->bjhd",
            prob_vals.astype(jnp.bfloat16),
            grad_heads,
            preferred_element_type=jnp.float32,
        )
        row_dot = jnp.sum(prob_vals * grad_probs, axis=-1, keepdims=True)
        grad_scores = (prob_vals * (grad_probs - row_dot)).astype(jnp.bfloat16)
        grad_queries = (
            jnp.einsum(
                "bhij,bjhd->bihd", grad_scores, key_heads, preferred_element_type=jnp.float32
            )
            * score_scale
        )
        grad_keys = (
            jnp.einsum("bhij,bihd->bjhd", grad_scores, q_blk, preferred_element_type=jnp.float32)
            * score_scale
        )
        grad_window = jnp.concatenate(
            [
                grad_keys.reshape(per_block, 3 * FRAME, feat_width),
                grad_values.reshape(per_block, 3 * FRAME, feat_width),
            ],
            axis=-1,
        )
        folded = jnp.pad(grad_window[:, :FRAME], ((0, 2), (0, 0), (0, 0)))
        folded = folded + jnp.pad(grad_window[:, FRAME : 2 * FRAME], ((1, 1), (0, 0), (0, 0)))
        folded = folded + jnp.pad(grad_window[:, 2 * FRAME :], ((2, 0), (0, 0), (0, 0)))
        current = lax.dynamic_slice_in_dim(grad_acc, block_start, per_block + 2, 0)
        grad_acc = lax.dynamic_update_slice_in_dim(grad_acc, current + folded, block_start, 0)
        return (grad_acc, grad_queries.reshape(per_block, FRAME, feat_width))

    empty_ext = jnp.zeros((frames + 2, FRAME, 2 * feat_width), jnp.float32)
    grad_kv_ext, grad_q = lax.scan(back_block, empty_ext, jnp.arange(n_blocks))
    grad_q = grad_q.reshape(frames, FRAME, feat_width)
    rim_pair = jnp.stack([grad_kv_ext[0], grad_kv_ext[-1]])
    rim_back = padded(rim_pair.astype(jnp.bfloat16), (("tm", 0),), 1).astype(rim_pair.dtype)
    grad_kv = grad_kv_ext[1:-1]
    grad_kv = grad_kv.at[0].add(rim_back[0]).at[-1].add(rim_back[3])
    grad_qkv_bf = (
        jnp.concatenate([grad_q, grad_kv], axis=-1)
        .astype(jnp.bfloat16)
        .reshape(tok_count, 3 * feat_width)
    )
    column_sums = jnp.sum(grad_qkv_bf, axis=0, dtype=jnp.float32)
    g_qv_bias = jnp.stack([column_sums[:feat_width], column_sums[2 * feat_width :]])
    g_w_qkv = cross(attn_in_bf, grad_qkv_bf)
    back_attn, g_ln1_gain, g_ln1_bias = norm_backward(
        back_through(grad_qkv_bf, w_qkv), attn_hat, attn_inv, gain_one
    )
    input_grad = grad_resid + back_attn
    (
        g_ln1_gain,
        g_ln1_bias,
        g_w_qkv,
        g_qv_bias,
        g_w_out,
        g_b_out,
        g_ln2_gain,
        g_ln2_bias,
        g_w_fc1,
        g_b_fc1,
        g_w_fc2,
        g_b_fc2,
    ) = lax.psum(
        (
            g_ln1_gain,
            g_ln1_bias,
            g_w_qkv,
            g_qv_bias,
            g_w_out,
            g_b_out,
            g_ln2_gain,
            g_ln2_bias,
            g_w_fc1,
            g_b_fc1,
            g_w_fc2,
            g_b_fc2,
        ),
        ("clips", "tm"),
    )
    return (
        block_out,
        input_grad,
        g_ln1_gain,
        g_ln1_bias,
        g_w_qkv,
        g_qv_bias,
        g_w_out,
        g_b_out,
        g_ln2_gain,
        g_ln2_bias,
        g_w_fc1,
        g_b_fc1,
        g_w_fc2,
        g_b_fc2,
    )


def solution(mesh):
    return jax.shard_map(
        per_device,
        mesh=mesh,
        in_specs=(
            P(("clips", "tm"), None),
            P("clips"),
            P(),
            P(),
            P(),
            P(),
            P(),
            P(),
            P(),
            P(),
            P(),
            P(),
            P(),
            P(),
            P(("clips", "tm"), None),
        ),
        out_specs=(
            P(("clips", "tm"), None),
            P(("clips", "tm"), None),
            P(),
            P(),
            P(),
            P(),
            P(),
            P(),
            P(),
            P(),
            P(),
            P(),
            P(),
            P(),
        ),
        check_vma=False,
    )
```

profile of v0, /device:TPU:0, one launch (start us, length us, event | category | flops | bytes accessed | tf_op | source)
XLA Modules:
  0.0 786.0 jit_solution(9921535305908239948)
XLA Ops:
  22.6 8.8 %reshape.241 = bf16[16,196,1152]{2,1,0:T(8,128)(2,1)} reshape(bf16[3136,1152]{1,0:T(8,128)(2,1)} %fusion.35) | data formatting | bytes 14450688 | tf_op jit(solution)/shard_map/reshape | solution.py:130
  58.9 9.1 %copy.57 = bf16[18,196,768]{1,2,0:T(8,128)(2,1)} copy(bf16[18,196,768]{2,1,0:T(8,128)(2,1)} %pad_maximum_fusion.2) | data formatting | bytes 10838016 | tf_op jit(solution)/shard_map/while | solution.py:156
  70.0 77.8 %while.28 = (s32[]{:T(128)}, bf16[4,4,196,384]{2,3,1,0:T(8,128)(2,1)}, f32[4,4,6,196]{3,2,1,0:T(8,128)S(1)}, s32[4]{0:T(128)S(1)}, bf16[18,196,768]{1,2,0:T(8,12...) while((s32[]{:T(128)}, ...), condition=%wide.region_5.6_spmd, body=%wide.region_2.5_spmd.sunk | while | flops 752108416 | bytes 62481540 | solution.py:156
  162.0 48.4 %fusion.21 = (bf16[3136,1536]{1,0:T(8,128)(2,1)}, f32[3136,1536]{1,0:T(8,128)}) fusion(f32[1536]{0:T(1024)S(1)} %copy-done.28, bf16[384,1536]{1,0:T(8,128)(2,1)S(1)} %copy-done, f32[3136,384]{1,0:T(8,128)S(1)} %get-tuple-element.333, f32[384]{0:T(512)S(1)} %copy-done.35, f32[384]{0:T(512)S(1)} %copy-done.26, f32[3136]{0:T(1024)S(1)} %add_rsqrt_fusion, ...), kind=kOutput, calls=%fused_computation.54 | convolution fusion | flops 4023312384 | bytes 34932224 | tf_op jit(solution)/shard_map/dot_general | solution.py:165
  210.5 15.9 %convert_reduce_fusion = (f32[1536]{0:T(1024)}, bf16[3136,1536]{1,0:T(8,128)(2,1)S(1)}) fusion(f32[3136,1536]{1,0:T(8,128)} %get-tuple-element.335, f32[1536]{0:T(1024)S(1)} %copy-done.28, bf16[3136,384]{1,0:T(8,128)(2,1)S(1)} %copy-done.9, bf16[1536,384]{1,0:T(8,128)(2,1)S(1)} %copy-done.40), kind=kOutput, calls=%fused_computation.61 | convolution fusion | flops 3761994240 | bytes 32501760 | tf_op jit(solution)/shard_map/dot_general | solution.py:53
  260.1 198.6 %while.29 = (s32[]{:T(128)}, f32[18,196,768]{1,2,0:T(8,128)}, bf16[4,4,196,384]{2,3,1,0:T(8,128)(2,1)}, s32[4]{0:T(128)S(1)}, bf16[16,196,384]{1,2,0:T(8,128)(2,...) while((s32[]{:T(128)}, f32[18,196,768]{1,2,0:T(8,128)}, ...), condition=%wide.region_12.13_spmd, body=%wide.region_10.12_spmd.sunk | while | flops 1831563520 | bytes 174483632 | solution.py:246
  278.4 8.4 %multiply_reduce_fusion.7 = (f32[4,6,196]{2,1,0:T(8,128)S(1)}, f32[4,6,196,588]{3,2,1,0:T(8,128)}) fusion(f32[4,6,196,588]{3,2,1,0:T(8,128)S(1)} %fusion.142, f32[4,6,196]{2,1,0:T(8,128)S(1)} %constant_dynamic-slice_fusion.26, pred[4,588]{1,0:T(4,128)(4,1)S(1)} %constant_dynamic-slice_fusion.27, bf16[4,196,6,64]{1,3,2,0:T(8,128)(2,1)S(1)} %bitcast.123, ...), kind=kOutput, calls=%fused_computation.17.clone.1 | convolution fusion | flops 367866912 | bytes 24576048 | tf_op jit(solution)/shard_map/while/body/eval_jaxpr/bihd,bjhd->bhij/dot_general | solution.py:210
  328.0 8.4 %multiply_reduce_fusion.7 = (f32[4,6,196]{2,1,0:T(8,128)S(1)}, f32[4,6,196,588]{3,2,1,0:T(8,128)}) fusion(f32[4,6,196,588]{3,2,1,0:T(8,128)S(1)} %fusion.142, f32[4,6,196]{2,1,0:T(8,128)S(1)} %constant_dynamic-slice_fusion.26, pred[4,588]{1,0:T(4,128)(4,1)S(1)} %constant_dynamic-slice_fusion.27, bf16[4,196,6,64]{1,3,2,0:T(8,128)(2,1)S(1)} %bitcast.123, ...), kind=kOutput, calls=%fused_computation.17.clone.1 | convolution fusion | flops 367866912 | bytes 24576048 | tf_op jit(solution)/shard_map/while/body/eval_jaxpr/bihd,bjhd->bhij/dot_general | solution.py:210
  352.1 7.3 fusion.145
  377.5 8.4 %multiply_reduce_fusion.7 = (f32[4,6,196]{2,1,0:T(8,128)S(1)}, f32[4,6,196,588]{3,2,1,0:T(8,128)}) fusion(f32[4,6,196,588]{3,2,1,0:T(8,128)S(1)} %fusion.142, f32[4,6,196]{2,1,0:T(8,128)S(1)} %constant_dynamic-slice_fusion.26, pred[4,588]{1,0:T(4,128)(4,1)S(1)} %constant_dynamic-slice_fusion.27, bf16[4,196,6,64]{1,3,2,0:T(8,128)(2,1)S(1)} %bitcast.123, ...), kind=kOutput, calls=%fused_computation.17.clone.1 | convolution fusion | flops 367866912 | bytes 24576048 | tf_op jit(solution)/shard_map/while/body/eval_jaxpr/bihd,bjhd->bhij/dot_general | solution.py:210
  427.2 8.4 %multiply_reduce_fusion.7 = (f32[4,6,196]{2,1,0:T(8,128)S(1)}, f32[4,6,196,588]{3,2,1,0:T(8,128)}) fusion(f32[4,6,196,588]{3,2,1,0:T(8,128)S(1)} %fusion.142, f32[4,6,196]{2,1,0:T(8,128)S(1)} %constant_dynamic-slice_fusion.26, pred[4,588]{1,0:T(4,128)(4,1)S(1)} %constant_dynamic-slice_fusion.27, bf16[4,196,6,64]{1,3,2,0:T(8,128)(2,1)S(1)} %bitcast.123, ...), kind=kOutput, calls=%fused_computation.17.clone.1 | convolution fusion | flops 367866912 | bytes 24576048 | tf_op jit(solution)/shard_map/while/body/eval_jaxpr/bihd,bjhd->bhij/dot_general | solution.py:210
  451.3 7.2 fusion.145
  459.9 16.0 %copy.64 = f32[18,196,768]{2,0,1:T(8,128)} copy(f32[18,196,768]{1,2,0:T(8,128)} %get-tuple-element.193) | data formatting | bytes 21676032 | tf_op jit(solution)/shard_map/while | solution.py:246
  475.9 8.8 %convert.17 = bf16[18,196,768]{2,0,1:T(8,128)(2,1)} convert(f32[18,196,768]{2,0,1:T(8,128)} %copy.64) | non-fusion elementwise | flops 2709504 | bytes 16257024 | tf_op jit(solution)/shard_map/convert.8
  484.7 10.4 %slice.193 = f32[16,196,768]{2,0,1:T(8,128)} slice(f32[18,196,768]{2,0,1:T(8,128)} %copy.64), slice={[1:17], [0:196], [0:768]} | slice | bytes 19267584 | tf_op jit(solution)/shard_map/slice | solution.py:250
  495.1 9.9 %fusion.70 = f32[1536,384]{1,0:T(8,128)} fusion(bf16[3136,1536]{1,0:T(8,128)(2,1)} %get-tuple-element.334, bf16[3136,384]{1,0:T(8,128)(2,1)} %param.37), kind=kOutput, calls=%fused_computation.149 | convolution fusion | flops 3699376128 | bytes 14401536 | tf_op jit(solution)/shard_map/dot_general | solution.py:47
  505.0 10.1 %fusion.44 = bf16[3136,384]{1,0:T(8,128)(2,1)} fusion(f32[3136,384]{1,0:T(8,128)S(1)} %bitcast.129, bf16[3136,1536]{1,0:T(8,128)(2,1)} %get-tuple-element.334, bf16[1536,384]{1,0:T(8,128)(2,1)S(1)} %copy-done.41, f32[384]{0:T(512)S(1)} %copy-done.34), kind=kOutput, calls=%fused_computation.95 | convolution fusion | flops 3702988800 | bytes 18040320 | tf_op jit(solution)/shard_map/dot_general | solution.py:176
  543.7 12.5 %scatter-add.6 = f32[16,196,768]{2,0,1:T(8,128)} dynamic-update-slice(f32[16,196,768]{2,0,1:T(8,128)} %slice.193, f32[1,196,768]{2,0,1:T(1,128)} %convert_add_fusion.2, s32[]{:T(128)} %constant.187.clone.1, s32[]{:T(128)} %constant.187.clone.1, s32[]{:T(128)} %constant.187.clone.1) | dynamic-update-slice | bytes 1204228 | tf_op jit(solution)/shard_map/scatter-add | solution.py:251
  561.7 12.5 %scatter-add.9 = f32[16,196,768]{2,0,1:T(8,128)} dynamic-update-slice(f32[16,196,768]{2,0,1:T(8,128)} %scatter-add.6, f32[1,196,768]{2,0,1:T(1,128)} %fusion.54, s32[]{:T(128)} %constant.227.clone.1, s32[]{:T(128)} %constant.187.clone.1, s32[]{:T(128)} %constant.187.clone.1) | dynamic-update-slice | bytes 1204228 | tf_op jit(solution)/shard_map/scatter-add | solution.py:251
  594.7 8.0 %fusion.58 = f32[384,1152]{1,0:T(8,128)} fusion(bf16[3136,1152]{1,0:T(8,128)(2,1)} %constant_dynamic-update-slice_fusion.2, bf16[3136,384]{1,0:T(8,128)(2,1)S(1)} %copy-done.6, f32[384]{0:T(512)S(1)} %copy-done.33, f32[384]{0:T(512)S(1)} %copy-done.25, f32[3136]{0:T(1024)S(1)} %copy-done.20, f32[3136]{0:T(1024)S(1)} %copy-done.17), kind=kOutput, calls=%fused_computation.139 | convolution fusion | flops 2781757440 | bytes 11431424 | tf_op jit(solution)/shard_map/dot_general | solution.py:47
  607.1 10.2 %fusion.51 = (f32[384]{0:T(512)S(1)}, f32[3136]{0:T(1024)S(1)}, f32[3136]{0:T(1024)S(1)}, f32[384]{0:T(512)S(1)}, f32[3136,384]{1,0:T(8,128)}) fusion(bf16[3136,384]{1,0:T(8,128)(2,1)S(1)} %copy-done.7, f32[3136]{0:T(1024)S(1)} %copy-done.20, f32[3136]{0:T(1024)S(1)} %copy-done.17, f32[384]{0:T(512)S(1)} %copy-done.25, ...), kind=kOutput, calls=%fused_computation.102 | convolution fusion | flops 2786567168 | bytes 15390208 | tf_op jit(solution)/shard_map/dot_general | solution.py:53
  617.4 43.2 %all-reduce.3 = (f32[384]{0:T(512)}, f32[384]{0:T(512)}, f32[2,384]{1,0:T(2,128)}, f32[384]{0:T(512)}, f32[384]{0:T(512)}, /*index=5*/f32[384]{0:T(512)}, f32[1536]{0:T(1024)}, f32[384]{0:T(512)}) all-reduce(f32[384]{0:T(512)S(1)} %get-tuple-element.253, ...), channel_id=1, replica_groups=mesh['clips'=16,'tm'=2] {'clips','tm'}, use_global_device_ids=true, to_apply=%region_16.17 | all-reduce | flops 4608 | bytes 36864 | tf_op jit(solution)/shard_map/psum | solution.py:277
  660.5 8.3 %fusion.50 = f32[3136,384]{1,0:T(8,128)} fusion(f32[3136,384]{1,0:T(8,128)} %copy-done.3, bf16[3136,384]{1,0:T(8,128)(2,1)} %param.23, f32[3136,384]{1,0:T(8,128)} %get-tuple-element.337, f32[3136]{0:T(1024)S(1)} %broadcast_multiply_fusion, f32[3136]{0:T(1024)S(1)} %broadcast_multiply_fusion.1, f32[384]{0:T(512)S(1)} %copy-done.25, f32[3136]{0:T(1024)S(1)} %copy-done.20, ...), kind=kLoop, calls=%fused_computation.101 | loop fusion | flops 10838016 | bytes 16910848 | tf_op jit(solution)/shard_map/add | solution.py:263
  668.8 102.4 %all-reduce.7.cloned.1.call-done = (f32[384,1152]{1,0:T(8,128)}, f32[384,384]{1,0:T(8,128)}, f32[384,1536]{1,0:T(8,128)}, f32[1536,384]{1,0:T(8,128)}) async-done(((f32[384,1152]{1,0:T(8,128)}, f32[384,384]{1,0:T(8,128)}, f32[384,1536]{1,0:T(8,128)}, f32[1536,384]{1,0:T(8,128)}), (f32[384,1152]{1,0:T(8,128)}, f32[384,384]{1,0:T(8,128)}, f32[384,1536]{1,0:T(8,128)}, ...) | async-done | bytes 7077904 | tf_op jit(solution)/shard_map/psum | solution.py:277
  (300 shorter events, 382.4 us)
Async XLA Ops:
  7.2 154.8 %copy-start = (bf16[384,1536]{1,0:T(8,128)(2,1)S(1)}, bf16[384,1536]{1,0:T(8,128)(2,1)}, u32[]{:S(2)}) copy-start(bf16[384,1536]{1,0:T(8,128)(2,1)} %param.33) | copy-start | bytes 3538948
  7.2 764.0 %all-reduce.7.cloned.1.call-start = ((), (), s32[]{:S(2)}) async-start(), calls=%async_computation | async-start | bytes 14155776 | tf_op jit(solution)/shard_map/psum | solution.py:277
  22.6 13.7 %copy-start.44 = (s32[32]{0:T(128)S(1)}, s32[32]{0:T(128)}, u32[]{:S(2)}) copy-start(s32[32]{0:T(128)} %param.24) | copy-start | bytes 388
  32.5 20.4 %collective-permute-start = (bf16[1,196,768]{2,1,0:T(8,128)(2,1)S(1)}, bf16[1,196,768]{2,1,0:T(8,128)(2,1)S(1)}, u32[]{:S(2)}, u32[]{:S(2)}) collective-permute-start(bf16[1,196,768]{2,1,0:T(8,128)(2,1)S(1)} %get-tuple-element.323), channel_id=1, source_target_pairs={{0,1},{2,3},{4,5},{6,7},{8,9},{10,11},{12,13},{14,15},{16,17},{18,... | collective-permute-start | bytes 903176 | tf_op jit(solution)/shard_map/ppermute | solution.py:23
  34.9 18.0 %collective-permute-start.1 = (bf16[1,196,768]{2,1,0:T(8,128)(2,1)S(1)}, bf16[1,196,768]{2,1,0:T(8,128)(2,1)S(1)}, u32[]{:S(2)}, u32[]{:S(2)}) collective-permute-start(bf16[1,196,768]{2,1,0:T(8,128)(2,1)S(1)} %get-tuple-element.324), channel_id=1, source_target_pairs={{1,0},{3,2},{5,4},{7,6},{9,8},{11,10},{13,12},{15,14},{17,16},{19,... | collective-permute-start | bytes 903176 | tf_op jit(solution)/shard_map/ppermute | solution.py:24
  147.8 8.7 %copy-start.13 = (bf16[384,384]{1,0:T(8,128)(2,1)S(1)}, bf16[384,384]{1,0:T(8,128)(2,1)}, u32[]{:S(2)}) copy-start(bf16[384,384]{1,0:T(8,128)(2,1)} %param.29) | copy-start | bytes 884740
  147.8 8.7 %copy-start.21 = (f32[384]{0:T(512)S(1)}, f32[384]{0:T(512)}, u32[]{:S(2)}) copy-start(f32[384]{0:T(512)} %convert_element_type.119) | copy-start | bytes 4612
  160.9 78.1 %copy-start.4 = (f32[3136,384]{1,0:T(8,128)}, f32[3136,384]{1,0:T(8,128)S(1)}, u32[]{:S(2)}) copy-start(f32[3136,384]{1,0:T(8,128)S(1)} %get-tuple-element.333) | copy-start | bytes 14450692
  162.0 48.4 %copy-start.9 = (bf16[3136,384]{1,0:T(8,128)(2,1)S(1)}, bf16[3136,384]{1,0:T(8,128)(2,1)}, u32[]{:S(2)}) copy-start(bf16[3136,384]{1,0:T(8,128)(2,1)} %param.37) | copy-start | bytes 7225348
  162.0 48.4 %copy-start.40 = (bf16[1536,384]{1,0:T(8,128)(2,1)S(1)}, bf16[1536,384]{1,0:T(8,128)(2,1)}, u32[]{:S(2)}) copy-start(bf16[1536,384]{1,0:T(8,128)(2,1)} %param.35) | copy-start | bytes 3538948
  475.9 29.1 %slice-start.2 = ((s8[4816896]{0:T(1024)(128)(4,1)}), s8[622592]{0:T(1024)(128)(4,1)S(1)}, s32[]{:S(2)}) async-start(s8[4816896]{0:T(1024)(128)(4,1)} %bitcast.128), calls=%async_computation.3 | async-start | bytes 1245184
  484.7 20.3 %slice-start.3 = ((s8[4816896]{0:T(1024)(128)(4,1)}), s8[4194304]{0:T(1024)(128)(4,1)S(1)}, s32[]{:S(2)}) async-start(s8[4816896]{0:T(1024)(128)(4,1)} %bitcast.128), calls=%async_computation.4 | async-start | bytes 8388608
  495.1 9.9 %copy-start.34 = (f32[384]{0:T(512)S(1)}, f32[384]{0:T(512)}, u32[]{:S(2)}) copy-start(f32[384]{0:T(512)} %convert_element_type.125) | copy-start | bytes 4612
  495.1 9.9 %copy-start.41 = (bf16[1536,384]{1,0:T(8,128)(2,1)S(1)}, bf16[1536,384]{1,0:T(8,128)(2,1)}, u32[]{:S(2)}) copy-start(bf16[1536,384]{1,0:T(8,128)(2,1)} %param.35) | copy-start | bytes 3538948
  523.7 12.7 %slice-start = ((s8[4816896]{0:T(1024)(128)(4,1)}), s8[622592]{0:T(1024)(128)(4,1)S(1)}, s32[]{:S(2)}) async-start(s8[4816896]{0:T(1024)(128)(4,1)} %bitcast.124), calls=%async_computation.1 | async-start | bytes 1245184
  524.8 11.6 %slice-start.1 = ((s8[4816896]{0:T(1024)(128)(4,1)}), s8[4194304]{0:T(1024)(128)(4,1)S(1)}, s32[]{:S(2)}) async-start(s8[4816896]{0:T(1024)(128)(4,1)} %bitcast.124), calls=%async_computation.2 | async-start | bytes 8388608
  524.8 11.6 %copy-start.8 = (bf16[3136,384]{1,0:T(8,128)(2,1)S(1)}, bf16[3136,384]{1,0:T(8,128)(2,1)}, u32[]{:S(2)}) copy-start(bf16[3136,384]{1,0:T(8,128)(2,1)} %convert_element_type.118) | copy-start | bytes 7225348
  531.9 6.9 collective-permute-start.3
  533.3 5.9 collective-permute-start.2
  607.1 10.3 %copy-start.22 = (f32[384]{0:T(512)S(1)}, f32[384]{0:T(512)}, u32[]{:S(2)}) copy-start(f32[384]{0:T(512)} %get-tuple-element.305) | copy-start | bytes 4612
  607.1 10.2 %copy-start.23 = (f32[384]{0:T(512)S(1)}, f32[384]{0:T(512)}, u32[]{:S(2)}) copy-start(f32[384]{0:T(512)} %get-tuple-element.327) | copy-start | bytes 4612
  607.1 10.2 %copy-start.27 = (f32[1536]{0:T(1024)S(1)}, f32[1536]{0:T(1024)}, u32[]{:S(2)}) copy-start(f32[1536]{0:T(1024)} %get-tuple-element.338) | copy-start | bytes 18436
  607.1 10.2 %copy-start.30 = (f32[384]{0:T(512)S(1)}, f32[384]{0:T(512)}, u32[]{:S(2)}) copy-start(f32[384]{0:T(512)} %get-tuple-element.251) | copy-start | bytes 4612
  607.1 10.2 %copy-start.31 = (f32[384]{0:T(512)S(1)}, f32[384]{0:T(512)}, u32[]{:S(2)}) copy-start(f32[384]{0:T(512)} %get-tuple-element.257) | copy-start | bytes 4612
  (33 other events, 159.7 us)
Sparse Core Ops, SparseCore 0:
  602.9 168.3 all-reduce.6
where the time goes:
time: 800 us; the launch traced here: 786 us
  matrix products  233 us (29%)
  local copies, waits for them, and re-layouts  221 us (28%)
  other arithmetic  157 us (20%)
  waiting for transfers between devices  102 us (13%)
  blocking collectives  43.2 us (5%)
  between operations  14.8 us (2%)
  starting transfers between devices  8.41 us (1%)
    psum x1, waiting for transfers between devices, per_device(): lax.psum((g_ln1_gain, g_ln1_bias, g_w_qkv, g_qv_bias, g_w_out, g_b_out, g...  102 us
    dot_general x1, matrix products, per_device(): jnp.dot(mlp_in_bf, w_fc1, preferred_element_type=jnp.float32) + bias_up  48.4 us
    psum x1, blocking collectives, per_device(): lax.psum((g_ln1_gain, g_ln1_bias, g_w_qkv, g_qv_bias, g_w_out, g_b_out, g...  43.2 us
    dot_general x4, matrix products, back_through(): lax.dot_general(upstream, weight, (((1,), (1,)), ((), ())), preferred_ele...  35.9 us
    dot_general x4, matrix products, back_block(): jnp.einsum('bihd,bjhd->bhij', grad_heads, value_heads, preferred_element_...  33.8 us
    dynamic_update_slice x4, other arithmetic, back_block(): lax.dynamic_update_slice_in_dim(grad_acc, current + folded, block_start, 0)  28.9 us
    convert_element_type x4, other arithmetic, back_block(): grad_scores = (prob_vals * (grad_probs - row_dot)).astype(jnp.bfloat16)  27.1 us
    dot_general x4, matrix products, cross(): lax.dot_general(left_arr, right_arr, (((0,), (0,)), ((), ())), preferred_...  26.1 us
  transfers between devices with their start and end apart: 5, of which 1 were waited for; matrix products, arithmetic and copies ran while one was open for 5% of the time, Pallas kernels for 0%

commit v1 on v0

v1 whole, which is shorter than its diff:
```python
import functools
import math

import jax
import jax.numpy as jnp
from jax import lax
from jax.experimental import pallas as pl
from jax.experimental.pallas import tpu as pltpu
from jax.sharding import PartitionSpec as P

HEADS = 6
FRAME = 196
ROWS = 208
WIN = 640
EPS = 1e-6
LOG2E = math.log2(math.e)

bf16 = jnp.bfloat16
f32 = jnp.float32


def mm(a, b):
    return jnp.dot(a, b, preferred_element_type=f32)


def mm_nt(a, b):
    return lax.dot_general(a, b, (((1,), (1,)), ((), ())), preferred_element_type=f32)


def mm_tn(a, b):
    return lax.dot_general(a, b, (((0,), (0,)), ((), ())), preferred_element_type=f32)


def normed_of(x):
    mean = jnp.mean(x, axis=-1, keepdims=True)
    centred = x - mean
    var = jnp.mean(centred * centred, axis=-1, keepdims=True)
    inverse = lax.rsqrt(var + EPS)
    return centred * inverse, inverse


def norm_back(upstream, normed, inverse, gain):
    scaled = upstream * gain
    mean = jnp.mean(scaled, axis=-1, keepdims=True)
    along = jnp.mean(scaled * normed, axis=-1, keepdims=True)
    return inverse * (scaled - mean - normed * along)


def fold8(v):
    rows, cols = v.shape
    return jnp.sum(v.reshape(rows // 8, 8, cols), axis=0)


def forward_kernel(
    clip_ref,
    x_ref,
    ghost_ref,
    cot_ref,
    g1_ref,
    s1_ref,
    wqkv_ref,
    bqkv_ref,
    wout_ref,
    bout_ref,
    g2_ref,
    s2_ref,
    w1_ref,
    b1_ref,
    w2_ref,
    b2_ref,
    q_ref,
    kv_ref,
    prob_ref,
    out_ref,
    gatt_ref,
    gres_ref,
    gw1_ref,
    gw2_ref,
    gwo_ref,
    sb1_ref,
    s384_ref,
):
    step = pl.program_id(0)
    steps = pl.num_programs(0)
    frames = 2 * steps
    width = x_ref.shape[-1]
    hidden = w1_ref.shape[-1]
    tm = lax.axis_index("tm")

    @pl.when(step == 0)
    def _():
        gw1_ref[...] = jnp.zeros_like(gw1_ref)
        gw2_ref[...] = jnp.zeros_like(gw2_ref)
        gwo_ref[...] = jnp.zeros_like(gwo_ref)
        sb1_ref[...] = jnp.zeros_like(sb1_ref)
        s384_ref[...] = jnp.zeros_like(s384_ref)
        gain = g1_ref[...].astype(f32)
        shift = s1_ref[...].astype(f32)
        bias = bqkv_ref[...]
        zero_slot = jnp.where(tm == 0, 0, frames + 1)
        ghost_slot = frames + 1 - zero_slot
        kv_ref[pl.ds(pl.multiple_of(zero_slot * ROWS, 16), ROWS), :] = jnp.zeros((ROWS, 2 * width), bf16)
        kv_ref[(frames + 2) * ROWS :, :] = jnp.zeros((WIN - 3 * ROWS, 2 * width), bf16)

        x = ghost_ref[...].astype(f32)
        n, _ = normed_of(x)
        kv = mm((n * gain + shift).astype(bf16), wqkv_ref[:, width:]) + bias[:, width:]
        kv_ref[pl.ds(pl.multiple_of(ghost_slot * ROWS, 16), ROWS), :] = kv.astype(bf16)

        def project(i, carry):
            x = x_ref[pl.ds(2 * i, 2)].reshape(2 * ROWS, width).astype(f32)
            n, _ = normed_of(x)
            qkv = (mm((n * gain + shift).astype(bf16), wqkv_ref[...]) + bias).astype(bf16)
            q_ref[pl.ds(2 * i, 2)] = qkv[:, :width].reshape(2, ROWS, width)
            kv_ref[pl.ds(pl.multiple_of((2 * i + 1) * ROWS, 16), 2 * ROWS), :] = qkv[:, width:]
            return carry

        lax.fori_loop(0, frames // 2, project, 0)

    lane = lax.broadcasted_iota(jnp.int32, (ROWS, 128), 1)
    low_half = lane < 64
    col = lax.broadcasted_iota(jnp.int32, (1, WIN), 1)
    scale = LOG2E / math.sqrt(width // HEADS)
    attended = []
    for sub in range(2):
        frame = 2 * step + sub
        here = tm * frames + frame
        own = clip_ref[here]
        before = jnp.where(here > 0, clip_ref[jnp.maximum(here - 1, 0)], -1)
        after = jnp.where(here < 2 * frames - 1, clip_ref[jnp.minimum(here + 1, 2 * frames - 1)], -1)
        lo = jnp.where(before == own, 0, ROWS)
        hi = jnp.where(after == own, 3 * ROWS, 2 * ROWS)
        slot = col // ROWS
        live = (col >= lo) & (col < hi) & (col - slot * ROWS < FRAME)
        mask = jnp.where(live, 0.0, -1e30).astype(f32)
        window = pl.ds(pl.multiple_of(frame * ROWS, 16), WIN)
        for pair in range(HEADS // 2):
            q = q_ref[frame, :, 128 * pair : 128 * pair + 128]
            k = kv_ref[window, 128 * pair : 128 * pair + 128]
            v = kv_ref[window, width + 128 * pair : width + 128 * pair + 128]
            parts = []
            for half in range(2):
                mine = low_half if half == 0 else ~low_half
                s = mm_nt(jnp.where(mine, q, jnp.zeros_like(q)), k) + mask
                top = jnp.max(s, axis=-1, keepdims=True)
                e = jnp.exp2((s - top) * scale)
                total = jnp.sum(e, axis=-1, keepdims=True)
                prob = (e * (1.0 / total)).astype(bf16)
                prob_ref[sub, 2 * pair + half] = prob
                parts.append(mm(prob, v))
            attended.append(jnp.where(low_half, parts[0], parts[1]).astype(bf16))
    att = jnp.concatenate(
        [
            jnp.concatenate([attended[p], attended[HEADS // 2 + p]], axis=0)
            for p in range(HEADS // 2)
        ],
        axis=1,
    )
    x = x_ref[pl.ds(2 * step, 2)].reshape(2 * ROWS, width).astype(f32)
    resid = x + mm(att, wout_ref[...]) + bout_ref[...].astype(f32)
    n2, inv2 = normed_of(resid)
    mlp_in = (n2 * g2_ref[...].astype(f32) + s2_ref[...].astype(f32)).astype(bf16)
    cot = cot_ref[...].reshape(2 * ROWS, width)
    out = resid + b2_ref[...].astype(f32)
    up = jnp.zeros((2 * ROWS, width), f32)
    chunk = 512
    for c in range(hidden // chunk):
        cols = slice(c * chunk, (c + 1) * chunk)
        pre = mm(mlp_in, w1_ref[:, cols]) + b1_ref[:, cols].astype(f32)
        cdf = 0.5 * (1.0 + lax.erf(pre * (1.0 / math.sqrt(2.0))))
        hid = (pre * cdf).astype(bf16)
        dens = jnp.exp2(pre * pre * (-0.5 * LOG2E)) * (1.0 / math.sqrt(2.0 * math.pi))
        out = out + mm(hid, w2_ref[cols, :])
        gw2_ref[:, cols] += mm_tn(cot, hid)
        gpre32 = mm_nt(cot, w2_ref[cols, :]) * (cdf + pre * dens)
        gpre = gpre32.astype(bf16)
        sb1_ref[:, cols] += fold8(gpre.astype(f32))
        gw1_ref[:, cols] += mm_tn(mlp_in, gpre)
        up = up + mm_nt(gpre, w1_ref[:, cols])
    out_ref[...] = out.astype(bf16).reshape(2, ROWS, width)
    cot32 = cot.astype(f32)
    gres = cot32 + norm_back(up, n2, inv2, g2_ref[...].astype(f32))
    gres_ref[...] = gres.reshape(2, ROWS, width)
    branch = gres.astype(bf16)
    gwo_ref[...] += mm_tn(att, branch)
    gatt_ref[...] = mm_nt(branch, wout_ref[...]).astype(bf16).reshape(2, ROWS, width)
    s384_ref[0] += fold8(up * n2)
    s384_ref[1] += fold8(up)
    s384_ref[2] += fold8(branch.astype(f32))
    s384_ref[3] += fold8(cot32)


def back_kernel(q_ref, kv_ref, prob_ref, gatt_ref, dq_ref, dkv_ref, edge_ref, acc_ref):
    step = pl.program_id(0)
    steps = pl.num_programs(0)
    frames = 2 * steps
    width = q_ref.shape[-1]
    tm = lax.axis_index("tm")
    inv_scale = 1.0 / math.sqrt(width // HEADS)

    @pl.when(step == 0)
    def _():
        acc_ref[...] = jnp.zeros_like(acc_ref)

    lane = lax.broadcasted_iota(jnp.int32, (ROWS, 128), 1)
    low_half = lane < 64
    for sub in range(2):
        frame = 2 * step + sub
        window = pl.ds(pl.multiple_of(frame * ROWS, 16), WIN)
        for pair in range(HEADS // 2):
            cols = slice(128 * pair, 128 * pair + 128)
            vcols = slice(width + 128 * pair, width + 128 * pair + 128)
            q = q_ref[sub, :, cols]
            g = gatt_ref[sub, :, cols]
            k = kv_ref[window, cols]
            v = kv_ref[window, vcols]
            dq, dk, dv = [], 0.0, 0.0
            for half in range(2):
                mine = low_half if half == 0 else ~low_half
                gm = jnp.where(mine, g, jnp.zeros_like(g))
                qm = jnp.where(mine, q, jnp.zeros_like(q))
                prob_bf = prob_ref[sub, 2 * pair + half]
                prob = prob_bf.astype(f32)
                dp = mm_nt(gm, v)
                dot = jnp.sum(prob * dp, axis=-1, keepdims=True)
                ds = (prob * (dp - dot)).astype(bf16)
                dq.append(mm(ds, k))
                dk = dk + mm_tn(ds, qm)
                dv = dv + mm_tn(prob_bf, gm)
            dq_ref[sub, :, cols] = (jnp.where(low_half, dq[0], dq[1]) * inv_scale).astype(bf16)
            acc_ref[window, cols] += dk
            acc_ref[window, vcols] += dv

    @pl.when(step == steps - 1)
    def _():
        def finish(i, carry):
            rows = pl.ds(pl.multiple_of((i + 1) * ROWS, 16), ROWS)
            dkv_ref[i, :, :width] = (acc_ref[rows, :width] * inv_scale).astype(bf16)
            dkv_ref[i, :, width:] = acc_ref[rows, width:].astype(bf16)
            return carry

        lax.fori_loop(0, frames, finish, 0)
        own = pl.ds(pl.multiple_of(jnp.where(tm == 0, frames, 1) * ROWS, 16), ROWS)
        ghost = pl.ds(pl.multiple_of(jnp.where(tm == 0, frames + 1, 0) * ROWS, 16), ROWS)
        edge_ref[0, :, :width] = acc_ref[own, :width] * inv_scale
        edge_ref[0, :, width:] = acc_ref[own, width:]
        edge_ref[1, :, :width] = acc_ref[ghost, :width] * inv_scale
        edge_ref[1, :, width:] = acc_ref[ghost, width:]


def input_kernel(x_ref, dq_ref, dkv_ref, edge_ref, got_ref, gres_ref, g1_ref, s1_ref, wqkv_ref,
                 out_ref, gw_ref, sq_ref, s384_ref):
    step = pl.program_id(0)
    steps = pl.num_programs(0)
    frames = 2 * steps
    width = x_ref.shape[-1]
    tm = lax.axis_index("tm")

    @pl.when(step == 0)
    def _():
        gw_ref[...] = jnp.zeros_like(gw_ref)
        sq_ref[...] = jnp.zeros_like(sq_ref)
        s384_ref[...] = jnp.zeros_like(s384_ref)

    edge_frame = jnp.where(tm == 0, frames - 1, 0)

    @pl.when(step == edge_frame // 2)
    def _():
        dkv_ref[edge_frame % 2] = (edge_ref[0] + got_ref[...].astype(f32)).astype(bf16)

    x = x_ref[...].reshape(2 * ROWS, width).astype(f32)
    n, inv = normed_of(x)
    gain = g1_ref[...].astype(f32)
    attn_in = (n * gain + s1_ref[...].astype(f32)).astype(bf16)
    dq = dq_ref[...].reshape(2 * ROWS, width)
    dkv = dkv_ref[...].reshape(2 * ROWS, 2 * width)
    gw_ref[:, :width] += mm_tn(attn_in, dq)
    gw_ref[:, width:] += mm_tn(attn_in, dkv)
    sq_ref[:, :width] += fold8(dq.astype(f32))
    sq_ref[:, width:] += fold8(dkv[:, width:].astype(f32))
    up = mm_nt(dq, wqkv_ref[:, :width]) + mm_nt(dkv, wqkv_ref[:, width:])
    gres = gres_ref[...].reshape(2 * ROWS, width)
    out_ref[...] = (gres + norm_back(up, n, inv, gain)).reshape(2, ROWS, width)
    s384_ref[0] += fold8(up * n)
    s384_ref[1] += fold8(up)


def whole(shape):
    return pl.BlockSpec(shape, lambda i: (0,) * len(shape), pipeline_mode=pl.Buffered(1))


def pairs(shape):
    return pl.BlockSpec((2,) + shape, lambda i: (i,) + (0,) * len(shape))


def params():
    return pltpu.CompilerParams(vmem_limit_bytes=60 * 2**20)


def per_device(tokens, frame_clip, ln1_gain, ln1_bias, w_qkv, qv_bias, w_out, b_out, ln2_gain, ln2_bias,
               w_fc1, b_fc1, w_fc2, b_fc2, cotangent):
    count, width = tokens.shape
    hidden = w_fc1.shape[1]
    frames = count // FRAME
    steps = frames // 2
    tm = lax.axis_index("tm")
    pad = ((0, 0), (0, ROWS - FRAME), (0, 0))
    x_pad = jnp.pad(tokens.reshape(frames, FRAME, width), pad)
    cot_pad = jnp.pad(cotangent.reshape(frames, FRAME, width), pad)
    edge = jnp.where(tm == 0, tokens[count - FRAME :], tokens[:FRAME])
    ghost = jnp.pad(lax.ppermute(edge, "tm", [(0, 1), (1, 0)]), pad[1:])
    row = lambda v: v.reshape(1, -1)
    bias_qkv = jnp.concatenate([qv_bias[0], jnp.zeros((width,), bf16), qv_bias[1]]).astype(f32)
    kv_rows = (frames + 2) * ROWS + WIN - 3 * ROWS
    shape = jax.ShapeDtypeStruct
    q, kv, prob, out_pad, gatt, gres, gw1, gw2t, gwo, sb1, s2 = pl.pallas_call(
        forward_kernel,
        grid=(steps,),
        in_specs=[
            pl.BlockSpec(memory_space=pltpu.SMEM),
            whole((frames, ROWS, width)),
            whole((ROWS, width)),
            pairs((ROWS, width)),
            whole((1, width)),
            whole((1, width)),
            whole((width, 3 * width)),
            whole((1, 3 * width)),
            whole((width, width)),
            whole((1, width)),
            whole((1, width)),
            whole((1, width)),
            whole((width, hidden)),
            whole((1, hidden)),
            whole((hidden, width)),
            whole((1, width)),
        ],
        out_specs=[
            whole((frames, ROWS, width)),
            whole((kv_rows, 2 * width)),
            pairs((HEADS, ROWS, WIN)),
            pairs((ROWS, width)),
            pairs((ROWS, width)),
            pairs((ROWS, width)),
            whole((width, hidden)),
            whole((width, hidden)),
            whole((width, width)),
            whole((8, hidden)),
            whole((4, 8, width)),
        ],
        out_shape=[
            shape((frames, ROWS, width), bf16),
            shape((kv_rows, 2 * width), bf16),
            shape((frames, HEADS, ROWS, WIN), bf16),
            shape((frames, ROWS, width), bf16),
            shape((frames, ROWS, width), bf16),
            shape((frames, ROWS, width), f32),
            shape((width, hidden), f32),
            shape((width, hidden), f32),
            shape((width, width), f32),
            shape((8, hidden), f32),
            shape((4, 8, width), f32),
        ],
        compiler_params=params(),
    )(frame_clip, x_pad, ghost, cot_pad, row(ln1_gain), row(ln1_bias), w_qkv, row(bias_qkv), w_out, row(b_out),
      row(ln2_gain), row(ln2_bias), w_fc1, row(b_fc1), w_fc2, row(b_fc2))

    dq, dkv, edges = pl.pallas_call(
        back_kernel,
        grid=(steps,),
        in_specs=[
            pairs((ROWS, width)),
            whole((kv_rows, 2 * width)),
            pairs((HEADS, ROWS, WIN)),
            pairs((ROWS, width)),
        ],
        out_specs=[
            pairs((ROWS, width)),
            whole((frames, ROWS, 2 * width)),
            whole((2, ROWS, 2 * width)),
        ],
        out_shape=[
            shape((frames, ROWS, width), bf16),
            shape((frames, ROWS, 2 * width), bf16),
            shape((2, ROWS, 2 * width), f32),
        ],
        scratch_shapes=[pltpu.VMEM((kv_rows, 2 * width), f32)],
        compiler_params=params(),
    )(q, kv, prob, gatt)

    got = lax.ppermute(edges[1].astype(bf16), "tm", [(0, 1), (1, 0)])

    in_pad, gwqkv, sqkv, s1 = pl.pallas_call(
        input_kernel,
        grid=(steps,),
        in_specs=[
            pairs((ROWS, width)),
            pairs((ROWS, width)),
            pairs((ROWS, 2 * width)),
            whole((2, ROWS, 2 * width)),
            whole((ROWS, 2 * width)),
            pairs((ROWS, width)),
            whole((1, width)),
            whole((1, width)),
            whole((width, 3 * width)),
        ],
        out_specs=[
            pairs((ROWS, width)),
            whole((width, 3 * width)),
            whole((8, 2 * width)),
            whole((2, 8, width)),
        ],
        out_shape=[
            shape((frames, ROWS, width), f32),
            shape((width, 3 * width), f32),
            shape((8, 2 * width), f32),
            shape((2, 8, width), f32),
        ],
        compiler_params=params(),
    )(x_pad, dq, dkv, edges, got, gres, row(ln1_gain), row(ln1_bias), w_qkv)

    block_out = out_pad[:, :FRAME].reshape(count, width)
    input_grad = in_pad[:, :FRAME].reshape(count, width)
    s1 = jnp.sum(s1, axis=1)
    s2 = jnp.sum(s2, axis=1)
    sq = jnp.sum(sqkv, axis=0).reshape(2, width)
    grads = lax.psum(
        (s1[0], s1[1], gwqkv, sq, gwo, s2[2], s2[0], s2[1], gw1, jnp.sum(sb1, axis=0), gw2t.T, s2[3]),
        ("clips", "tm"),
    )
    return (block_out, input_grad) + tuple(grads)


def solution(mesh):
    rows = P(("clips", "tm"), None)
    rep = P()
    return jax.shard_map(
        per_device,
        mesh=mesh,
        in_specs=(rows, P("clips")) + (rep,) * 12 + (rows,),
        out_specs=(rows, rows) + (rep,) * 12,
        check_vma=False,
    )
```

time: 800 us -> 405 us (0.51); the launches traced: 786 us -> 405 us
  matrix products: 233 us -> 0 us
  Pallas kernels: 0 us -> 192 us
  local copies, waits for them, and re-layouts: 221 us -> 40.3 us
  other arithmetic: 157 us -> 1.71 us
  waiting for transfers between devices: 102 us -> 112 us
    dot_general x40 -> x0, matrix products: 233 us -> none  [the longest x1 48.4 us: per_device(): jnp.dot(mlp_in_bf, w_fc1, preferred_element_type=jnp.float32) + bias_up]
    pallas_call x0 -> x3, Pallas kernels: none -> 192 us  [the longest x1 111 us: per_device(): pl.pallas_call(forward_kernel, grid=(steps,), in_specs=[pl.BlockSpec(memo...]
    slice x24 -> x4, local copies, waits for them, and re-layouts: 53.4 us -> 7.33 us  [the longest x1 5.34 us: per_device(): input_grad = in_pad[:, :FRAME].reshape(count, width)]
    concatenate x15 -> x0, other arithmetic: 37.9 us -> none  [the longest x8 20.7 us: frame_windows(): return jnp.concatenate([window[:-2], window[1:-1], window[2:]], axis=1)]
    while x11 -> x0, local copies, waits for them, and re-layouts: 34.1 us -> none  [the longest x1 16 us: per_device(): grad_kv_ext, grad_q = lax.scan(back_block, empty_ext, jnp.arange(n_blocks))]
    convert_element_type x12 -> x1, other arithmetic: 32.5 us -> 0.6 us  [per_device(): jnp.concatenate([qv_bias[0], jnp.zeros((width,), bf16), qv_bias[1]])]
    dynamic_update_slice x8 -> x0, other arithmetic: 29 us -> none  [the longest x4 28.9 us: back_block(): lax.dynamic_update_slice_in_dim(grad_acc, current + folded, block_start, 0)]
    reduce_sum x9 -> x4, other arithmetic: 26.9 us -> 0.07 us  [the longest x1 0.02 us: per_device(): s2 = jnp.sum(s2, axis=1)]
  transfers between devices with their start and end apart: 5 -> 3, of which waited for: 1 -> 2; matrix products, arithmetic and copies ran while one was open for 5% -> 8% of each run, Pallas kernels for 0% -> 0%
where the time goes in v1:
time: 405 us
  Pallas kernels  192 us (47%)
  waiting for transfers between devices  112 us (28%)
  blocking collectives  43.4 us (11%)
  local copies, waits for them, and re-layouts  40.3 us (10%)
  between operations  14.2 us (4%)
    pallas_call x1, Pallas kernels, per_device(): pl.pallas_call(forward_kernel, grid=(steps,), in_specs=[pl.BlockSpec(memo...  111 us
    psum x1, waiting for transfers between devices, per_device(): lax.psum((s1[0], s1[1], gwqkv, sq, gwo, s2[2], s2[0], s2[1], gw1, jnp.sum...  111 us
    pallas_call x1, Pallas kernels, per_device(): pl.pallas_call(back_kernel, grid=(steps,), in_specs=[pairs((ROWS, width))...  63.5 us
    psum x1, blocking collectives, per_device(): lax.psum((s1[0], s1[1], gwqkv, sq, gwo, s2[2], s2[0], s2[1], gw1, jnp.sum...  43.4 us
    pallas_call x1, Pallas kernels, per_device(): pl.pallas_call(input_kernel, grid=(steps,), in_specs=[pairs((ROWS, width)...  17 us
  transfers between devices with their start and end apart: 3, of which 2 were waited for; matrix products, arithmetic and copies ran while one was open for 8% of the time, Pallas kernels for 0%

profile of v1, /device:TPU:0, one launch (start us, length us, event | category | flops | bytes accessed | tf_op | source)
XLA Modules:
  0.0 404.6 jit_solution(15427050850247144135)
XLA Ops:
  7.2 1.0 slice_select_fusion
  8.9 2.6 reshape.100
  14.9 0.6 reshape.107.b1_ref
  15.5 4.0 %reshape.101 = bf16[16,196,384]{2,1,0:T(8,128)(2,1)} reshape(bf16[3136,384]{1,0:T(8,128)(2,1)} %param.29) | data formatting | bytes 4816896 | tf_op jit(solution)/shard_map/reshape | solution.py:309
  19.6 3.5 pad.13.cot_ref
  23.0 1.7 pad.11.x_ref
  24.8 0.6 fusion.2.bqkv_ref
  25.4 0.7 pad.12.ghost_ref
  26.1 111.5 %shard_map.254 = (bf16[16,208,384]{2,1,0:T(8,128)(2,1)}, bf16[3760,768]{1,0:T(8,128)(2,1)}, bf16[16,6,208,640]{3,2,1,0:T(8,128)(2,1)}, bf16[16,208,384]{2,1,0:T(...) custom-call(s32[32]{0:T(128)} %clip_ref.1, ...), custom_call_target="tpu_custom_call" | custom-call | tf_op jit(solution)/shard_map/pallas_call | solution.py:316
  137.6 63.5 %shard_map.255 = (bf16[16,208,384]{2,1,0:T(8,128)(2,1)}, bf16[16,208,768]{2,1,0:T(8,128)(2,1)}, f32[2,208,768]{2,1,0:T(8,128)}) custom-call(bf16[16,208,384]{2,1,0:T(8,128)(2,1)} %get-tuple-element.33.q_ref, bf16[3760,768]{1,0:T(8,128)(2,1)} %get-tuple-element.34.kv_ref, bf16[16,6,208,640]{3,2,1,0:T(8,128)(2,1)} %get-tuple-element.35.prob_ref, ...), custom_call_target="tpu_custom_call" | custom-call | tf_op jit(solution)/shard_map/pallas_call | solution.py:367
  201.1 1.1 fusion
  202.3 1.6 collective-permute-done.1.got_ref
  203.9 0.7 copy-done.3
  204.6 17.0 %shard_map.256 = (f32[16,208,384]{2,1,0:T(8,128)}, f32[384,1152]{1,0:T(8,128)}, f32[8,768]{1,0:T(8,128)}, f32[2,8,384]{2,1,0:T(8,128)}) custom-call(bf16[16,208,384]{2,1,0:T(8,128)(2,1)} %pad.11.x_ref, bf16[16,208,384]{2,1,0:T(8,128)(2,1)} %get-tuple-element.37.dq_ref, bf16[16,208,768]{2,1,0:T(8,128)(2,1)} %get-tuple-element.38.dkv_ref, ...), custom_call_target="tpu_custom_call" | custom-call | tf_op jit(solution)/shard_map/pallas_call | solution.py:392
  221.7 1.9 slice.44
  223.6 2.1 reshape.109
  225.8 5.3 %slice.46 = f32[16,196,384]{2,1,0:T(8,128)} slice(f32[16,208,384]{2,1,0:T(8,128)} %get-tuple-element.41), slice={[0:16], [0:196], [0:384]} | slice | bytes 9633792 | tf_op jit(solution)/shard_map/slice | solution.py:422
  231.1 5.2 %reshape.110 = f32[3136,384]{1,0:T(8,128)} reshape(f32[16,196,384]{2,1,0:T(8,128)} %slice.46) | data formatting | bytes 9633792 | tf_op jit(solution)/shard_map/reshape | solution.py:422
  236.4 43.4 %all-reduce.3 = (f32[384]{0:T(512)}, f32[384]{0:T(512)}, f32[2,384]{1,0:T(2,128)}, f32[384]{0:T(512)}, f32[384]{0:T(512)}, /*index=5*/f32[384]{0:T(512)}, f32[1536]{0:T(1024)}, f32[384]{0:T(512)}) all-reduce(f32[384]{0:T(512)S(1)} %get-tuple-element.98, ...), channel_id=1, replica_groups=mesh['clips'=16,'tm'=2] {'clips','tm'}, use_global_device_ids=true, to_apply=%region_1.2 | all-reduce | flops 4608 | bytes 36864 | tf_op jit(solution)/shard_map/psum | solution.py:426
  279.7 110.7 %all-reduce.7.cloned.1.call-done = (f32[384,1152]{1,0:T(8,128)}, f32[384,384]{1,0:T(8,128)}, f32[384,1536]{1,0:T(8,128)}, f32[1536,384]{0,1:T(8,128)}) async-done(((f32[384,1152]{1,0:T(8,128)}, f32[384,384]{1,0:T(8,128)}, f32[384,1536]{1,0:T(8,128)}, f32[1536,384]{0,1:T(8,128)}), (f32[384,1152]{1,0:T(8,128)}, f32[384,384]{1,0:T(8,128)}, f32[384,1536]{1,0:T(8,128)}, ...) | async-done | bytes 7077904 | tf_op jit(solution)/shard_map/psum | solution.py:426
  390.5 3.2 copy.30
  393.7 1.2 copy.35
  395.1 0.8 copy.36
  396.3 1.4 copy.37
  (51 shorter events, 4.9 us)
Async XLA Ops:
  7.2 383.3 %all-reduce.7.cloned.1.call-start = ((), (), s32[]{:S(2)}) async-start(), calls=%async_computation | async-start | bytes 14155776 | tf_op jit(solution)/shard_map/psum | solution.py:426
  8.3 3.2 copy-start.10
  8.3 3.8 copy-start.11
  8.3 4.3 %copy-start.12 = (bf16[384]{0:T(512)(128)(2,1)S(1)}, bf16[384]{0:T(512)(128)(2,1)}, u32[]{:S(2)}) copy-start(bf16[384]{0:T(512)(128)(2,1)} %param.22) | copy-start | bytes 2308
  8.3 4.9 %copy-start.13 = (bf16[384]{0:T(512)(128)(2,1)S(1)}, bf16[384]{0:T(512)(128)(2,1)}, u32[]{:S(2)}) copy-start(bf16[384]{0:T(512)(128)(2,1)} %param.23) | copy-start | bytes 2308
  8.3 5.5 %copy-start.14 = (bf16[384]{0:T(512)(128)(2,1)S(1)}, bf16[384]{0:T(512)(128)(2,1)}, u32[]{:S(2)}) copy-start(bf16[384]{0:T(512)(128)(2,1)} %param.24) | copy-start | bytes 2308
  8.3 6.0 %copy-start.15 = (bf16[384]{0:T(512)(128)(2,1)S(1)}, bf16[384]{0:T(512)(128)(2,1)}, u32[]{:S(2)}) copy-start(bf16[384]{0:T(512)(128)(2,1)} %param.28) | copy-start | bytes 2308
  8.3 6.6 %copy-start.8 = (bf16[2,384]{1,0:T(2,128)(2,1)S(1)}, bf16[2,384]{1,0:T(2,128)(2,1)}, u32[]{:S(2)}) copy-start(bf16[2,384]{1,0:T(2,128)(2,1)} %param.20) | copy-start | bytes 4612
  8.4 6.6 %copy-start.9 = (bf16[1536]{0:T(1024)(128)(2,1)S(1)}, bf16[1536]{0:T(1024)(128)(2,1)}, u32[]{:S(2)}) copy-start(bf16[1536]{0:T(1024)(128)(2,1)} %param.26) | copy-start | bytes 9220
  8.4 17.0 %collective-permute-start = (bf16[196,384]{1,0:T(8,128)(2,1)S(1)}, bf16[196,384]{1,0:T(8,128)(2,1)S(1)}, u32[]{:S(2)}, u32[]{:S(2)}) collective-permute-start(bf16[196,384]{1,0:T(8,128)(2,1)S(1)} %slice_select_fusion), channel_id=1, source_target_pairs={{0,1},{1,0},{2,3},{3,2},{4,5},{5,4},{6,7},{7,6},{8,9},{9,8},{10,11... | collective-permute-start | bytes 451592 | tf_op jit(solution)/shard_map/ppermute | solution.py:311
  202.2 1.7 collective-permute-start.1
  203.9 0.7 copy-start.3
  223.6 2.1 copy-start.5
  223.6 2.1 copy-start.4
  231.1 5.2 %copy-start.7 = (f32[2,8,384]{2,1,0:T(8,128)S(1)}, f32[2,8,384]{2,1,0:T(8,128)}, u32[]{:S(2)}) copy-start(f32[2,8,384]{2,1,0:T(8,128)} %get-tuple-element.42) | copy-start | bytes 73732
  231.1 5.2 %copy-start.6 = (f32[8,768]{1,0:T(8,128)S(1)}, f32[8,768]{1,0:T(8,128)}, u32[]{:S(2)}) copy-start(f32[8,768]{1,0:T(8,128)} %get-tuple-element.44) | copy-start | bytes 73732
  390.5 3.2 copy-start.1
  393.7 1.4 copy-start.2
  393.7 2.7 copy-start
Sparse Core Ops, SparseCore 0:
  221.8 168.6 all-reduce.6

commit v2 on v1

--- a/solution.py
+++ b/solution.py
@@ -49,6 +49,164 @@
 def fold8(v):
     rows, cols = v.shape
     return jnp.sum(v.reshape(rows // 8, 8, cols), axis=0)
+
+
+MESH = pl.DeviceIdType.MESH
+
+
+def stages_of(clips):
+    stages, stride = [("tm", 1, 2)], 1
+    while clips > 1:
+        size = 4 if clips % 4 == 0 else (2 if clips % 2 == 0 else clips)
+        stages.append(("clips", stride, size))
+        stride, clips = stride * size, clips // size
+    return stages
+
+
+def digit(stage):
+    axis, stride, size = stage
+    return lax.rem(lax.axis_index(axis) // stride, size)
+
+
+def partner(stage, turn):
+    axis, stride, size = stage
+    mine = digit(stage)
+    return {axis: lax.axis_index(axis) + (lax.rem(mine + turn, size) - mine) * stride}
+
+
+def greet(stages):
+    sem, count = pltpu.get_barrier_semaphore(), 0
+    for stage in stages:
+        for turn in range(1, stage[2]):
+            pl.semaphore_signal(sem, inc=1, device_id=partner(stage, turn), device_id_type=MESH)
+            count += 1
+    pl.semaphore_wait(sem, count)
+
+
+class Sum:
+    def __init__(self, stages, pack, result, landing, sent, came):
+        self.stages, self.pack, self.result, self.landing = stages, pack, result, landing
+        self.sent, self.came = sent, came
+        self.segments, start, length = [], 0, pack.shape[0]
+        for stage in stages:
+            self.segments.append((start, length))
+            length = length // stage[2]
+            start = start + digit(stage) * length
+        self.segments.append((start, length))
+        self.first = [sum(s[2] - 1 for s in stages[:i]) for i in range(len(stages) + 1)]
+
+    def _scatter(self, i):
+        stage, (start, length) = self.stages[i], self.segments[i]
+        part = length // stage[2]
+        for turn in range(1, stage[2]):
+            slot = self.first[i] + turn - 1
+            other = lax.rem(digit(stage) + turn, stage[2])
+            yield pltpu.make_async_remote_copy(
+                src_ref=self.pack.at[pl.ds(start + other * part, part)],
+                dst_ref=self.landing[i].at[turn - 1],
+                send_sem=self.sent.at[slot],
+                recv_sem=self.came.at[slot],
+                device_id=partner(stage, turn),
+                device_id_type=MESH,
+            )
+
+    def _gather(self, i):
+        stage, (start, length) = self.stages[i], self.segments[i + 1]
+        for turn in range(1, stage[2]):
+            slot = self.first[-1] + self.first[i] + turn - 1
+            here = self.result.at[pl.ds(start, length)]
+            yield pltpu.make_async_remote_copy(
+                src_ref=here,
+                dst_ref=here,
+                send_sem=self.sent.at[slot],
+                recv_sem=self.came.at[slot],
+                device_id=partner(stage, turn),
+                device_id_type=MESH,
+            )
+
+    def send(self, i):
+        for copy in self._scatter(i):
+            copy.start()
+
+    def take(self, i):
+        for copy in self._scatter(i):
+            copy.wait()
+        start, length = self.segments[i + 1]
+        into = self.result if i == len(self.stages) - 1 else self.pack
+        block = next(b for b in (28, 24, 21, 16, 14, 12, 8, 7, 6, 4, 3, 2, 1) if length % b == 0)
+
+        def add(j, carry):
+            total = self.pack[pl.ds(start + j * block, block)].astype(f32)
+            for turn in range(1, self.stages[i][2]):
+                total = total + self.landing[i][turn - 1, pl.ds(j * block, block)].astype(f32)
+            into[pl.ds(start + j * block, block)] = total.astype(bf16)
+            return carry
+
+        lax.fori_loop(0, length // block, add, 0)
+
+    def spread(self, i):
+        for copy in self._gather(i):
+            copy.start()
+
+    def settle(self, i):
+        for copy in self._gather(i):
+            copy.wait()
+
+
+def sum_scratch(stages, units):
+    shapes, left = [], units
+    for stage in stages:
+        left //= stage[2]
+        shapes.append(pltpu.VMEM((stage[2] - 1, left, 16, 128), bf16))
+    copies = 2 * sum(s[2] - 1 for s in stages)
+    return shapes + [pltpu.SemaphoreType.DMA((copies,)), pltpu.SemaphoreType.DMA((copies,))]
+
+
+def pack_matrix(pack, first, value):
+    rows, cols = value.shape
+    tiles = rows // 16
+    for c in range(cols // 128):
+        pack[first + c * tiles : first + (c + 1) * tiles] = (
+            value[:, 128 * c : 128 * (c + 1)].astype(bf16).reshape(tiles, 16, 128)
+        )
+    return first + cols // 128 * tiles
+
+
+def pack_rows(pack, first, vectors):
+    rows = [v[:, c : c + 128] for v in vectors for c in range(0, v.shape[1], 128)]
+    rows += [jnp.zeros((1, 128), f32)] * (-len(rows) % 16)
+    for r in range(0, len(rows), 16):
+        pack[first + r // 16] = jnp.concatenate(rows[r : r + 16], axis=0).astype(bf16)
+    last = first + len(rows) // 16
+    if last < pack.shape[0]:
+        pack[last:] = jnp.zeros((pack.shape[0] - last, 16, 128), bf16)
+
+
+def unpack_matrix(res, first, rows, cols):
+    tiles = rows // 16
+    part = res[first : first + cols // 128 * tiles].reshape(cols // 128, tiles, 16, 128)
+    return part.transpose(1, 2, 0, 3).reshape(rows, cols).astype(f32)
+
+
+def units_for(needed, devices):
+    return -(-needed // devices) * devices
+
+
+def colsum(v):
+    return jnp.sum(v, axis=0, keepdims=True)
+
+
+def reduce_kernel(stages, pack_ref, res_ref, own_ref, sum_ref, *rest):
+    total = Sum(stages, own_ref, sum_ref, rest[: len(stages)], *rest[len(stages) :])
+    greet(stages)
+    own_ref[...] = pack_ref[...]
+    for i in range(len(stages)):
+        total.send(i)
+        total.take(i)
+    for i in reversed(range(len(stages))):
+        total.spread(i)
+        total.settle(i)
+    res_ref[...] = sum_ref[...]
 
 
 def forward_kernel(
@@ -74,6 +232,7 @@
     out_ref,
     gatt_ref,
     gres_ref,
+    pack_ref,
     gw1_ref,
     gw2_ref,
     gwo_ref,
@@ -189,18 +348,48 @@
     s384_ref[2] += fold8(branch.astype(f32))
     s384_ref[3] += fold8(cot32)
 
-
-def back_kernel(q_ref, kv_ref, prob_ref, gatt_ref, dq_ref, dkv_ref, edge_ref, acc_ref):
+    @pl.when(step == steps - 1)
+    def _():
+        at = pack_matrix(pack_ref, 0, gw1_ref[...])
+        at = pack_matrix(pack_ref, at, gw2_ref[...])
+        at = pack_matrix(pack_ref, at, gwo_ref[...])
+        pack_rows(pack_ref, at, [colsum(s384_ref[i]) for i in range(4)] + [colsum(sb1_ref[...])])
+
+
+def back_kernel(stages, q_ref, kv_ref, prob_ref, gatt_ref, pack_ref, dq_ref, dkv_ref, edge_ref, res_ref,
+                acc_ref, own_ref, sum_ref, *rest):
     step = pl.program_id(0)
     steps = pl.num_programs(0)
     frames = 2 * steps
     width = q_ref.shape[-1]
     tm = lax.axis_index("tm")
     inv_scale = 1.0 / math.sqrt(width // HEADS)
+    total = Sum(stages, own_ref, sum_ref, rest[: len(stages)], *rest[len(stages) :])
+    last = len(stages) - 1
 
     @pl.when(step == 0)
     def _():
+        own_ref[...] = pack_ref[...]
+        greet(stages)
+        total.send(0)
         acc_ref[...] = jnp.zeros_like(acc_ref)
+
+    def at(when, *todo):
+        @pl.when(step == when)
+        def _():
+            for act, i in todo:
+                act(i)
+
+    at(1, (total.take, 0), (total.send, 1))
+    if len(stages) == 3:
+        at(3, (total.take, 1), (total.send, 2))
+        at(4, (total.take, 2), (total.spread, 2))
+        at(5, (total.settle, 2), (total.spread, 1))
+        at(7, (total.settle, 1), (total.spread, 0))
+    else:
+        at(3, *[t for i in range(1, last) for t in ((total.take, i), (total.send, i + 1))])
+        at(5, (total.take, last), (total.spread, last))
+        at(7, *[t for i in range(last, 0, -1) for t in ((total.settle, i), (total.spread, i - 1))])
 
     lane = lax.broadcasted_iota(jnp.int32, (ROWS, 128), 1)
     low_half = lane < 64
@@ -246,10 +435,12 @@
         edge_ref[0, :, width:] = acc_ref[own, width:]
         edge_ref[1, :, :width] = acc_ref[ghost, :width] * inv_scale
         edge_ref[1, :, width:] = acc_ref[ghost, width:]
+        total.settle(0)
+        res_ref[...] = sum_ref[...]
 
 
 def input_kernel(x_ref, dq_ref, dkv_ref, edge_ref, got_ref, gres_ref, g1_ref, s1_ref, wqkv_ref,
-                 out_ref, gw_ref, sq_ref, s384_ref):
+                 out_ref, pack_ref, gw_ref, sq_ref, s384_ref):
     step = pl.program_id(0)
     steps = pl.num_programs(0)
     frames = 2 * steps
@@ -284,6 +475,12 @@
     s384_ref[0] += fold8(up * n)
     s384_ref[1] += fold8(up)
 
+    @pl.when(step == steps - 1)
+    def _():
+        at = pack_matrix(pack_ref, 0, gw_ref[...])
+        sq = colsum(sq_ref[...])
+        pack_rows(pack_ref, at, [colsum(s384_ref[0]), colsum(s384_ref[1]), sq])
+
 
 def whole(shape):
     return pl.BlockSpec(shape, lambda i: (0,) * len(shape), pipeline_mode=pl.Buffered(1))
@@ -293,8 +490,10 @@
     return pl.BlockSpec((2,) + shape, lambda i: (i,) + (0,) * len(shape))
 
 
-def params():
-    return pltpu.CompilerParams(vmem_limit_bytes=60 * 2**20)
+def params(collective=None):
+    if collective is None:
+        return pltpu.CompilerParams(vmem_limit_bytes=60 * 2**20)
+    return pltpu.CompilerParams(vmem_limit_bytes=60 * 2**20, collective_id=collective, has_side_effects=True)
 
 
 def per_device(tokens, frame_clip, ln1_gain, ln1_bias, w_qkv, qv_bias, w_out, b_out, ln2_gain, ln2_bias,
@@ -313,7 +512,12 @@
     bias_qkv = jnp.concatenate([qv_bias[0], jnp.zeros((width,), bf16), qv_bias[1]]).astype(f32)
     kv_rows = (frames + 2) * ROWS + WIN - 3 * ROWS
     shape = jax.ShapeDtypeStruct
-    q, kv, prob, out_pad, gatt, gres, gw1, gw2t, gwo, sb1, s2 = pl.pallas_call(
+    stages = stages_of(lax.axis_size("clips"))
+    devices = 2 * lax.axis_size("clips")
+    tiles = width // 16
+    units = units_for((2 * hidden + width) // 128 * tiles + 2, devices)
+    units2 = units_for(3 * width // 128 * tiles + 1, devices)
+    q, kv, prob, out_pad, gatt, gres, pack = pl.pallas_call(
         forward_kernel,
         grid=(steps,),
         in_specs=[
@@ -341,11 +545,7 @@
             pairs((ROWS, width)),
             pairs((ROWS, width)),
             pairs((ROWS, width)),
-            whole((width, hidden)),
-            whole((width, hidden)),
-            whole((width, width)),
-            whole((8, hidden)),
-            whole((4, 8, width)),
+            whole((units, 16, 128)),
         ],
         out_shape=[
             shape((frames, ROWS, width), bf16),
@@ -354,42 +554,49 @@
             shape((frames, ROWS, width), bf16),
             shape((frames, ROWS, width), bf16),
             shape((frames, ROWS, width), f32),
-            shape((width, hidden), f32),
-            shape((width, hidden), f32),
-            shape((width, width), f32),
-            shape((8, hidden), f32),
-            shape((4, 8, width), f32),
+            shape((units, 16, 128), bf16),
+        ],
+        scratch_shapes=[
+            pltpu.VMEM((width, hidden), f32),
+            pltpu.VMEM((width, hidden), f32),
+            pltpu.VMEM((width, width), f32),
+            pltpu.VMEM((8, hidden), f32),
+            pltpu.VMEM((4, 8, width), f32),
         ],
         compiler_params=params(),
     )(frame_clip, x_pad, ghost, cot_pad, row(ln1_gain), row(ln1_bias), w_qkv, row(bias_qkv), w_out, row(b_out),
       row(ln2_gain), row(ln2_bias), w_fc1, row(b_fc1), w_fc2, row(b_fc2))
 
-    dq, dkv, edges = pl.pallas_call(
-        back_kernel,
+    dq, dkv, edges, res = pl.pallas_call(
+        functools.partial(back_kernel, stages),
         grid=(steps,),
         in_specs=[
             pairs((ROWS, width)),
             whole((kv_rows, 2 * width)),
             pairs((HEADS, ROWS, WIN)),
             pairs((ROWS, width)),
+            whole((units, 16, 128)),
         ],
         out_specs=[
             pairs((ROWS, width)),
             whole((frames, ROWS, 2 * width)),
             whole((2, ROWS, 2 * width)),
+            whole((units, 16, 128)),
         ],
         out_shape=[
             shape((frames, ROWS, width), bf16),
             shape((frames, ROWS, 2 * width), bf16),
             shape((2, ROWS, 2 * width), f32),
-        ],
-        scratch_shapes=[pltpu.VMEM((kv_rows, 2 * width), f32)],
-        compiler_params=params(),
-    )(q, kv, prob, gatt)
+            shape((units, 16, 128), bf16),
+        ],
+        scratch_shapes=[pltpu.VMEM((kv_rows, 2 * width), f32), pltpu.VMEM((units, 16, 128), bf16), pltpu.VMEM((units, 16, 128), bf16)]
+        + sum_scratch(stages, units),
+        compiler_params=params(0),
+    )(q, kv, prob, gatt, pack)
 
     got = lax.ppermute(edges[1].astype(bf16), "tm", [(0, 1), (1, 0)])
 
-    in_pad, gwqkv, sqkv, s1 = pl.pallas_call(
+    in_pad, pack2 = pl.pallas_call(
         input_kernel,
         grid=(steps,),
         in_specs=[
@@ -405,29 +612,43 @@
         ],
         out_specs=[
             pairs((ROWS, width)),
-            whole((width, 3 * width)),
-            whole((8, 2 * width)),
-            whole((2, 8, width)),
+            whole((units2, 16, 128)),
         ],
         out_shape=[
             shape((frames, ROWS, width), f32),
-            shape((width, 3 * width), f32),
-            shape((8, 2 * width), f32),
-            shape((2, 8, width), f32),
+            shape((units2, 16, 128), bf16),
+        ],
+        scratch_shapes=[
+            pltpu.VMEM((width, 3 * width), f32),
+            pltpu.VMEM((8, 2 * width), f32),
+            pltpu.VMEM((2, 8, width), f32),
         ],
         compiler_params=params(),
     )(x_pad, dq, dkv, edges, got, gres, row(ln1_gain), row(ln1_bias), w_qkv)
 
+    in_vmem = pl.BlockSpec(memory_space=pltpu.VMEM)
+    res2 = pl.pallas_call(
+        functools.partial(reduce_kernel, stages),
+        in_specs=[in_vmem],
+        out_specs=in_vmem,
+        out_shape=shape((units2, 16, 128), bf16),
+        scratch_shapes=[pltpu.VMEM((units2, 16, 128), bf16)] * 2 + sum_scratch(stages, units2),
+        compiler_params=params(1),
+    )(pack2)
+
     block_out = out_pad[:, :FRAME].reshape(count, width)
     input_grad = in_pad[:, :FRAME].reshape(count, width)
-    s1 = jnp.sum(s1, axis=1)
-    s2 = jnp.sum(s2, axis=1)
-    sq = jnp.sum(sqkv, axis=0).reshape(2, width)
-    grads = lax.psum(
-        (s1[0], s1[1], gwqkv, sq, gwo, s2[2], s2[0], s2[1], gw1, jnp.sum(sb1, axis=0), gw2t.T, s2[3]),
-        ("clips", "tm"),
-    )
-    return (block_out, input_grad) + tuple(grads)
+    across = hidden // 128 * tiles
+    gw1 = unpack_matrix(res, 0, width, hidden)
+    gw2 = unpack_matrix(res, across, width, hidden).T
+    gwo = unpack_matrix(res, 2 * across, width, width)
+    vec = res[2 * across + width // 128 * tiles :][:2].reshape(-1).astype(f32)
+    gwqkv = unpack_matrix(res2, 0, width, 3 * width)
+    vec2 = res2[3 * width // 128 * tiles].reshape(-1).astype(f32)
+    two = lambda i: vec[i * width : (i + 1) * width]
+    one = lambda i: vec2[i * width : (i + 1) * width]
+    return (block_out, input_grad, one(0), one(1), gwqkv, vec2[2 * width : 4 * width].reshape(2, width), gwo, two(2),
+            two(0), two(1), gw1, vec[4 * width : 4 * width + hidden], gw2, two(3))
 
 
 def solution(mesh):

time: 405 us -> 293 us (0.72)
  waiting for transfers between devices: 112 us -> 0.01 us
  Pallas kernels: 192 us -> 239 us
  blocking collectives: 43.4 us -> 0 us
  between operations: 14.2 us -> 0.86 us
  local copies, waits for them, and re-layouts: 40.3 us -> 49.2 us
    psum x1 -> x0, waiting for transfers between devices: 111 us -> none  [per_device(): lax.psum((s1[0], s1[1], gwqkv, sq, gwo, s2[2], s2[0], s2[1], gw1, jnp.sum...]
    pallas_call x1 -> x2, Pallas kernels: 63.5 us -> 110 us  [the longest x1 78.5 us: per_device(): pl.pallas_call(functools.partial(back_kernel, stages), grid=(steps,), in_...]
    psum x1 -> x0, blocking collectives: 43.4 us -> none  [per_device(): lax.psum((s1[0], s1[1], gwqkv, sq, gwo, s2[2], s2[0], s2[1], gw1, jnp.sum...]
    slice x1 -> x9, local copies, waits for them, and re-layouts: 0.04 us -> 7.05 us  [the longest x4 4.57 us: unpack_matrix(): res[first:first + cols // 128 * tiles].reshape(cols // 128, tiles, 16, 128)]
    unnamed x36 -> x29, local copies, waits for them, and re-layouts: 8.04 us -> 9.16 us
  transfers between devices with their start and end apart: 3 -> 2, of which waited for: 2 -> 0; matrix products, arithmetic and copies ran while one was open for 8% -> 11% of each run, Pallas kernels for 0% -> 0%
where the time goes in v2:
time: 293 us; the launch traced here: 292 us
  Pallas kernels  239 us (82%)
  local copies, waits for them, and re-layouts  49.2 us (17%)
    pallas_call x1, Pallas kernels, per_device(): pl.pallas_call(forward_kernel, grid=(steps,), in_specs=[pl.BlockSpec(memo...  112 us
    pallas_call x1, Pallas kernels, per_device(): pl.pallas_call(functools.partial(back_kernel, stages), grid=(steps,), in_...  78.5 us
    pallas_call x1, Pallas kernels, per_device(): pl.pallas_call(functools.partial(reduce_kernel, stages), in_specs=[in_vme...  31.3 us
    pallas_call x1, Pallas kernels, per_device(): pl.pallas_call(input_kernel, grid=(steps,), in_specs=[pairs((ROWS, width)...  17.4 us
    unnamed x29, local copies, waits for them, and re-layouts  9.16 us
  transfers between devices with their start and end apart: 2, of which 0 were waited for; matrix products, arithmetic and copies ran while one was open for 11% of the time, Pallas kernels for 0%

profile of v2, /device:TPU:0, one launch (start us, length us, event | category | flops | bytes accessed | tf_op | source)
XLA Modules:
  0.0 291.9 jit_solution(16553623731763445320)
XLA Ops:
  0.7 1.1 slice_select_fusion
  2.3 2.6 reshape.132
  9.0 4.0 %reshape.133 = bf16[16,196,384]{2,1,0:T(8,128)(2,1)} reshape(bf16[3136,384]{1,0:T(8,128)(2,1)} %param.29) | data formatting | bytes 4816896 | tf_op jit(solution)/shard_map/reshape | solution.py:508
  13.0 3.4 %pad.13.cot_ref = bf16[16,208,384]{2,1,0:T(8,128)(2,1)} pad(bf16[16,196,384]{2,1,0:T(8,128)(2,1)} %reshape.133, bf16[]{:T(256)} %constant.3.clone.1), padding=0_0x0_12x0_0 | pad | bytes 4964354 | tf_op jit(solution)/shard_map/jit(_pad)/pad | solution.py:508
  16.4 1.8 pad.11.x_ref
  19.5 111.7 %shard_map.254 = (bf16[16,208,384]{2,1,0:T(8,128)(2,1)}, bf16[3760,768]{1,0:T(8,128)(2,1)}, bf16[16,6,208,640]{3,2,1,0:T(8,128)(2,1)}, bf16[16,208,384]{2,1,0:T(...) custom-call(s32[32]{0:T(128)} %clip_ref.1, ...), custom_call_target="tpu_custom_call" | custom-call | tf_op jit(solution)/shard_map/pallas_call | solution.py:520
  131.2 78.5 %shard_map.255 = (bf16[16,208,384]{2,1,0:T(8,128)(2,1)}, bf16[16,208,768]{2,1,0:T(8,128)(2,1)}, f32[2,208,768]{2,1,0:T(8,128)}, bf16[672,16,128]{2,1,0:T(8,128)(2,1)}) custom-call(bf16[16,208,384]{2,1,0:T(8,128)(2,1)} %get-tuple-element.28.q_ref, bf16[3760,768]{1,0:T(8,128)(2,1)} %get-tuple-element.29.kv_ref, ...), custom_call_target="tpu_custom_call" | custom-call | tf_op jit(solution)/shard_map/pallas_call | solution.py:570
  209.7 1.1 fusion
  210.9 3.6 %fusion.3 = (bf16[288,16,128]{2,1,0:T(8,128)(2,1)}, bf16[288,16,128]{2,1,0:T(8,128)(2,1)}) fusion(bf16[672,16,128]{2,1,0:T(8,128)(2,1)} %get-tuple-element.39), kind=kLoop, calls=%fused_computation.13 | loop fusion | bytes 4718592 | tf_op jit(solution)/shard_map/slice | solution.py:187
  214.5 0.7 slice.88
  215.2 1.0 slice.87
  216.4 2.1 reshape.141
  219.4 0.9 copy.49
  220.3 0.7 copy.35
  221.0 2.5 copy.47
  223.5 0.7 copy.36
  224.2 1.1 copy.46
  225.3 2.0 copy.37
  227.8 0.7 copy-done.3
  228.5 17.4 %shard_map.256 = (f32[16,208,384]{2,1,0:T(8,128)}, bf16[224,16,128]{2,1,0:T(8,128)(2,1)}) custom-call(bf16[16,208,384]{2,1,0:T(8,128)(2,1)} %pad.11.x_ref, bf16[16,208,384]{2,1,0:T(8,128)(2,1)} %get-tuple-element.33.dq_ref, bf16[16,208,768]{2,1,0:T(8,128)(2,1)} %get-tuple-element.34.dkv_ref, f32[2,208,768]{2,1,0:T(8,128)} %get-tuple-element.35.edge_ref, ...), custom_call_target="tpu_custom_call" | custom-call | tf_op jit(solution)/shard_map/pallas_call | solution.py:599
  245.9 31.3 %shard_map.257 = bf16[224,16,128]{2,1,0:T(8,128)(2,1)} custom-call(bf16[224,16,128]{2,1,0:T(8,128)(2,1)} %get-tuple-element.38.pack_ref), custom_call_target="tpu_custom_call" | custom-call | tf_op jit(solution)/shard_map/pallas_call | solution.py:630
  278.5 4.9 %slice.79 = f32[16,196,384]{2,1,0:T(8,128)} slice(f32[16,208,384]{2,1,0:T(8,128)} %get-tuple-element.37), slice={[0:16], [0:196], [0:384]} | slice | bytes 9633792 | tf_op jit(solution)/shard_map/slice | solution.py:640
  283.4 5.2 %reshape.142 = f32[3136,384]{1,0:T(8,128)} reshape(f32[16,196,384]{2,1,0:T(8,128)} %slice.79) | data formatting | bytes 9633792 | tf_op jit(solution)/shard_map/reshape | solution.py:640
  289.9 2.0 copy.48
  (50 shorter events, 10.1 us)
Async XLA Ops:
  0.7 4.3 %copy-start.6 = (bf16[384]{0:T(512)(128)(2,1)S(1)}, bf16[384]{0:T(512)(128)(2,1)}, u32[]{:S(2)}) copy-start(bf16[384]{0:T(512)(128)(2,1)} %param.17) | copy-start | bytes 2308
  0.7 4.8 %copy-start.7 = (bf16[384]{0:T(512)(128)(2,1)S(1)}, bf16[384]{0:T(512)(128)(2,1)}, u32[]{:S(2)}) copy-start(bf16[384]{0:T(512)(128)(2,1)} %param.18) | copy-start | bytes 2308
  0.7 5.4 %copy-start.8 = (bf16[384]{0:T(512)(128)(2,1)S(1)}, bf16[384]{0:T(512)(128)(2,1)}, u32[]{:S(2)}) copy-start(bf16[384]{0:T(512)(128)(2,1)} %param.22) | copy-start | bytes 2308
  0.7 6.0 %copy-start.9 = (bf16[384]{0:T(512)(128)(2,1)S(1)}, bf16[384]{0:T(512)(128)(2,1)}, u32[]{:S(2)}) copy-start(bf16[384]{0:T(512)(128)(2,1)} %param.23) | copy-start | bytes 2308
  0.7 6.5 %copy-start.10 = (bf16[384]{0:T(512)(128)(2,1)S(1)}, bf16[384]{0:T(512)(128)(2,1)}, u32[]{:S(2)}) copy-start(bf16[384]{0:T(512)(128)(2,1)} %param.24) | copy-start | bytes 2308
  0.7 7.1 %copy-start.11 = (bf16[384]{0:T(512)(128)(2,1)S(1)}, bf16[384]{0:T(512)(128)(2,1)}, u32[]{:S(2)}) copy-start(bf16[384]{0:T(512)(128)(2,1)} %param.28) | copy-start | bytes 2308
  1.8 6.6 %copy-start.4 = (bf16[2,384]{1,0:T(2,128)(2,1)S(1)}, bf16[2,384]{1,0:T(2,128)(2,1)}, u32[]{:S(2)}) copy-start(bf16[2,384]{1,0:T(2,128)(2,1)} %param.20) | copy-start | bytes 4612
  1.8 6.6 %copy-start.5 = (bf16[1536]{0:T(1024)(128)(2,1)S(1)}, bf16[1536]{0:T(1024)(128)(2,1)}, u32[]{:S(2)}) copy-start(bf16[1536]{0:T(1024)(128)(2,1)} %param.26) | copy-start | bytes 9220
  1.8 17.0 %collective-permute-start = (bf16[196,384]{1,0:T(8,128)(2,1)S(1)}, bf16[196,384]{1,0:T(8,128)(2,1)S(1)}, u32[]{:S(2)}, u32[]{:S(2)}) collective-permute-start(bf16[196,384]{1,0:T(8,128)(2,1)S(1)} %slice_select_fusion), channel_id=1, source_target_pairs={{0,1},{1,0},{2,3},{3,2},{4,5},{5,4},{6,7},{7,6},{8,9},{9,8},{10,11... | collective-permute-start | bytes 451592 | tf_op jit(solution)/shard_map/ppermute | solution.py:510
  210.8 17.0 %collective-permute-start.1 = (bf16[208,768]{1,0:T(8,128)(2,1)S(1)}, bf16[208,768]{1,0:T(8,128)(2,1)S(1)}, u32[]{:S(2)}, u32[]{:S(2)}) collective-permute-start(bf16[208,768]{1,0:T(8,128)(2,1)S(1)} %fusion), channel_id=1, source_target_pairs={{0,1},{1,0},{2,3},{3,2},{4,5},{5,4},{6,7},{7,6},{8,9},{9,8},{10,11... | collective-permute-start | bytes 958472 | tf_op jit(solution)/shard_map/ppermute | solution.py:597
  210.9 5.3 %copy-start.2 = (bf16[16,208,384]{2,1,0:T(8,128)(2,1)S(1)}, bf16[16,208,384]{2,1,0:T(8,128)(2,1)}, u32[]{:S(2)}) copy-start(bf16[16,208,384]{2,1,0:T(8,128)(2,1)} %get-tuple-element.27) | copy-start | bytes 7667716
  218.5 1.7 copy-start.1
  221.0 2.5 copy-start
  227.8 0.7 copy-start.3
  283.4 5.8 %slice-start = ((bf16[224,16,128]{2,1,0:T(8,128)(2,1)}), bf16[216,16,128]{2,1,0:T(8,128)(2,1)S(1)}, s32[]{:S(2)}) async-start(bf16[224,16,128]{2,1,0:T(8,128)(2,1)} %shard_map.257), calls=%async_computation | async-start | bytes 1769472 | tf_op jit(solution)/shard_map/slice | solution.py:187

commit v3 on v2

v3 whole, which is shorter than its diff:
```python
import functools
import math

import jax
import jax.numpy as jnp
from jax import lax
from jax.experimental import pallas as pl
from jax.experimental.pallas import tpu as pltpu
from jax.sharding import PartitionSpec as P

HEADS = 6
FRAME = 196
ROWS = 208
WIN = 640
EPS = 1e-6
LOG2E = math.log2(math.e)

bf16 = jnp.bfloat16
f32 = jnp.float32


def mm(a, b):
    return jnp.dot(a, b, preferred_element_type=f32)


def mm_nt(a, b):
    return lax.dot_general(a, b, (((1,), (1,)), ((), ())), preferred_element_type=f32)


def mm_tn(a, b):
    return lax.dot_general(a, b, (((0,), (0,)), ((), ())), preferred_element_type=f32)


def normed_of(x):
    mean = jnp.mean(x, axis=-1, keepdims=True)
    centred = x - mean
    var = jnp.mean(centred * centred, axis=-1, keepdims=True)
    inverse = lax.rsqrt(var + EPS)
    return centred * inverse, inverse


def norm_back(upstream, normed, inverse, gain):
    scaled = upstream * gain
    mean = jnp.mean(scaled, axis=-1, keepdims=True)
    along = jnp.mean(scaled * normed, axis=-1, keepdims=True)
    return inverse * (scaled - mean - normed * along)


def fold8(v):
    rows, cols = v.shape
    return jnp.sum(v.reshape(rows // 8, 8, cols), axis=0)


MESH = pl.DeviceIdType.MESH


def stages_of(clips):
    stages, stride = [("tm", 1, 2)], 1
    while clips > 1:
        size = 4 if clips % 4 == 0 else (2 if clips % 2 == 0 else clips)
        stages.append(("clips", stride, size))
        stride, clips = stride * size, clips // size
    return stages


def digit(stage):
    axis, stride, size = stage
    return lax.rem(lax.axis_index(axis) // stride, size)


def partner(stage, turn):
    axis, stride, size = stage
    mine = digit(stage)
    return {axis: lax.axis_index(axis) + (lax.rem(mine + turn, size) - mine) * stride}


def greet(stages):
    sem, count = pltpu.get_barrier_semaphore(), 0
    for stage in stages:
        for turn in range(1, stage[2]):
            pl.semaphore_signal(sem, inc=1, device_id=partner(stage, turn), device_id_type=MESH)
            count += 1
    pl.semaphore_wait(sem, count)


class Sum:
    def __init__(self, stages, pack, result, landing, sent, came):
        self.stages, self.pack, self.result, self.landing = stages, pack, result, landing
        self.sent, self.came = sent, came
        self.segments, start, length = [], 0, pack.shape[0]
        for stage in stages:
            self.segments.append((start, length))
            length = length // stage[2]
            start = start + digit(stage) * length
        self.segments.append((start, length))
        self.first = [sum(s[2] - 1 for s in stages[:i]) for i in range(len(stages) + 1)]

    def _scatter(self, i):
        stage, (start, length) = self.stages[i], self.segments[i]
        part = length // stage[2]
        for turn in range(1, stage[2]):
            slot = self.first[i] + turn - 1
            other = lax.rem(digit(stage) + turn, stage[2])
            yield pltpu.make_async_remote_copy(
                src_ref=self.pack.at[pl.ds(start + other * part, part)],
                dst_ref=self.landing[i].at[turn - 1],
                send_sem=self.sent.at[slot],
                recv_sem=self.came.at[slot],
                device_id=partner(stage, turn),
                device_id_type=MESH,
            )

    def _gather(self, i):
        stage, (start, length) = self.stages[i], self.segments[i + 1]
        for turn in range(1, stage[2]):
            slot = self.first[-1] + self.first[i] + turn - 1
            here = self.result.at[pl.ds(start, length)]
            yield pltpu.make_async_remote_copy(
                src_ref=here,
                dst_ref=here,
                send_sem=self.sent.at[slot],
                recv_sem=self.came.at[slot],
                device_id=partner(stage, turn),
                device_id_type=MESH,
            )

    def send(self, i):
        for copy in self._scatter(i):
            copy.start()

    def take(self, i):
        for copy in self._scatter(i):
            copy.wait()
        start, length = self.segments[i + 1]
        into = self.result if i == len(self.stages) - 1 else self.pack
        block = next(b for b in (28, 24, 21, 16, 14, 12, 8, 7, 6, 4, 3, 2, 1) if length % b == 0)

        def add(j, carry):
            total = self.pack[pl.ds(start + j * block, block)].astype(f32)
            for turn in range(1, self.stages[i][2]):
                total = total + self.landing[i][turn - 1, pl.ds(j * block, block)].astype(f32)
            into[pl.ds(start + j * block, block)] = total.astype(bf16)
            return carry

        lax.fori_loop(0, length // block, add, 0)

    def spread(self, i):
        for copy in self._gather(i):
            copy.start()

    def settle(self, i):
        for copy in self._gather(i):
            copy.wait()


def sum_scratch(stages, units):
    shapes, left = [], units
    for stage in stages:
        left //= stage[2]
        shapes.append(pltpu.VMEM((stage[2] - 1, left, 16, 128), bf16))
    copies = 2 * sum(s[2] - 1 for s in stages)
    return shapes + [pltpu.SemaphoreType.DMA((copies,)), pltpu.SemaphoreType.DMA((copies,))]


def pack_matrix(pack, first, value):
    rows, cols = value.shape
    tiles = rows // 16
    for c in range(cols // 128):
        pack[first + c * tiles : first + (c + 1) * tiles] = (
            value[:, 128 * c : 128 * (c + 1)].astype(bf16).reshape(tiles, 16, 128)
        )
    return first + cols // 128 * tiles


def pack_rows(pack, first, vectors):
    rows = [v[:, c : c + 128] for v in vectors for c in range(0, v.shape[1], 128)]
    rows += [jnp.zeros((1, 128), f32)] * (-len(rows) % 16)
    for r in range(0, len(rows), 16):
        pack[first + r // 16] = jnp.concatenate(rows[r : r + 16], axis=0).astype(bf16)
    last = first + len(rows) // 16
    if last < pack.shape[0]:
        pack[last:] = jnp.zeros((pack.shape[0] - last, 16, 128), bf16)


def unpack_matrix(res, first, rows, cols):
    tiles = rows // 16
    part = res[first : first + cols // 128 * tiles].reshape(cols // 128, tiles, 16, 128)
    return part.transpose(1, 2, 0, 3).reshape(rows, cols).astype(f32)


def units_for(needed, devices):
    return -(-needed // devices) * devices


def colsum(v):
    return jnp.sum(v, axis=0, keepdims=True)


def widen(ref, group, which):
    start = which * FRAME // 16 * 16
    shift = which * FRAME - start
    v = ref[pl.ds(pl.multiple_of(group * 4 * FRAME + start, 16), ROWS), :].astype(f32)
    if shift:
        v = pltpu.roll(v, ROWS - shift, 0)
    row = lax.broadcasted_iota(jnp.int32, (16, v.shape[1]), 0)
    return v, jnp.where(row < 16 - (ROWS - FRAME), v[ROWS - 16 :], 0.0)


def narrow_into(ref, start, v):
    edge = FRAME // 8 * 8
    over = FRAME - edge
    second = pltpu.roll(v[ROWS:], over, 0)
    row = lax.broadcasted_iota(jnp.int32, (8, v.shape[1]), 0)
    ref[pl.ds(pl.multiple_of(start, 8), edge), :] = v[:edge]
    ref[pl.ds(pl.multiple_of(start + edge, 8), 8), :] = jnp.where(row < over, v[edge : edge + 8], second[:8])
    rest = 2 * FRAME - edge - 8
    ref[pl.ds(pl.multiple_of(start + edge + 8, 8), rest), :] = second[8 : 8 + rest]


def forward_kernel(
    clip_ref,
    tok_ref,
    ghost_ref,
    cot_ref,
    row_ref,
    wqkv_ref,
    wout_ref,
    w1_ref,
    w2_ref,
    x_ref,
    kv_ref,
    prob_ref,
    out_ref,
    qs_ref,
    ga_ref,
    gs_ref,
    gres_ref,
    li_ref,
    pack_ref,
    q_ref,
    cp_ref,
    flag_ref,
    s_ref,
    o_ref,
    flat_ref,
    gw1_ref,
    gw2_ref,
    gwo_ref,
    sb1_ref,
    s384_ref,
):
    step = pl.program_id(0)
    steps = pl.num_programs(0)
    frames = 2 * steps
    width = x_ref.shape[-1]
    hidden = w1_ref.shape[-1]
    tm = lax.axis_index("tm")
    vec = lambda i, n=width: row_ref[:, i * width : i * width + n]
    gain1, shift1, bias3, biaso, gain2, shift2, bias2, bias1 = (
        vec(0), vec(1), vec(2, 3 * width), vec(5), vec(6), vec(7), vec(8), vec(9, hidden))

    @pl.when(step == 0)
    def _():
        gw1_ref[...] = jnp.zeros_like(gw1_ref)
        gw2_ref[...] = jnp.zeros_like(gw2_ref)
        gwo_ref[...] = jnp.zeros_like(gwo_ref)
        sb1_ref[...] = jnp.zeros_like(sb1_ref)
        s384_ref[...] = jnp.zeros_like(s384_ref)
        at = lax.broadcasted_iota(jnp.int32, flag_ref.shape, 0)
        lane = lax.broadcasted_iota(jnp.int32, flag_ref.shape, 1) % 64
        slot = at // ROWS
        flag_ref[...] = jnp.where(
            lane == 0,
            jnp.where(at - slot * ROWS < FRAME, 0.0, -1e30),
            jnp.where(lane == 1 + slot % 4, 1.0, 0.0),
        ).astype(bf16)
        zero_slot = jnp.where(tm == 0, 0, frames + 1)
        ghost_slot = frames + 1 - zero_slot
        kv_ref[pl.ds(pl.multiple_of(zero_slot * ROWS, 16), ROWS), :] = jnp.zeros((ROWS, 2 * width), bf16)
        kv_ref[(frames + 2) * ROWS :, :] = jnp.zeros((WIN - 3 * ROWS, 2 * width), bf16)

        x = ghost_ref[...].astype(f32)
        n, _ = normed_of(x)
        kv = mm((n * gain1 + shift1).astype(bf16), wqkv_ref[:, width:]) + bias3[:, width:]
        kv_ref[pl.ds(pl.multiple_of(ghost_slot * ROWS, 16), ROWS), :] = kv.astype(bf16)

        def pad(i, carry):
            for which in range(4):
                for src, dst in ((tok_ref, x_ref), (cot_ref, cp_ref)):
                    v, end = widen(src, i, which)
                    dst[4 * i + which, : ROWS - 16] = v[: ROWS - 16].astype(bf16)
                    dst[4 * i + which, ROWS - 16 :] = end.astype(bf16)
            return carry

        lax.fori_loop(0, frames // 4, pad, 0)

        def project(i, carry):
            x = x_ref[pl.ds(2 * i, 2)].reshape(2 * ROWS, width).astype(f32)
            n, _ = normed_of(x)
            qkv = (mm((n * gain1 + shift1).astype(bf16), wqkv_ref[...]) + bias3).astype(bf16)
            q_ref[pl.ds(2 * i, 2)] = qkv[:, :width].reshape(2, ROWS, width)
            kv_ref[pl.ds(pl.multiple_of((2 * i + 1) * ROWS, 16), 2 * ROWS), :] = qkv[:, width:]
            return carry

        lax.fori_loop(0, frames // 2, project, 0)

    low = lax.broadcasted_iota(jnp.int32, (ROWS, 128), 1) < 64
    wide_low = lax.broadcasted_iota(jnp.int32, (WIN, 128), 1) < 64
    lane = lax.broadcasted_iota(jnp.int32, (1, 128), 1) % 64
    ones = jnp.ones((WIN, 128), bf16)
    scale = LOG2E / math.sqrt(width // HEADS)
    flags, windows = [], []
    for sub in range(2):
        frame = 2 * step + sub
        here = tm * frames + frame
        own = clip_ref[here]
        before = jnp.where(here > 0, clip_ref[jnp.maximum(here - 1, 0)], -1)
        after = jnp.where(here < 2 * frames - 1, clip_ref[jnp.minimum(here + 1, 2 * frames - 1)], -1)
        none = jnp.float32(-1e30)
        row = jnp.where(lane == 0, 1.0, 0.0)
        row = jnp.where(lane == 1 + frame % 4, jnp.where(before == own, 0.0, none), row)
        row = jnp.where(lane == 1 + (frame + 2) % 4, jnp.where(after == own, 0.0, none), row)
        row = jnp.where(lane == 1 + (frame + 3) % 4, none, row)
        flags.append(jnp.broadcast_to(row.astype(bf16), (ROWS, 128)))
        windows.append(pl.ds(pl.multiple_of(frame * ROWS, 16), WIN))

    def score(t):
        sub, h = divmod(t, HEADS)
        cols = slice(h // 2 * 128, h // 2 * 128 + 128)
        mine, wide = (low, wide_low) if h % 2 == 0 else (~low, ~wide_low)
        q = jnp.where(mine, q_ref[2 * step + sub, :, cols], flags[sub])
        k = jnp.where(wide, kv_ref[windows[sub], cols], flag_ref[windows[sub], :])
        s_ref[t % 3] = mm_nt(q, k)

    def soften(t):
        sub, h = divmod(t, HEADS)
        s = s_ref[t % 3]
        top = jnp.max(s, axis=-1, keepdims=True)
        prob_ref[sub, h] = jnp.exp2((s - top) * scale).astype(bf16)

    parts = {}

    def attend(t):
        sub, h = divmod(t, HEADS)
        at = h // 2 * 128
        wide = wide_low if h % 2 == 0 else ~wide_low
        v = jnp.where(wide, kv_ref[windows[sub], width + at : width + at + 128], ones)
        parts[t] = mm(prob_ref[sub, h], v)
        if h % 2:
            even, odd = parts.pop(t - 1), parts.pop(t)
            total = pltpu.roll(jnp.where(low, odd, even), 64, 1)
            inverse = 1.0 / total
            rows = slice(sub * ROWS, (sub + 1) * ROWS)
            o_ref[rows, at : at + 128] = jnp.where(low, even, odd) * inverse
            li_ref[sub, :, at : at + 128] = inverse

    score(0)
    for t in range(2 * HEADS + 1):
        if t + 1 < 2 * HEADS:
            score(t + 1)
        if t >= 1:
            attend(t - 1)
        if t < 2 * HEADS:
            soften(t)

    att = o_ref[...].astype(bf16)
    both = pl.ds(2 * step, 2)
    x = x_ref[both].reshape(2 * ROWS, width).astype(f32)
    resid = x + mm(att, wout_ref[...]) + biaso
    n2, inv2 = normed_of(resid)
    mlp_in = (n2 * gain2 + shift2).astype(bf16)
    cot = cp_ref[both].reshape(2 * ROWS, width)
    out = resid + bias2
    up = jnp.zeros((2 * ROWS, width), f32)
    chunk = 768
    for c in range(hidden // chunk):
        cols = slice(c * chunk, (c + 1) * chunk)
        pre = mm(mlp_in, w1_ref[:, cols]) + bias1[:, cols]
        cdf = 0.5 * (1.0 + lax.erf(pre * (1.0 / math.sqrt(2.0))))
        hid = (pre * cdf).astype(bf16)
        dens = jnp.exp2(pre * pre * (-0.5 * LOG2E)) * (1.0 / math.sqrt(2.0 * math.pi))
        out = out + mm(hid, w2_ref[cols, :])
        gw2_ref[:, cols] += mm_tn(cot, hid)
        gpre = (mm_nt(cot, w2_ref[cols, :]) * (cdf + pre * dens)).astype(bf16)
        sb1_ref[:, cols] += fold8(gpre.astype(f32))
        gw1_ref[:, cols] += mm_tn(mlp_in, gpre)
        up = up + mm_nt(gpre, w1_ref[:, cols])
    narrow_into(flat_ref, step % 2 * 2 * FRAME, out)

    @pl.when(step % 2 == 1)
    def _():
        out_ref[...] = flat_ref[...].astype(bf16)

    cot32 = cot.astype(f32)
    gres = cot32 + norm_back(up, n2, inv2, gain2)
    gres_ref[...] = gres.reshape(2, ROWS, width)
    branch = gres.astype(bf16)
    gwo_ref[...] += mm_tn(att, branch)
    g = mm_nt(branch, wout_ref[...]).astype(bf16)
    g32 = g.astype(f32)
    inverse = li_ref[...].reshape(2 * ROWS, width)
    gs_ref[...] = (g32 * inverse).astype(bf16).reshape(2, ROWS, width)
    qs_ref[...] = (q_ref[both].reshape(2 * ROWS, width).astype(f32) * inverse).astype(bf16).reshape(2, ROWS, width)
    dots = g32 * o_ref[...]
    low2 = lax.broadcasted_iota(jnp.int32, (2 * ROWS, 128), 1) < 64
    for pair in range(HEADS // 2):
        cols = slice(128 * pair, 128 * pair + 128)
        d = dots[:, cols]
        even = jnp.sum(jnp.where(low2, d, 0.0), axis=-1, keepdims=True)
        odd = jnp.sum(jnp.where(low2, 0.0, d), axis=-1, keepdims=True)
        less = -jnp.where(low2, odd, even)
        one = less.astype(bf16)
        two = (less - one.astype(f32)).astype(bf16)
        three = (less - one.astype(f32) - two.astype(f32)).astype(bf16)
        zero = jnp.zeros_like(one)
        lanes = jnp.broadcast_to(lane, (2 * ROWS, 128))
        tail = jnp.where(lanes == 0, one, jnp.where(lanes == 1, two, jnp.where(lanes == 2, three, zero)))
        gp = g[:, cols]
        ga_ref[:, :, 256 * pair : 256 * pair + 128] = jnp.where(low2, gp, tail).reshape(2, ROWS, 128)
        ga_ref[:, :, 256 * pair + 128 : 256 * pair + 256] = jnp.where(low2, tail, gp).reshape(2, ROWS, 128)
    s384_ref[0] += fold8(up * n2)
    s384_ref[1] += fold8(up)
    s384_ref[2] += fold8(branch.astype(f32))
    s384_ref[3] += fold8(cot32)

    @pl.when(step == steps - 1)
    def _():
        at = pack_matrix(pack_ref, 0, gw1_ref[...])
        at = pack_matrix(pack_ref, at, gw2_ref[...])
        at = pack_matrix(pack_ref, at, gwo_ref[...])
        pack_rows(pack_ref, at, [colsum(s384_ref[i]) for i in range(4)] + [colsum(sb1_ref[...])])


class Rows:
    def __init__(self, stages, boards, sent, came):
        self.stages, self.boards, self.sent, self.came = stages, boards, sent, came
        self.first = [sum(s[2] - 1 for s in stages[:i]) for i in range(len(stages) + 1)]

    def _copies(self, i):
        stage = self.stages[i]
        here = self.boards[i].at[digit(stage)]
        for turn in range(1, stage[2]):
            slot = self.first[i] + turn - 1
            yield pltpu.make_async_remote_copy(
                src_ref=here,
                dst_ref=here,
                send_sem=self.sent.at[slot],
                recv_sem=self.came.at[slot],
                device_id=partner(stage, turn),
                device_id_type=MESH,
            )

    def spread(self, i, tile):
        self.boards[i][digit(self.stages[i])] = tile
        for copy in self._copies(i):
            copy.start()

    def settle(self, i):
        for copy in self._copies(i):
            copy.wait()
        total = self.boards[i][0]
        for j in range(1, self.stages[i][2]):
            total = total + self.boards[i][j]
        return total


def rows_scratch(stages):
    copies = sum(s[2] - 1 for s in stages)
    return [pltpu.VMEM((s[2], 16, 128), f32) for s in stages] + [pltpu.SemaphoreType.DMA((copies,))] * 2


def halves(units, devices):
    first = -(-units // (2 * devices)) * devices
    return first, units - first


def back_kernel(stages, prob_ref, kv_ref, ga_ref, gs_ref, qs_ref, li_ref, x_ref, gres_ref, gain_ref, shift_ref,
                wqkv_ref, pack_hbm, in_ref, res_ref, res2_ref, rows_ref,
                acc_ref, d_ref, ds_ref, dq_ref, gw_ref, sq_ref, s384_ref, own_ref, sum_ref, own2_ref, sum2_ref,
                ghost_ref, got_ref, ghost_sems, load_sem, *rest):
    step = pl.program_id(0)
    width = gs_ref.shape[-1]
    frames = x_ref.shape[0]
    steps = frames + 1 + frames // 2
    tm = lax.axis_index("tm")
    inv_scale = 1.0 / math.sqrt(width // HEADS)
    count = len(stages)
    last = count - 1
    devices = 2
    for stage in stages[1:]:
        devices *= stage[2]
    cut, _ = halves(own_ref.shape[0], devices)
    sums = []
    for n, (own, res) in enumerate(
        ((own_ref.at[:cut], sum_ref.at[:cut]), (own_ref.at[cut:], sum_ref.at[cut:]), (own2_ref, sum2_ref))
    ):
        mine = rest[n * (count + 2) : (n + 1) * (count + 2)]
        sums.append(Sum(stages, own, res, mine[:count], *mine[count:]))
    one, two, tail = sums
    extra = rest[3 * (count + 2) :]
    rows = Rows(stages, extra[:count], *extra[count:])
    load = pltpu.make_async_copy(pack_hbm, own_ref, load_sem)
    swap = pltpu.make_async_remote_copy(
        src_ref=ghost_ref,
        dst_ref=got_ref,
        send_sem=ghost_sems.at[0],
        recv_sem=ghost_sems.at[1],
        device_id=partner(stages[0], 1),
        device_id_type=MESH,
    )

    @pl.when(step == 0)
    def _():
        load.start()
        greet(stages)
        load.wait()
        one.send(0)
        two.send(0)
        acc_ref[...] = jnp.zeros_like(acc_ref)
        gw_ref[...] = jnp.zeros_like(gw_ref)
        sq_ref[...] = jnp.zeros_like(sq_ref)
        s384_ref[...] = jnp.zeros_like(s384_ref)

    def at(when, *todo):
        @pl.when(step == when)
        def _():
            for act, i in todo:
                act(i)

    at(1, (one.take, 0), (two.take, 0), (one.send, 1))
    if count == 3:
        at(5, (one.take, 1), (one.send, 2), (two.send, 1))
        at(8, (one.take, 2), (one.spread, 2))
        at(9, (two.take, 1), (two.send, 2))
        at(11, (one.settle, 2), (one.spread, 1))
        at(13, (two.take, 2), (two.spread, 2))
        at(frames, (one.settle, 1), (two.settle, 2), (one.spread, 0), (two.spread, 1))
    else:
        at(5, *[t for i in range(1, last) for t in ((one.take, i), (one.send, i + 1))], (two.send, 1))
        at(8, (one.take, last), (one.spread, last))
        at(9, *[t for i in range(1, last) for t in ((two.take, i), (two.send, i + 1))])
        at(11, *[t for i in range(last, 1, -1) for t in ((one.settle, i), (one.spread, i - 1))])
        at(13, (two.take, last), (two.spread, last))
        at(frames, (one.settle, 1), *[t for i in range(last, 1, -1) for t in ((two.settle, i), (two.spread, i - 1))],
           (one.spread, 0))

    low = lax.broadcasted_iota(jnp.int32, (ROWS, 128), 1) < 64
    wide_low = lax.broadcasted_iota(jnp.int32, (WIN, 128), 1) < 64
    ones = jnp.ones((WIN, 128), bf16)
    edge_rows = pl.ds(pl.multiple_of(jnp.where(tm == 0, frames, 1) * ROWS, 16), ROWS)
    ghost_rows = pl.ds(pl.multiple_of(jnp.where(tm == 0, frames + 1, 0) * ROWS, 16), ROWS)

    @pl.when(step < frames)
    def _():
        window = pl.ds(pl.multiple_of(step * ROWS, 16), WIN)

        def differ(h):
            at = width + h // 2 * 128
            wide = wide_low if h % 2 == 0 else ~wide_low
            v = jnp.where(wide, kv_ref[window, at : at + 128], ones)
            d_ref[h % 3] = mm_nt(ga_ref[0, :, 128 * h : 128 * h + 128], v)

        def weigh(h):
            ds_ref[h % 3] = (prob_ref[0, h].astype(f32) * d_ref[h % 3]).astype(bf16)

        held = {}

        def spend(h):
            cols = slice(h // 2 * 128, h // 2 * 128 + 128)
            vcols = slice(width + h // 2 * 128, width + h // 2 * 128 + 128)
            mine = slice(h % 2 * 64, h % 2 * 64 + 64)
            ds = ds_ref[h % 3]
            if h % 2 == 0:
                held["qt"], held["gt"] = qs_ref[0, :, cols].T, gs_ref[0, :, cols].T
            held[h] = mm(ds, kv_ref[window, cols]), mm(held["qt"][mine], ds), mm(held["gt"][mine], prob_ref[0, h])
            if h % 2:
                even, odd = held.pop(h - 1), held.pop(h)
                dq = jnp.where(low, even[0], odd[0]) * (li_ref[0, :, cols] * inv_scale)
                dq_ref[pl.ds(pl.multiple_of(step * ROWS, 16), ROWS), cols] = dq.astype(bf16)
                acc_ref[window, cols] += jnp.concatenate([even[1], odd[1]], axis=0).T
                acc_ref[window, vcols] += jnp.concatenate([even[2], odd[2]], axis=0).T

        differ(0)
        for h in range(HEADS + 1):
            if h + 1 < HEADS:
                differ(h + 1)
            if h >= 1:
                spend(h - 1)
            if h < HEADS:
                weigh(h)

    @pl.when(step == frames - 1)
    def _():
        ghost_ref[:, :width] = (acc_ref[ghost_rows, :width] * inv_scale).astype(bf16)
        ghost_ref[:, width:] = acc_ref[ghost_rows, width:].astype(bf16)
        swap.start()

    block = 2 * ROWS

    def block_of(i):
        x = x_ref[pl.ds(2 * i, 2)].reshape(block, width).astype(f32)
        n, inverse = normed_of(x)
        dq = dq_ref[pl.ds(pl.multiple_of(i * block, 16), block), :]
        here = pl.ds(pl.multiple_of(ROWS + i * block, 16), block)
        dk = (acc_ref[here, :width] * inv_scale).astype(bf16)
        dv = acc_ref[here, width:].astype(bf16)
        return n, inverse, jnp.concatenate([dq, dk, dv], axis=1)

    @pl.when(step == frames)
    def _():
        swap.wait()
        got = got_ref[...].astype(f32)
        acc_ref[edge_rows, :width] += got[:, :width] * (1.0 / inv_scale)
        acc_ref[edge_rows, width:] += got[:, width:]

        def weights(i, carry):
            n, _, grads = block_of(i)
            attn_in = (n * gain_ref[...] + shift_ref[...]).astype(bf16)
            gw_ref[...] += mm_tn(attn_in, grads)
            sq_ref[...] += fold8(grads.astype(f32))
            return carry

        lax.fori_loop(0, frames // 2, weights, 0)
        end = pack_matrix(own2_ref, 0, gw_ref[...])
        own2_ref[end:] = jnp.zeros((own2_ref.shape[0] - end, 16, 128), bf16)
        tail.send(0)

    at(frames + 3, (tail.take, 0), (tail.send, 1))

    @pl.when(step > frames)
    def _():
        n, inverse, grads = block_of(step - frames - 1)
        up = mm_nt(grads, wqkv_ref[...])
        gres = gres_ref[...].reshape(block, width)
        narrow_into(in_ref, 0, gres + norm_back(up, n, inverse, gain_ref[...]))
        s384_ref[0] += fold8(up * n)
        s384_ref[1] += fold8(up)

    @pl.when(step == steps - 1)
    def _():
        sq = colsum(sq_ref[...])
        parts = [colsum(s384_ref[0]), colsum(s384_ref[1]), sq[:, :width], sq[:, 2 * width :]]
        lines = [v[:, c : c + 128] for v in parts for c in range(0, width, 128)]
        lines += [jnp.zeros((1, 128), f32)] * (16 - len(lines))
        tile = jnp.concatenate(lines, axis=0)
        for i in range(1, count):
            tail.take(i)
            if i < last:
                tail.send(i + 1)
        for i in range(last, -1, -1):
            tail.spread(i)
            rows.spread(i, tile)
            if i == 1:
                two.settle(1)
                two.spread(0)
            if i == 0:
                one.settle(0)
                two.settle(0)
            tail.settle(i)
            tile = rows.settle(i)
        res_ref[...] = sum_ref[...]
        res2_ref[...] = sum2_ref[...]
        rows_ref[...] = tile


def unpack_kernel(res_ref, res2_ref, rows_ref, gg1, gb1, gqkv, gqv, gwo, gbo, gg2, gb2, gw1, gbf1, gw2, gbf2):
    width, hidden = gw1.shape
    tiles = width // 16
    at = 0
    for c in range(hidden // 128):
        gw1[:, 128 * c : 128 * c + 128] = res_ref[at : at + tiles].reshape(width, 128).astype(f32)
        at += tiles
    for c in range(hidden // 128):
        gw2[128 * c : 128 * c + 128, :] = res_ref[at : at + tiles].reshape(width, 128).astype(f32).T
        at += tiles
    for c in range(width // 128):
        gwo[:, 128 * c : 128 * c + 128] = res_ref[at : at + tiles].reshape(width, 128).astype(f32)
        at += tiles
    row = 0
    for out in (gg2, gb2, gbo, gbf2, gbf1):
        for c in range(out.shape[0] // 128):
            out[128 * c : 128 * c + 128] = res_ref[at + row // 16].astype(f32)[row % 16]
            row += 1
    at = 0
    for c in range(3 * width // 128):
        gqkv[:, 128 * c : 128 * c + 128] = res2_ref[at : at + tiles].reshape(width, 128).astype(f32)
        at += tiles
    rows = rows_ref[...]
    each = width // 128
    for i, out in enumerate((gg1, gb1)):
        for c in range(each):
            out[128 * c : 128 * c + 128] = rows[i * each + c]
    for i in range(2):
        for c in range(each):
            gqv[i : i + 1, 128 * c : 128 * c + 128] = rows[(i + 2) * each + c : (i + 2) * each + c + 1]


def whole(shape):
    return pl.BlockSpec(shape, lambda i: (0,) * len(shape), pipeline_mode=pl.Buffered(1))


def pairs(shape):
    return pl.BlockSpec((2,) + shape, lambda i: (i,) + (0,) * len(shape))


def single(shape):
    return pl.BlockSpec((1,) + shape, lambda i: (i,) + (0,) * len(shape))


def params(collective=None):
    if collective is None:
        return pltpu.CompilerParams(vmem_limit_bytes=60 * 2**20)
    return pltpu.CompilerParams(vmem_limit_bytes=60 * 2**20, collective_id=collective, has_side_effects=True)


def per_device(tokens, frame_clip, ln1_gain, ln1_bias, w_qkv, qv_bias, w_out, b_out, ln2_gain, ln2_bias,
               w_fc1, b_fc1, w_fc2, b_fc2, cotangent):
    count, width = tokens.shape
    hidden = w_fc1.shape[1]
    frames = count // FRAME
    steps = frames // 2
    tm = lax.axis_index("tm")
    edge = jnp.where(tm == 0, tokens[count - FRAME :], tokens[:FRAME])
    ghost = jnp.pad(lax.ppermute(edge, "tm", [(0, 1), (1, 0)]), ((0, ROWS - FRAME), (0, 0)))
    row = jnp.concatenate(
        [ln1_gain, ln1_bias, qv_bias[0], jnp.zeros((width,), bf16), qv_bias[1], b_out, ln2_gain, ln2_bias, b_fc2, b_fc1]
    ).astype(f32)[None]
    kv_rows = (frames + 2) * ROWS + WIN - 3 * ROWS
    shape = jax.ShapeDtypeStruct
    stages = stages_of(lax.axis_size("clips"))
    devices = 2 * lax.axis_size("clips")
    tiles = width // 16
    units = units_for((2 * hidden + width) // 128 * tiles + 2, devices)
    units2 = units_for(3 * width // 128 * tiles + 1, devices)
    x_pad, kv, prob, block_out, qs, ga, gs, gres, li, pack = pl.pallas_call(
        forward_kernel,
        grid=(steps,),
        in_specs=[
            pl.BlockSpec(memory_space=pltpu.SMEM),
            whole((count, width)),
            whole((ROWS, width)),
            whole((count, width)),
            whole(row.shape),
            whole((width, 3 * width)),
            whole((width, width)),
            whole((width, hidden)),
            whole((hidden, width)),
        ],
        out_specs=[
            whole((frames, ROWS, width)),
            whole((kv_rows, 2 * width)),
            pairs((HEADS, ROWS, WIN)),
            pl.BlockSpec((4 * FRAME, width), lambda i: (i // 2, 0)),
            pairs((ROWS, width)),
            pairs((ROWS, 2 * width)),
            pairs((ROWS, width)),
            pairs((ROWS, width)),
            pairs((ROWS, width)),
            whole((units, 16, 128)),
        ],
        out_shape=[
            shape((frames, ROWS, width), bf16),
            shape((kv_rows, 2 * width), bf16),
            shape((frames, HEADS, ROWS, WIN), bf16),
            shape((count, width), bf16),
            shape((frames, ROWS, width), bf16),
            shape((frames, ROWS, 2 * width), bf16),
            shape((frames, ROWS, width), bf16),
            shape((frames, ROWS, width), f32),
            shape((frames, ROWS, width), f32),
            shape((units, 16, 128), bf16),
        ],
        scratch_shapes=[
            pltpu.VMEM((frames, ROWS, width), bf16),
            pltpu.VMEM((frames, ROWS, width), bf16),
            pltpu.VMEM((kv_rows, 128), bf16),
            pltpu.VMEM((3, ROWS, WIN), f32),
            pltpu.VMEM((2 * ROWS, width), f32),
            pltpu.VMEM((4 * FRAME, width), f32),
            pltpu.VMEM((width, hidden), f32),
            pltpu.VMEM((width, hidden), f32),
            pltpu.VMEM((width, width), f32),
            pltpu.VMEM((8, hidden), f32),
            pltpu.VMEM((4, 8, width), f32),
        ],
        compiler_params=params(),
    )(frame_clip, tokens, ghost, cotangent, row, w_qkv, w_out, w_fc1, w_fc2)

    first, second = halves(units, devices)
    early = lambda sh: pl.BlockSpec((1,) + sh, lambda i: (jnp.minimum(i, frames - 1),) + (0,) * len(sh))
    late = lambda i: jnp.maximum(i - frames - 1, 0)
    in_vmem = pl.BlockSpec(memory_space=pltpu.VMEM)
    input_grad, res, res2, sums = pl.pallas_call(
        functools.partial(back_kernel, stages),
        grid=(frames + 1 + steps,),
        in_specs=[
            early((HEADS, ROWS, WIN)),
            whole((kv_rows, 2 * width)),
            early((ROWS, 2 * width)),
            early((ROWS, width)),
            early((ROWS, width)),
            early((ROWS, width)),
            whole((frames, ROWS, width)),
            pl.BlockSpec((2, ROWS, width), lambda i: (late(i), 0, 0)),
            whole((1, width)),
            whole((1, width)),
            whole((width, 3 * width)),
            pl.BlockSpec(memory_space=pl.ANY),
        ],
        out_specs=[
            pl.BlockSpec((2 * FRAME, width), lambda i: (late(i), 0)),
            whole((units, 16, 128)),
            whole((units2, 16, 128)),
            whole((16, 128)),
        ],
        out_shape=[
            shape((count, width), f32),
            shape((units, 16, 128), bf16),
            shape((units2, 16, 128), bf16),
            shape((16, 128), f32),
        ],
        scratch_shapes=[
            pltpu.VMEM((kv_rows, 2 * width), f32),
            pltpu.VMEM((3, ROWS, WIN), f32),
            pltpu.VMEM((3, ROWS, WIN), bf16),
            pltpu.VMEM((frames * ROWS, width), bf16),
            pltpu.VMEM((width, 3 * width), f32),
            pltpu.VMEM((8, 3 * width), f32),
            pltpu.VMEM((2, 8, width), f32),
            pltpu.VMEM((units, 16, 128), bf16),
            pltpu.VMEM((units, 16, 128), bf16),
            pltpu.VMEM((units2, 16, 128), bf16),
            pltpu.VMEM((units2, 16, 128), bf16),
            pltpu.VMEM((ROWS, 2 * width), bf16),
            pltpu.VMEM((ROWS, 2 * width), bf16),
            pltpu.SemaphoreType.DMA((2,)),
            pltpu.SemaphoreType.DMA,
        ]
        + sum_scratch(stages, first)
        + sum_scratch(stages, second)
        + sum_scratch(stages, units2)
        + rows_scratch(stages),
        compiler_params=params(0),
    )(prob, kv, ga, gs, qs, li, x_pad, gres, row[:, :width], row[:, width : 2 * width], w_qkv, pack)

    sizes = [(width,), (width,), (width, 3 * width), (2, width), (width, width), (width,), (width,), (width,),
             (width, hidden), (hidden,), (hidden, width), (width,)]
    grads = pl.pallas_call(
        unpack_kernel,
        in_specs=[in_vmem] * 3,
        out_specs=[in_vmem] * len(sizes),
        out_shape=[shape(s, f32) for s in sizes],
        compiler_params=params(),
    )(res, res2, sums)
    return (block_out, input_grad) + tuple(grads)


def solution(mesh):
    rows = P(("clips", "tm"), None)
    rep = P()
    return jax.shard_map(
        per_device,
        mesh=mesh,
        in_specs=(rows, P("clips")) + (rep,) * 12 + (rows,),
        out_specs=(rows, rows) + (rep,) * 12,
        check_vma=False,
    )
```

time: 293 us -> 202 us (0.69)
  Pallas kernels: 239 us -> 187 us
  local copies, waits for them, and re-layouts: 49.2 us -> 12.3 us
    pallas_call x3 -> x2, Pallas kernels: 127 us -> 95.6 us  [the longest x1 90.1 us: per_device(): pl.pallas_call(functools.partial(back_kernel, stages), grid=(frames + 1 +...]
    pallas_call x1, Pallas kernels: 112 us -> 91 us  [per_device(): pl.pallas_call(forward_kernel, grid=(steps,), in_specs=[pl.BlockSpec(memo...]
    reshape x12 -> x0, local copies, waits for them, and re-layouts: 18.5 us -> none  [the longest x1 5.24 us: per_device(): input_grad = in_pad[:, :FRAME].reshape(count, width)]
    slice x12 -> x1, local copies, waits for them, and re-layouts: 12.2 us -> 0.57 us  [per_device(): row[:, width:2 * width]]
    pad x3 -> x1, local copies, waits for them, and re-layouts: 5.89 us -> 0.68 us  [per_device(): jnp.pad(lax.ppermute(edge, 'tm', [(0, 1), (1, 0)]), ((0, ROWS - FRAME), (...]
    unnamed x29 -> x10, local copies, waits for them, and re-layouts: 9.16 us -> 10.4 us
  transfers between devices with their start and end apart: 2 -> 1, of which waited for: 0 -> 0; matrix products, arithmetic and copies ran while one was open for 11% -> 4% of each run, Pallas kernels for 0% -> 0%
where the time goes in v3:
time: 202 us
  Pallas kernels  187 us (93%)
  local copies, waits for them, and re-layouts  12.3 us (6%)
    pallas_call x1, Pallas kernels, per_device(): pl.pallas_call(forward_kernel, grid=(steps,), in_specs=[pl.BlockSpec(memo...  91 us
    pallas_call x1, Pallas kernels, per_device(): pl.pallas_call(functools.partial(back_kernel, stages), grid=(frames + 1 +...  90.1 us
    unnamed x10, local copies, waits for them, and re-layouts  10.4 us
    pallas_call x1, Pallas kernels, per_device(): pl.pallas_call(unpack_kernel, in_specs=[in_vmem] * 3, out_specs=[in_vmem]...  5.5 us
  transfers between devices with their start and end apart: 1, of which 0 were waited for; matrix products, arithmetic and copies ran while one was open for 4% of the time, Pallas kernels for 0%

profile of v3, /device:TPU:0, one launch (start us, length us, event | category | flops | bytes accessed | tf_op | source)
XLA Modules:
  0.0 201.9 jit_solution(2827041912999245665)
XLA Ops:
  0.6 1.0 slice_select_fusion
  1.7 0.5 collective-permute-start
  2.2 0.7 constant_dynamic-update-slice_fusion.9
  2.9 0.7 constant_dynamic-update-slice_fusion.8
  3.6 0.7 constant_dynamic-update-slice_fusion.7
  4.3 0.7 constant_dynamic-update-slice_fusion.5
  5.0 0.7 constant_dynamic-update-slice_fusion.4
  5.7 0.7 constant_dynamic-update-slice_fusion.3
  6.3 0.7 constant_dynamic-update-slice_fusion.2
  7.0 0.7 constant_dynamic-update-slice_fusion.1
  7.7 0.7 constant_dynamic-update-slice_fusion
  8.4 0.6 convert_element_type.12.row_ref
  9.0 0.6 fusion
  9.6 0.0 collective-permute-done
  9.6 0.7 pad.4.ghost_ref
  10.3 91.0 %shard_map.254 = (bf16[16,208,384]{2,1,0:T(8,128)(2,1)}, bf16[3760,768]{1,0:T(8,128)(2,1)}, bf16[16,6,208,640]{3,2,1,0:T(8,128)(2,1)}, bf16[3136,384]{1,0:T(8,12...) custom-call(s32[32]{0:T(128)} %clip_ref.1, ...), custom_call_target="tpu_custom_call" | custom-call | tf_op jit(solution)/shard_map/pallas_call | solution.py:735
  101.3 90.1 %shard_map.255 = (f32[3136,384]{1,0:T(8,128)}, bf16[672,16,128]{2,1,0:T(8,128)(2,1)}, bf16[224,16,128]{2,1,0:T(8,128)(2,1)}, f32[16,128]{1,0:T(8,128)}) custom-call(bf16[16,6,208,640]{3,2,1,0:T(8,128)(2,1)} %get-tuple-element.41.prob_ref, bf16[3760,768]{1,0:T(8,128)(2,1)} %get-tuple-element.42.kv_ref, bf16[16,208,768]{2,1,0:T(8,128)(2,1)} %get-tuple-element.43.ga_ref, ...), custom_call_target="tpu_custom_call" | custom-call | tf_op jit(solution)/shard_map/pallas_call | solution.py:793
  191.5 5.5 %shard_map.256 = (f32[384]{0:T(512)}, f32[384]{0:T(512)}, f32[384,1152]{1,0:T(8,128)}, f32[2,384]{1,0:T(2,128)}, f32[384,384]{1,0:T(8,128)}, /*index=5*/f32[384]...) custom-call(bf16[672,16,128]{2,1,0:T(8,128)(2,1)} %get-tuple-element, ...), custom_call_target="tpu_custom_call" | custom-call | tf_op jit(solution)/shard_map/pallas_call | solution.py:848
  197.0 4.9 %copy.39 = f32[3136,384]{1,0:T(8,128)} copy(f32[3136,384]{1,0:T(8,128)} %get-tuple-element.83) | data formatting | bytes 9633792
  (1 shorter events, 0.0 us)
Async XLA Ops:
  1.7 7.9 %collective-permute-start = (bf16[196,384]{1,0:T(8,128)(2,1)S(1)}, bf16[196,384]{1,0:T(8,128)(2,1)S(1)}, u32[]{:S(2)}, u32[]{:S(2)}) collective-permute-start(bf16[196,384]{1,0:T(8,128)(2,1)S(1)} %slice_select_fusion), channel_id=1, source_target_pairs={{0,1},{1,0},{2,3},{3,2},{4,5},{5,4},{6,7},{7,6},{8,9},{9,8},{10,11... | collective-permute-start | bytes 451592 | tf_op jit(solution)/shard_map/ppermute | solution.py:724

commit v4 on v3

--- a/solution.py
+++ b/solution.py
@@ -221,14 +221,21 @@
     clip_ref,
     tok_ref,
     ghost_ref,
-    cot_ref,
-    row_ref,
+    g1_ref,
+    s1_ref,
+    qv_ref,
+    bo_ref,
+    g2_ref,
+    s2_ref,
+    bf1_ref,
+    bf2_ref,
     wqkv_ref,
-    wout_ref,
-    w1_ref,
-    w2_ref,
-    x_ref,
-    kv_ref,
+    cot_hbm,
+    wout_hbm,
+    w1_hbm,
+    w2_hbm,
+    x_hbm,
+    kv_hbm,
     prob_ref,
     out_ref,
     qs_ref,
@@ -236,7 +243,14 @@
     gs_ref,
     gres_ref,
     li_ref,
+    row_ref,
     pack_ref,
+    x_ref,
+    kv_ref,
+    cot_ref,
+    wout_ref,
+    w1_ref,
+    w2_ref,
     q_ref,
     cp_ref,
     flag_ref,
@@ -248,13 +262,34 @@
     gwo_ref,
     sb1_ref,
     s384_ref,
+    sems,
 ):
     step = pl.program_id(0)
     steps = pl.num_programs(0)
-    frames = 2 * steps
+    frames = x_ref.shape[0]
     width = x_ref.shape[-1]
     hidden = w1_ref.shape[-1]
     tm = lax.axis_index("tm")
+    copies = [
+        pltpu.make_async_copy(src, dst, sems.at[i])
+        for i, (src, dst) in enumerate(
+            ((cot_hbm, cot_ref), (wout_hbm, wout_ref), (w1_hbm, w1_ref), (w2_hbm, w2_ref), (x_ref, x_hbm), (kv_ref, kv_hbm))
+        )
+    ]
+
+    @pl.when(step == 0)
+    def _():
+        for copy in copies[:4]:
+            copy.start()
+        vectors = [g1_ref[...], s1_ref[...], None, None, None, bo_ref[...], g2_ref[...], s2_ref[...], bf2_ref[...]]
+        for i, v in enumerate(vectors):
+            if v is not None:
+                row_ref[:, i * width : (i + 1) * width] = v.astype(f32)[None, :]
+        row_ref[:, 2 * width : 3 * width] = qv_ref[0:1, :].astype(f32)
+        row_ref[:, 3 * width : 4 * width] = jnp.zeros((1, width), f32)
+        row_ref[:, 4 * width : 5 * width] = qv_ref[1:2, :].astype(f32)
+        row_ref[:, 9 * width :] = bf1_ref[...].astype(f32)[None, :]
+
     vec = lambda i, n=width: row_ref[:, i * width : i * width + n]
     gain1, shift1, bias3, biaso, gain2, shift2, bias2, bias1 = (
         vec(0), vec(1), vec(2, 3 * width), vec(5), vec(6), vec(7), vec(8), vec(9, hidden))
@@ -280,29 +315,40 @@
         kv_ref[(frames + 2) * ROWS :, :] = jnp.zeros((WIN - 3 * ROWS, 2 * width), bf16)
 
         x = ghost_ref[...].astype(f32)
+        x = jnp.where(tm == 0, x, pltpu.roll(x, FRAME, 0))
         n, _ = normed_of(x)
         kv = mm((n * gain1 + shift1).astype(bf16), wqkv_ref[:, width:]) + bias3[:, width:]
         kv_ref[pl.ds(pl.multiple_of(ghost_slot * ROWS, 16), ROWS), :] = kv.astype(bf16)
 
-        def pad(i, carry):
+        def pad(i, src, dst):
             for which in range(4):
-                for src, dst in ((tok_ref, x_ref), (cot_ref, cp_ref)):
-                    v, end = widen(src, i, which)
-                    dst[4 * i + which, : ROWS - 16] = v[: ROWS - 16].astype(bf16)
-                    dst[4 * i + which, ROWS - 16 :] = end.astype(bf16)
-            return carry
-
-        lax.fori_loop(0, frames // 4, pad, 0)
-
-        def project(i, carry):
-            x = x_ref[pl.ds(2 * i, 2)].reshape(2 * ROWS, width).astype(f32)
+                v, end = widen(src, i, which)
+                dst[4 * i + which, : ROWS - 16] = v[: ROWS - 16].astype(bf16)
+                dst[4 * i + which, ROWS - 16 :] = end.astype(bf16)
+
+        def ready(i):
+            x = x_ref[4 * i : 4 * i + 4].reshape(4 * ROWS, width).astype(f32)
             n, _ = normed_of(x)
-            qkv = (mm((n * gain1 + shift1).astype(bf16), wqkv_ref[...]) + bias3).astype(bf16)
-            q_ref[pl.ds(2 * i, 2)] = qkv[:, :width].reshape(2, ROWS, width)
-            kv_ref[pl.ds(pl.multiple_of((2 * i + 1) * ROWS, 16), 2 * ROWS), :] = qkv[:, width:]
-            return carry
-
-        lax.fori_loop(0, frames // 2, project, 0)
+            return (n * gain1 + shift1).astype(bf16)
+
+        def project(i, normed):
+            qkv = (mm(normed, wqkv_ref[...]) + bias3).astype(bf16)
+            q_ref[4 * i : 4 * i + 4] = qkv[:, :width].reshape(4, ROWS, width)
+            kv_ref[(4 * i + 1) * ROWS : (4 * i + 5) * ROWS, :] = qkv[:, width:]
+
+        for i in range(frames // 4):
+            pad(i, tok_ref, x_ref)
+        normed = ready(0)
+        for i in range(frames // 4):
+            following = ready(i + 1) if i + 1 < frames // 4 else None
+            project(i, normed)
+            normed = following
+        for copy in copies[4:]:
+            copy.start()
+        for copy in copies[:4]:
+            copy.wait()
+        for i in range(frames // 4):
+            pad(i, cot_ref, cp_ref)
 
     low = lax.broadcasted_iota(jnp.int32, (ROWS, 128), 1) < 64
     wide_low = lax.broadcasted_iota(jnp.int32, (WIN, 128), 1) < 64
@@ -370,33 +416,42 @@
     n2, inv2 = normed_of(resid)
     mlp_in = (n2 * gain2 + shift2).astype(bf16)
     cot = cp_ref[both].reshape(2 * ROWS, width)
-    out = resid + bias2
-    up = jnp.zeros((2 * ROWS, width), f32)
-    chunk = 768
-    for c in range(hidden // chunk):
-        cols = slice(c * chunk, (c + 1) * chunk)
-        pre = mm(mlp_in, w1_ref[:, cols]) + bias1[:, cols]
-        cdf = 0.5 * (1.0 + lax.erf(pre * (1.0 / math.sqrt(2.0))))
-        hid = (pre * cdf).astype(bf16)
+    chunk = 512
+    chunks = [slice(c, c + chunk) for c in range(0, hidden, chunk)]
+    held = {}
+
+    def start(c):
+        held[c] = mm(mlp_in, w1_ref[:, chunks[c]]), mm_nt(cot, w2_ref[chunks[c], :])
+
+    def middle(c):
+        pre, ghid = held[c]
+        pre = pre + bias1[:, chunks[c]]
+        cdf = 0.5 + 0.5 * lax.erf(pre * (1.0 / math.sqrt(2.0)))
         dens = jnp.exp2(pre * pre * (-0.5 * LOG2E)) * (1.0 / math.sqrt(2.0 * math.pi))
-        out = out + mm(hid, w2_ref[cols, :])
-        gw2_ref[:, cols] += mm_tn(cot, hid)
-        gpre = (mm_nt(cot, w2_ref[cols, :]) * (cdf + pre * dens)).astype(bf16)
-        sb1_ref[:, cols] += fold8(gpre.astype(f32))
-        gw1_ref[:, cols] += mm_tn(mlp_in, gpre)
-        up = up + mm_nt(gpre, w1_ref[:, cols])
-    narrow_into(flat_ref, step % 2 * 2 * FRAME, out)
-
-    @pl.when(step % 2 == 1)
-    def _():
-        out_ref[...] = flat_ref[...].astype(bf16)
-
+        gpre = (ghid * (cdf + pre * dens)).astype(bf16)
+        sb1_ref[:, chunks[c]] += fold8(gpre.astype(f32))
+        held[c] = (pre * cdf).astype(bf16), gpre
+
+    def weights(c):
+        gw2_ref[:, chunks[c]] += mm_tn(cot, held[c][0])
+        gw1_ref[:, chunks[c]] += mm_tn(mlp_in, held[c][1])
+
+    start(0)
+    for c in range(len(chunks)):
+        if c + 1 < len(chunks):
+            start(c + 1)
+        middle(c)
+    hid = jnp.concatenate([held[c][0] for c in range(len(chunks))], axis=1)
+    gpre = jnp.concatenate([held[c][1] for c in range(len(chunks))], axis=1)
+    up = mm_nt(gpre, w1_ref[...])
     cot32 = cot.astype(f32)
     gres = cot32 + norm_back(up, n2, inv2, gain2)
     gres_ref[...] = gres.reshape(2, ROWS, width)
     branch = gres.astype(bf16)
-    gwo_ref[...] += mm_tn(att, branch)
+    weights(0)
     g = mm_nt(branch, wout_ref[...]).astype(bf16)
+    for c in range(1, len(chunks) - 1):
+        weights(c)
     g32 = g.astype(f32)
     inverse = li_ref[...].reshape(2 * ROWS, width)
     gs_ref[...] = (g32 * inverse).astype(bf16).reshape(2, ROWS, width)
@@ -422,6 +477,14 @@
     s384_ref[1] += fold8(up)
     s384_ref[2] += fold8(branch.astype(f32))
     s384_ref[3] += fold8(cot32)
+    weights(len(chunks) - 1)
+    gwo_ref[...] += mm_tn(att, branch)
+    out = resid + bias2 + mm(hid, w2_ref[...])
+    narrow_into(flat_ref, step % 2 * 2 * FRAME, out)
+
+    @pl.when(step % 2 == 1)
+    def _():
+        out_ref[...] = flat_ref[...].astype(bf16)
 
     @pl.when(step == steps - 1)
     def _():
@@ -429,6 +492,8 @@
         at = pack_matrix(pack_ref, at, gw2_ref[...])
         at = pack_matrix(pack_ref, at, gwo_ref[...])
         pack_rows(pack_ref, at, [colsum(s384_ref[i]) for i in range(4)] + [colsum(sb1_ref[...])])
+        for copy in copies[4:]:
+            copy.wait()
 
 
 class Rows:
@@ -474,13 +539,13 @@
     return first, units - first
 
 
-def back_kernel(stages, prob_ref, kv_ref, ga_ref, gs_ref, qs_ref, li_ref, x_ref, gres_ref, gain_ref, shift_ref,
-                wqkv_ref, pack_hbm, in_ref, res_ref, res2_ref, rows_ref,
+def back_kernel(stages, prob_ref, kv_hbm, ga_ref, gs_ref, qs_ref, li_ref, x_hbm, gres_ref, row_ref,
+                wqkv_hbm, pack_hbm, in_ref, res_ref, res2_ref, rows_ref,
                 acc_ref, d_ref, ds_ref, dq_ref, gw_ref, sq_ref, s384_ref, own_ref, sum_ref, own2_ref, sum2_ref,
-                ghost_ref, got_ref, ghost_sems, load_sem, *rest):
+                ghost_ref, got_ref, kv_ref, x_ref, wqkv_ref, ghost_sems, load_sems, *rest):
     step = pl.program_id(0)
     width = gs_ref.shape[-1]
-    frames = x_ref.shape[0]
+    frames = x_hbm.shape[0]
     steps = frames + 1 + frames // 2
     tm = lax.axis_index("tm")
     inv_scale = 1.0 / math.sqrt(width // HEADS)
@@ -499,7 +564,19 @@
     one, two, tail = sums
     extra = rest[3 * (count + 2) :]
     rows = Rows(stages, extra[:count], *extra[count:])
-    load = pltpu.make_async_copy(pack_hbm, own_ref, load_sem)
+    near = 6 * ROWS
+    loads = [
+        pltpu.make_async_copy(src, dst, load_sems.at[i])
+        for i, (src, dst) in enumerate(
+            (
+                (pack_hbm, own_ref),
+                (kv_hbm.at[:near], kv_ref.at[:near]),
+                (kv_hbm.at[near:], kv_ref.at[near:]),
+                (x_hbm, x_ref),
+                (wqkv_hbm, wqkv_ref),
+            )
+        )
+    ]
     swap = pltpu.make_async_remote_copy(
         src_ref=ghost_ref,
         dst_ref=got_ref,
@@ -511,15 +588,21 @@
 
     @pl.when(step == 0)
     def _():
-        load.start()
+        for load in loads:
+            load.start()
         greet(stages)
-        load.wait()
+        loads[0].wait()
         one.send(0)
         two.send(0)
         acc_ref[...] = jnp.zeros_like(acc_ref)
         gw_ref[...] = jnp.zeros_like(gw_ref)
         sq_ref[...] = jnp.zeros_like(sq_ref)
         s384_ref[...] = jnp.zeros_like(s384_ref)
+        loads[1].wait()
+
+    @pl.when(step == 1)
+    def _():
+        loads[2].wait()
 
     def at(when, *todo):
         @pl.when(step == when)
@@ -608,6 +691,8 @@
 
     @pl.when(step == frames)
     def _():
+        loads[3].wait()
+        loads[4].wait()
         swap.wait()
         got = got_ref[...].astype(f32)
         acc_ref[edge_rows, :width] += got[:, :width] * (1.0 / inv_scale)
@@ -615,7 +700,7 @@
 
         def weights(i, carry):
             n, _, grads = block_of(i)
-            attn_in = (n * gain_ref[...] + shift_ref[...]).astype(bf16)
+            attn_in = (n * row_ref[:, :width] + row_ref[:, width : 2 * width]).astype(bf16)
             gw_ref[...] += mm_tn(attn_in, grads)
             sq_ref[...] += fold8(grads.astype(f32))
             return carry
@@ -632,7 +717,7 @@
         n, inverse, grads = block_of(step - frames - 1)
         up = mm_nt(grads, wqkv_ref[...])
         gres = gres_ref[...].reshape(block, width)
-        narrow_into(in_ref, 0, gres + norm_back(up, n, inverse, gain_ref[...]))
+        narrow_into(in_ref, 0, gres + norm_back(up, n, inverse, row_ref[:, :width]))
         s384_ref[0] += fold8(up * n)
         s384_ref[1] += fold8(up)
 
@@ -663,28 +748,58 @@
         rows_ref[...] = tile
 
 
-def unpack_kernel(res_ref, res2_ref, rows_ref, gg1, gb1, gqkv, gqv, gwo, gbo, gg2, gb2, gw1, gbf1, gw2, gbf2):
+def unpack_kernel(in_hbm, res_hbm, res2_ref, rows_ref, out_hbm, gg1, gb1, gqkv_hbm, gqv, gwo_hbm, gbo, gg2, gb2, gw1_hbm,
+                  gbf1, gw2_hbm, gbf2, gqkv, gwo, gw1, gw2, res_ref, mid_ref, sems):
     width, hidden = gw1.shape
     tiles = width // 16
+    across = hidden // 128 * tiles
+    pieces = 4
+    piece = in_hbm.shape[0] // pieces
+    come, go = [], []
+    for i in range(pieces):
+        rows = slice(i * piece, (i + 1) * piece)
+        come.append(pltpu.make_async_copy(in_hbm.at[rows], mid_ref.at[rows], sems.at[7 + i]))
+        go.append(pltpu.make_async_copy(mid_ref.at[rows], out_hbm.at[rows], sems.at[7 + pieces + i]))
+    parts = (0, across, 2 * across, res_hbm.shape[0])
+    loads = [
+        pltpu.make_async_copy(res_hbm.at[lo:hi], res_ref.at[lo:hi], sems.at[i])
+        for i, (lo, hi) in enumerate(zip(parts, parts[1:]))
+    ]
+    stores = [
+        pltpu.make_async_copy(src, dst, sems.at[3 + i])
+        for i, (src, dst) in enumerate(((gqkv, gqkv_hbm), (gwo, gwo_hbm), (gw1, gw1_hbm), (gw2, gw2_hbm)))
+    ]
+    for copy in loads + come:
+        copy.start()
+    at = 0
+    for c in range(3 * width // 128):
+        gqkv[:, 128 * c : 128 * c + 128] = res2_ref[at : at + tiles].reshape(width, 128).astype(f32)
+        at += tiles
+    stores[0].start()
+    loads[0].wait()
     at = 0
     for c in range(hidden // 128):
         gw1[:, 128 * c : 128 * c + 128] = res_ref[at : at + tiles].reshape(width, 128).astype(f32)
         at += tiles
+    stores[2].start()
+    for i in range(pieces):
+        come[i].wait()
+        go[i].start()
+    loads[1].wait()
     for c in range(hidden // 128):
         gw2[128 * c : 128 * c + 128, :] = res_ref[at : at + tiles].reshape(width, 128).astype(f32).T
         at += tiles
+    stores[3].start()
+    loads[2].wait()
     for c in range(width // 128):
         gwo[:, 128 * c : 128 * c + 128] = res_ref[at : at + tiles].reshape(width, 128).astype(f32)
         at += tiles
+    stores[1].start()
     row = 0
     for out in (gg2, gb2, gbo, gbf2, gbf1):
         for c in range(out.shape[0] // 128):
             out[128 * c : 128 * c + 128] = res_ref[at + row // 16].astype(f32)[row % 16]
             row += 1
-    at = 0
-    for c in range(3 * width // 128):
-        gqkv[:, 128 * c : 128 * c + 128] = res2_ref[at : at + tiles].reshape(width, 128).astype(f32)
-        at += tiles
     rows = rows_ref[...]
     each = width // 128
     for i, out in enumerate((gg1, gb1)):
@@ -693,6 +808,8 @@
     for i in range(2):
         for c in range(each):
             gqv[i : i + 1, 128 * c : 128 * c + 128] = rows[(i + 2) * each + c : (i + 2) * each + c + 1]
+    for copy in stores + go:
+        copy.wait()
 
 
 def whole(shape):
@@ -720,11 +837,10 @@
     frames = count // FRAME
     steps = frames // 2
     tm = lax.axis_index("tm")
-    edge = jnp.where(tm == 0, tokens[count - FRAME :], tokens[:FRAME])
-    ghost = jnp.pad(lax.ppermute(edge, "tm", [(0, 1), (1, 0)]), ((0, ROWS - FRAME), (0, 0)))
-    row = jnp.concatenate(
-        [ln1_gain, ln1_bias, qv_bias[0], jnp.zeros((width,), bf16), qv_bias[1], b_out, ln2_gain, ln2_bias, b_fc2, b_fc1]
-    ).astype(f32)[None]
+    edge = jnp.where(tm == 0, tokens[count - ROWS :], tokens[:ROWS])
+    ghost = lax.ppermute(edge, "tm", [(0, 1), (1, 0)])
+    in_vmem = pl.BlockSpec(memory_space=pltpu.VMEM)
+    in_hbm = pl.BlockSpec(memory_space=pl.ANY)
     kv_rows = (frames + 2) * ROWS + WIN - 3 * ROWS
     shape = jax.ShapeDtypeStruct
     stages = stages_of(lax.axis_size("clips"))
@@ -732,23 +848,30 @@
     tiles = width // 16
     units = units_for((2 * hidden + width) // 128 * tiles + 2, devices)
     units2 = units_for(3 * width // 128 * tiles + 1, devices)
-    x_pad, kv, prob, block_out, qs, ga, gs, gres, li, pack = pl.pallas_call(
+    x_pad, kv, prob, block_out, qs, ga, gs, gres, li, row, pack = pl.pallas_call(
         forward_kernel,
         grid=(steps,),
         in_specs=[
             pl.BlockSpec(memory_space=pltpu.SMEM),
             whole((count, width)),
             whole((ROWS, width)),
-            whole((count, width)),
-            whole(row.shape),
+            whole((width,)),
+            whole((width,)),
+            whole((2, width)),
+            whole((width,)),
+            whole((width,)),
+            whole((width,)),
+            whole((hidden,)),
+            whole((width,)),
             whole((width, 3 * width)),
-            whole((width, width)),
-            whole((width, hidden)),
-            whole((hidden, width)),
+            in_hbm,
+            in_hbm,
+            in_hbm,
+            in_hbm,
         ],
         out_specs=[
-            whole((frames, ROWS, width)),
-            whole((kv_rows, 2 * width)),
+            in_hbm,
+            in_hbm,
             pairs((HEADS, ROWS, WIN)),
             pl.BlockSpec((4 * FRAME, width), lambda i: (i // 2, 0)),
             pairs((ROWS, width)),
@@ -756,6 +879,7 @@
             pairs((ROWS, width)),
             pairs((ROWS, width)),
             pairs((ROWS, width)),
+            whole((1, 9 * width + hidden)),
             whole((units, 16, 128)),
         ],
         out_shape=[
@@ -768,9 +892,16 @@
             shape((frames, ROWS, width), bf16),
             shape((frames, ROWS, width), f32),
             shape((frames, ROWS, width), f32),
+            shape((1, 9 * width + hidden), f32),
             shape((units, 16, 128), bf16),
         ],
         scratch_shapes=[
+            pltpu.VMEM((frames, ROWS, width), bf16),
+            pltpu.VMEM((kv_rows, 2 * width), bf16),
+            pltpu.VMEM((count, width), bf16),
+            pltpu.VMEM((width, width), bf16),
+            pltpu.VMEM((width, hidden), bf16),
+            pltpu.VMEM((hidden, width), bf16),
             pltpu.VMEM((frames, ROWS, width), bf16),
             pltpu.VMEM((frames, ROWS, width), bf16),
             pltpu.VMEM((kv_rows, 128), bf16),
@@ -782,30 +913,30 @@
             pltpu.VMEM((width, width), f32),
             pltpu.VMEM((8, hidden), f32),
             pltpu.VMEM((4, 8, width), f32),
+            pltpu.SemaphoreType.DMA((6,)),
         ],
         compiler_params=params(),
-    )(frame_clip, tokens, ghost, cotangent, row, w_qkv, w_out, w_fc1, w_fc2)
+    )(frame_clip, tokens, ghost, ln1_gain, ln1_bias, qv_bias, b_out, ln2_gain, ln2_bias, b_fc1, b_fc2, w_qkv, cotangent,
+      w_out, w_fc1, w_fc2)
 
     first, second = halves(units, devices)
     early = lambda sh: pl.BlockSpec((1,) + sh, lambda i: (jnp.minimum(i, frames - 1),) + (0,) * len(sh))
     late = lambda i: jnp.maximum(i - frames - 1, 0)
-    in_vmem = pl.BlockSpec(memory_space=pltpu.VMEM)
     input_grad, res, res2, sums = pl.pallas_call(
         functools.partial(back_kernel, stages),
         grid=(frames + 1 + steps,),
         in_specs=[
             early((HEADS, ROWS, WIN)),
-            whole((kv_rows, 2 * width)),
+            in_hbm,
             early((ROWS, 2 * width)),
             early((ROWS, width)),
             early((ROWS, width)),
             early((ROWS, width)),
-            whole((frames, ROWS, width)),
+            in_hbm,
             pl.BlockSpec((2, ROWS, width), lambda i: (late(i), 0, 0)),
-            whole((1, width)),
-            whole((1, width)),
-            whole((width, 3 * width)),
-            pl.BlockSpec(memory_space=pl.ANY),
+            whole(row.shape),
+            in_hbm,
+            in_hbm,
         ],
         out_specs=[
             pl.BlockSpec((2 * FRAME, width), lambda i: (late(i), 0)),
@@ -833,26 +964,39 @@
             pltpu.VMEM((units2, 16, 128), bf16),
             pltpu.VMEM((ROWS, 2 * width), bf16),
             pltpu.VMEM((ROWS, 2 * width), bf16),
+            pltpu.VMEM((kv_rows, 2 * width), bf16),
+            pltpu.VMEM((frames, ROWS, width), bf16),
+            pltpu.VMEM((width, 3 * width), bf16),
             pltpu.SemaphoreType.DMA((2,)),
-            pltpu.SemaphoreType.DMA,
+            pltpu.SemaphoreType.DMA((5,)),
         ]
         + sum_scratch(stages, first)
         + sum_scratch(stages, second)
         + sum_scratch(stages, units2)
         + rows_scratch(stages),
         compiler_params=params(0),
-    )(prob, kv, ga, gs, qs, li, x_pad, gres, row[:, :width], row[:, width : 2 * width], w_qkv, pack)
+    )(prob, kv, ga, gs, qs, li, x_pad, gres, row, w_qkv, pack)
 
     sizes = [(width,), (width,), (width, 3 * width), (2, width), (width, width), (width,), (width,), (width,),
              (width, hidden), (hidden,), (hidden, width), (width,)]
-    grads = pl.pallas_call(
+    big = [len(z) == 2 and z[0] > 2 for z in sizes]
+    outs = pl.pallas_call(
         unpack_kernel,
-        in_specs=[in_vmem] * 3,
-        out_specs=[in_vmem] * len(sizes),
-        out_shape=[shape(s, f32) for s in sizes],
+        in_specs=[in_hbm, in_hbm, in_vmem, in_vmem],
+        out_specs=[in_hbm] + [in_hbm if far else in_vmem for far in big],
+        out_shape=[shape((count, width), f32)] + [shape(z, f32) for z in sizes],
+        scratch_shapes=[
+            pltpu.VMEM((width, 3 * width), f32),
+            pltpu.VMEM((width, width), f32),
+            pltpu.VMEM((width, hidden), f32),
+            pltpu.VMEM((hidden, width), f32),
+            pltpu.VMEM((units, 16, 128), bf16),
+            pltpu.VMEM((count, width), f32),
+            pltpu.SemaphoreType.DMA((15,)),
+        ],
         compiler_params=params(),
-    )(res, res2, sums)
-    return (block_out, input_grad) + tuple(grads)
+    )(input_grad, res, res2, sums)
+    return (block_out,) + tuple(outs)
 
 
 def solution(mesh):

time: 202 us -> 181 us (0.90)
  local copies, waits for them, and re-layouts: 12.3 us -> 0.66 us
  Pallas kernels: 187 us -> 176 us
    pallas_call x1, Pallas kernels: 91 us -> 79.1 us  [per_device(): pl.pallas_call(forward_kernel, grid=(steps,), in_specs=[pl.BlockSpec(memo...]
    unnamed x10 -> x2, local copies, waits for them, and re-layouts: 10.4 us -> 0.66 us
    pallas_call x1, Pallas kernels: 5.5 us -> 9.57 us  [per_device(): pl.pallas_call(unpack_kernel, in_specs=[in_hbm, in_hbm, in_vmem, in_vmem]...]
    pallas_call x1, Pallas kernels: 90.1 us -> 87.6 us  [per_device(): pl.pallas_call(functools.partial(back_kernel, stages), grid=(frames + 1 +...]
  transfers between devices with their start and end apart: 1 -> 1, of which waited for: 0 -> 1; matrix products, arithmetic and copies ran while one was open for 4% -> 0% of each run, Pallas kernels for 0% -> 0%
where the time goes in v4:
time: 181 us; the launch traced here: 180 us
  Pallas kernels  176 us (97%)
    pallas_call x1, Pallas kernels, per_device(): pl.pallas_call(functools.partial(back_kernel, stages), grid=(frames + 1 +...  87.6 us
    pallas_call x1, Pallas kernels, per_device(): pl.pallas_call(forward_kernel, grid=(steps,), in_specs=[pl.BlockSpec(memo...  79.1 us
    pallas_call x1, Pallas kernels, per_device(): pl.pallas_call(unpack_kernel, in_specs=[in_hbm, in_hbm, in_vmem, in_vmem]...  9.57 us
  transfers between devices with their start and end apart: 1, of which 1 were waited for; matrix products, arithmetic and copies ran while one was open for 0% of the time, Pallas kernels for 0%

profile of v4, /device:TPU:0, one launch (start us, length us, event | category | flops | bytes accessed | tf_op | source)
XLA Modules:
  0.0 180.3 jit_solution(8736105547809890986)
XLA Ops:
  0.6 1.0 slice_select_fusion
  1.7 0.5 collective-permute-start
  2.2 1.0 collective-permute-done.ghost_ref
  3.2 0.0 copy-start
  3.2 0.7 copy-done
  3.9 79.1 %shard_map.254 = (bf16[16,208,384]{2,1,0:T(8,128)(2,1)}, bf16[3760,768]{1,0:T(8,128)(2,1)}, bf16[16,6,208,640]{3,2,1,0:T(8,128)(2,1)}, bf16[3136,384]{1,0:T(8,12...) custom-call(s32[32]{0:T(128)} %clip_ref.1, ...), custom_call_target="tpu_custom_call" | custom-call | tf_op jit(solution)/shard_map/pallas_call | solution.py:851
  83.0 87.6 %shard_map.255 = (f32[3136,384]{1,0:T(8,128)}, bf16[672,16,128]{2,1,0:T(8,128)(2,1)}, bf16[224,16,128]{2,1,0:T(8,128)(2,1)}, f32[16,128]{1,0:T(8,128)}) custom-call(bf16[16,6,208,640]{3,2,1,0:T(8,128)(2,1)} %get-tuple-element.43.prob_ref, bf16[3760,768]{1,0:T(8,128)(2,1)} %get-tuple-element.44.kv_hbm, bf16[16,208,768]{2,1,0:T(8,128)(2,1)} %get-tuple-element.45.ga_ref, ...), custom_call_target="tpu_custom_call" | custom-call | tf_op jit(solution)/shard_map/pallas_call | solution.py:925
  170.5 9.6 %shard_map.256 = (f32[3136,384]{1,0:T(8,128)}, f32[384]{0:T(512)}, f32[384]{0:T(512)}, f32[384,1152]{1,0:T(8,128)}, f32[2,384]{1,0:T(2,128)}, /*index=5*/f32[384...) custom-call(f32[3136,384]{1,0:T(8,128)} %get-tuple-element.53.in_hbm, ...), custom_call_target="tpu_custom_call" | custom-call | tf_op jit(solution)/shard_map/pallas_call | solution.py:983
Async XLA Ops:
  1.7 1.5 collective-permute-start
  3.2 0.7 copy-start

commit v5 on v4

--- a/solution.py
+++ b/solution.py
@@ -235,6 +235,7 @@
     w1_hbm,
     w2_hbm,
     x_hbm,
+    ain_hbm,
     kv_hbm,
     prob_ref,
     out_ref,
@@ -246,6 +247,7 @@
     row_ref,
     pack_ref,
     x_ref,
+    ain_ref,
     kv_ref,
     cot_ref,
     wout_ref,
@@ -273,7 +275,8 @@
     copies = [
         pltpu.make_async_copy(src, dst, sems.at[i])
         for i, (src, dst) in enumerate(
-            ((cot_hbm, cot_ref), (wout_hbm, wout_ref), (w1_hbm, w1_ref), (w2_hbm, w2_ref), (x_ref, x_hbm), (kv_ref, kv_hbm))
+            ((cot_hbm, cot_ref), (wout_hbm, wout_ref), (w1_hbm, w1_ref), (w2_hbm, w2_ref), (x_ref, x_hbm), (kv_ref, kv_hbm),
+             (ain_ref, ain_hbm))
         )
     ]
 
@@ -329,7 +332,9 @@
         def ready(i):
             x = x_ref[4 * i : 4 * i + 4].reshape(4 * ROWS, width).astype(f32)
             n, _ = normed_of(x)
-            return (n * gain1 + shift1).astype(bf16)
+            normed = (n * gain1 + shift1).astype(bf16)
+            ain_ref[4 * i : 4 * i + 4] = normed.reshape(4, ROWS, width)
+            return normed
 
         def project(i, normed):
             qkv = (mm(normed, wqkv_ref[...]) + bias3).astype(bf16)
@@ -539,10 +544,10 @@
     return first, units - first
 
 
-def back_kernel(stages, prob_ref, kv_hbm, ga_ref, gs_ref, qs_ref, li_ref, x_hbm, gres_ref, row_ref,
-                wqkv_hbm, pack_hbm, in_ref, res_ref, res2_ref, rows_ref,
-                acc_ref, d_ref, ds_ref, dq_ref, gw_ref, sq_ref, s384_ref, own_ref, sum_ref, own2_ref, sum2_ref,
-                ghost_ref, got_ref, kv_ref, x_ref, wqkv_ref, ghost_sems, load_sems, *rest):
+def back_kernel(stages, prob_ref, kv_hbm, ga_ref, gs_ref, qs_ref, li_ref, x_hbm, ain_hbm, gres_ref, row_ref,
+                wqkv_hbm, pack_hbm, in_ref, res_hbm, res2_ref, rows_ref,
+                acc_ref, d_ref, ds_ref, dq_ref, sq_ref, s384_ref, own_ref, sum_ref, own2_ref, sum2_ref,
+                ghost_ref, got_ref, kv_ref, x_ref, ain_ref, wqkv_ref, ghost_sems, load_sems, *rest):
     step = pl.program_id(0)
     width = gs_ref.shape[-1]
     frames = x_hbm.shape[0]
@@ -555,14 +560,22 @@
     for stage in stages[1:]:
         devices *= stage[2]
     cut, _ = halves(own_ref.shape[0], devices)
+    tiles = width // 16
+    early_cols = 3 * width // 128 // 2 * 128
+    cut2 = units_for(early_cols // 128 * tiles, devices)
     sums = []
     for n, (own, res) in enumerate(
-        ((own_ref.at[:cut], sum_ref.at[:cut]), (own_ref.at[cut:], sum_ref.at[cut:]), (own2_ref, sum2_ref))
+        (
+            (own_ref.at[:cut], sum_ref.at[:cut]),
+            (own_ref.at[cut:], sum_ref.at[cut:]),
+            (own2_ref.at[:cut2], sum2_ref.at[:cut2]),
+            (own2_ref.at[cut2:], sum2_ref.at[cut2:]),
+        )
     ):
         mine = rest[n * (count + 2) : (n + 1) * (count + 2)]
         sums.append(Sum(stages, own, res, mine[:count], *mine[count:]))
-    one, two, tail = sums
-    extra = rest[3 * (count + 2) :]
+    one, two, three, four = sums
+    extra = rest[4 * (count + 2) :]
     rows = Rows(stages, extra[:count], *extra[count:])
     near = 6 * ROWS
     loads = [
@@ -573,10 +586,12 @@
                 (kv_hbm.at[:near], kv_ref.at[:near]),
                 (kv_hbm.at[near:], kv_ref.at[near:]),
                 (x_hbm, x_ref),
+                (ain_hbm, ain_ref),
                 (wqkv_hbm, wqkv_ref),
             )
         )
     ]
+    keep = pltpu.make_async_copy(sum_ref, res_hbm, load_sems.at[6])
     swap = pltpu.make_async_remote_copy(
         src_ref=ghost_ref,
         dst_ref=got_ref,
@@ -591,13 +606,12 @@
         for load in loads:
             load.start()
         greet(stages)
+        acc_ref[: 2 * ROWS] = jnp.zeros((2 * ROWS, 2 * width), f32)
+        sq_ref[...] = jnp.zeros_like(sq_ref)
+        s384_ref[...] = jnp.zeros_like(s384_ref)
         loads[0].wait()
         one.send(0)
         two.send(0)
-        acc_ref[...] = jnp.zeros_like(acc_ref)
-        gw_ref[...] = jnp.zeros_like(gw_ref)
-        sq_ref[...] = jnp.zeros_like(sq_ref)
-        s384_ref[...] = jnp.zeros_like(s384_ref)
         loads[1].wait()
 
     @pl.when(step == 1)
@@ -610,22 +624,20 @@
             for act, i in todo:
                 act(i)
 
+    def scatter(total):
+        return [t for i in range(1, last) for t in ((total.take, i), (total.send, i + 1))]
+
+    def gather(total):
+        return [t for i in range(last, 1, -1) for t in ((total.settle, i), (total.spread, i - 1))]
+
+    norm_step = frames + 1
     at(1, (one.take, 0), (two.take, 0), (one.send, 1))
-    if count == 3:
-        at(5, (one.take, 1), (one.send, 2), (two.send, 1))
-        at(8, (one.take, 2), (one.spread, 2))
-        at(9, (two.take, 1), (two.send, 2))
-        at(11, (one.settle, 2), (one.spread, 1))
-        at(13, (two.take, 2), (two.spread, 2))
-        at(frames, (one.settle, 1), (two.settle, 2), (one.spread, 0), (two.spread, 1))
-    else:
-        at(5, *[t for i in range(1, last) for t in ((one.take, i), (one.send, i + 1))], (two.send, 1))
-        at(8, (one.take, last), (one.spread, last))
-        at(9, *[t for i in range(1, last) for t in ((two.take, i), (two.send, i + 1))])
-        at(11, *[t for i in range(last, 1, -1) for t in ((one.settle, i), (one.spread, i - 1))])
-        at(13, (two.take, last), (two.spread, last))
-        at(frames, (one.settle, 1), *[t for i in range(last, 1, -1) for t in ((two.settle, i), (two.spread, i - 1))],
-           (one.spread, 0))
+    at(5, *scatter(one), (two.send, 1))
+    at(8, (one.take, last), (one.spread, last))
+    at(9, *scatter(two))
+    at(11, *gather(one))
+    at(12, (two.take, last), (two.spread, last))
+    at(15, *gather(two), (one.settle, 1), (one.spread, 0))
 
     low = lax.broadcasted_iota(jnp.int32, (ROWS, 128), 1) < 64
     wide_low = lax.broadcasted_iota(jnp.int32, (WIN, 128), 1) < 64
@@ -636,6 +648,8 @@
     @pl.when(step < frames)
     def _():
         window = pl.ds(pl.multiple_of(step * ROWS, 16), WIN)
+        seen = pl.ds(pl.multiple_of(step * ROWS, 16), 2 * ROWS)
+        fresh = pl.ds(pl.multiple_of((step + 2) * ROWS, 16), ROWS)
 
         def differ(h):
             at = width + h // 2 * 128
@@ -660,8 +674,10 @@
                 even, odd = held.pop(h - 1), held.pop(h)
                 dq = jnp.where(low, even[0], odd[0]) * (li_ref[0, :, cols] * inv_scale)
                 dq_ref[pl.ds(pl.multiple_of(step * ROWS, 16), ROWS), cols] = dq.astype(bf16)
-                acc_ref[window, cols] += jnp.concatenate([even[1], odd[1]], axis=0).T
-                acc_ref[window, vcols] += jnp.concatenate([even[2], odd[2]], axis=0).T
+                for i, into in ((1, cols), (2, vcols)):
+                    grad = jnp.concatenate([even[i], odd[i]], axis=0).T
+                    acc_ref[seen, into] += grad[: 2 * ROWS]
+                    acc_ref[fresh, into] = grad[2 * ROWS : 3 * ROWS]
 
         differ(0)
         for h in range(HEADS + 1):
@@ -677,45 +693,66 @@
         ghost_ref[:, :width] = (acc_ref[ghost_rows, :width] * inv_scale).astype(bf16)
         ghost_ref[:, width:] = acc_ref[ghost_rows, width:].astype(bf16)
         swap.start()
-
-    block = 2 * ROWS
-
-    def block_of(i):
-        x = x_ref[pl.ds(2 * i, 2)].reshape(block, width).astype(f32)
-        n, inverse = normed_of(x)
-        dq = dq_ref[pl.ds(pl.multiple_of(i * block, 16), block), :]
-        here = pl.ds(pl.multiple_of(ROWS + i * block, 16), block)
-        dk = (acc_ref[here, :width] * inv_scale).astype(bf16)
-        dv = acc_ref[here, width:].astype(bf16)
-        return n, inverse, jnp.concatenate([dq, dk, dv], axis=1)
+        for load in loads[3:]:
+            load.wait()
+
+    def grads_of(start, size, lo, hi):
+        here = pl.ds(pl.multiple_of(start, 16), size)
+        below = pl.ds(pl.multiple_of(start + ROWS, 16), size)
+        parts = []
+        if lo < width:
+            parts.append(dq_ref[here, lo : min(hi, width)])
+        if lo < 2 * width and hi > width:
+            parts.append((acc_ref[below, max(lo - width, 0) : min(hi, 2 * width) - width] * inv_scale).astype(bf16))
+        if hi > 2 * width:
+            parts.append(acc_ref[below, max(lo, 2 * width) - width : hi - width].astype(bf16))
+        return jnp.concatenate(parts, axis=1)
 
     @pl.when(step == frames)
     def _():
-        loads[3].wait()
-        loads[4].wait()
         swap.wait()
         got = got_ref[...].astype(f32)
         acc_ref[edge_rows, :width] += got[:, :width] * (1.0 / inv_scale)
         acc_ref[edge_rows, width:] += got[:, width:]
 
-        def weights(i, carry):
-            n, _, grads = block_of(i)
-            attn_in = (n * row_ref[:, :width] + row_ref[:, width : 2 * width]).astype(bf16)
-            gw_ref[...] += mm_tn(attn_in, grads)
-            sq_ref[...] += fold8(grads.astype(f32))
-            return carry
-
-        lax.fori_loop(0, frames // 2, weights, 0)
-        end = pack_matrix(own2_ref, 0, gw_ref[...])
-        own2_ref[end:] = jnp.zeros((own2_ref.shape[0] - end, 16, 128), bf16)
-        tail.send(0)
-
-    at(frames + 3, (tail.take, 0), (tail.send, 1))
+        def weights(lo, hi):
+            total = 0.0
+            for i in range(frames // 4):
+                grads = grads_of(4 * i * ROWS, 4 * ROWS, lo, hi)
+                total = total + mm_tn(ain_ref[4 * i : 4 * i + 4].reshape(4 * ROWS, width), grads)
+                sq_ref[:, lo:hi] += fold8(grads.astype(f32))
+            return total
+
+        def pad(end, stop):
+            if end < stop:
+                own2_ref[end:stop] = jnp.zeros((stop - end, 16, 128), bf16)
+
+        pad(pack_matrix(own2_ref, 0, weights(0, early_cols)), cut2)
+        three.send(0)
+        late = weights(early_cols, 3 * width)
+        three.take(0)
+        three.send(1)
+        pad(pack_matrix(own2_ref, cut2, late), own2_ref.shape[0])
+        four.send(0)
+
+    at(norm_step + 1, (four.take, 0), (four.send, 1))
+    at(norm_step + 3, (one.settle, 0), (two.settle, 1), (two.spread, 0))
+    at(norm_step + 4, (three.take, 1), (three.send, 2))
+
+    @pl.when(step == norm_step + 5)
+    def _():
+        two.settle(0)
+        keep.start()
+
+    at(norm_step + 7, (four.take, 1), (four.send, 2))
 
     @pl.when(step > frames)
     def _():
-        n, inverse, grads = block_of(step - frames - 1)
-        up = mm_nt(grads, wqkv_ref[...])
+        i = step - norm_step
+        block = 2 * ROWS
+        x = x_ref[pl.ds(2 * i, 2)].reshape(block, width).astype(f32)
+        n, inverse = normed_of(x)
+        up = mm_nt(grads_of(i * block, block, 0, 3 * width), wqkv_ref[...])
         gres = gres_ref[...].reshape(block, width)
         narrow_into(in_ref, 0, gres + norm_back(up, n, inverse, row_ref[:, :width]))
         s384_ref[0] += fold8(up * n)
@@ -727,28 +764,28 @@
         parts = [colsum(s384_ref[0]), colsum(s384_ref[1]), sq[:, :width], sq[:, 2 * width :]]
         lines = [v[:, c : c + 128] for v in parts for c in range(0, width, 128)]
         lines += [jnp.zeros((1, 128), f32)] * (16 - len(lines))
-        tile = jnp.concatenate(lines, axis=0)
-        for i in range(1, count):
-            tail.take(i)
-            if i < last:
-                tail.send(i + 1)
-        for i in range(last, -1, -1):
-            tail.spread(i)
-            rows.spread(i, tile)
-            if i == 1:
-                two.settle(1)
-                two.spread(0)
-            if i == 0:
-                one.settle(0)
-                two.settle(0)
-            tail.settle(i)
+        rows.spread(last, jnp.concatenate(lines, axis=0))
+        for i in range(2, count):
+            for total in (three, four):
+                total.take(i)
+                if i < last:
+                    total.send(i + 1)
+                else:
+                    total.spread(last)
+        for i in range(last, 0, -1):
             tile = rows.settle(i)
-        res_ref[...] = sum_ref[...]
+            rows.spread(i - 1, tile)
+            for total in (three, four):
+                total.settle(i)
+                total.spread(i - 1)
+        rows_ref[...] = rows.settle(0)
+        three.settle(0)
+        four.settle(0)
         res2_ref[...] = sum2_ref[...]
-        rows_ref[...] = tile
-
-
-def unpack_kernel(in_hbm, res_hbm, res2_ref, rows_ref, out_hbm, gg1, gb1, gqkv_hbm, gqv, gwo_hbm, gbo, gg2, gb2, gw1_hbm,
+        keep.wait()
+
+
+def unpack_kernel(cut2, in_hbm, res_hbm, res2_ref, rows_ref, out_hbm, gg1, gb1, gqkv_hbm, gqv, gwo_hbm, gbo, gg2, gb2, gw1_hbm,
                   gbf1, gw2_hbm, gbf2, gqkv, gwo, gw1, gw2, res_ref, mid_ref, sems):
     width, hidden = gw1.shape
     tiles = width // 16
@@ -771,10 +808,10 @@
     ]
     for copy in loads + come:
         copy.start()
-    at = 0
+    early = 3 * width // 128 // 2
     for c in range(3 * width // 128):
+        at = c * tiles if c < early else cut2 + (c - early) * tiles
         gqkv[:, 128 * c : 128 * c + 128] = res2_ref[at : at + tiles].reshape(width, 128).astype(f32)
-        at += tiles
     stores[0].start()
     loads[0].wait()
     at = 0
@@ -847,8 +884,11 @@
     devices = 2 * lax.axis_size("clips")
     tiles = width // 16
     units = units_for((2 * hidden + width) // 128 * tiles + 2, devices)
-    units2 = units_for(3 * width // 128 * tiles + 1, devices)
-    x_pad, kv, prob, block_out, qs, ga, gs, gres, li, row, pack = pl.pallas_call(
+    across2 = 3 * width // 128
+    first2 = units_for(across2 // 2 * tiles, devices)
+    second2 = units_for((across2 - across2 // 2) * tiles, devices)
+    units2 = first2 + second2
+    x_pad, ain, kv, prob, block_out, qs, ga, gs, gres, li, row, pack = pl.pallas_call(
         forward_kernel,
         grid=(steps,),
         in_specs=[
@@ -872,6 +912,7 @@
         out_specs=[
             in_hbm,
             in_hbm,
+            in_hbm,
             pairs((HEADS, ROWS, WIN)),
             pl.BlockSpec((4 * FRAME, width), lambda i: (i // 2, 0)),
             pairs((ROWS, width)),
@@ -883,6 +924,7 @@
             whole((units, 16, 128)),
         ],
         out_shape=[
+            shape((frames, ROWS, width), bf16),
             shape((frames, ROWS, width), bf16),
             shape((kv_rows, 2 * width), bf16),
             shape((frames, HEADS, ROWS, WIN), bf16),
@@ -896,6 +938,7 @@
             shape((units, 16, 128), bf16),
         ],
         scratch_shapes=[
+            pltpu.VMEM((frames, ROWS, width), bf16),
             pltpu.VMEM((frames, ROWS, width), bf16),
             pltpu.VMEM((kv_rows, 2 * width), bf16),
             pltpu.VMEM((count, width), bf16),
@@ -913,7 +956,7 @@
             pltpu.VMEM((width, width), f32),
             pltpu.VMEM((8, hidden), f32),
             pltpu.VMEM((4, 8, width), f32),
-            pltpu.SemaphoreType.DMA((6,)),
+            pltpu.SemaphoreType.DMA((7,)),
         ],
         compiler_params=params(),
     )(frame_clip, tokens, ghost, ln1_gain, ln1_bias, qv_bias, b_out, ln2_gain, ln2_bias, b_fc1, b_fc2, w_qkv, cotangent,
@@ -933,6 +976,7 @@
             early((ROWS, width)),
             early((ROWS, width)),
             in_hbm,
+            in_hbm,
             pl.BlockSpec((2, ROWS, width), lambda i: (late(i), 0, 0)),
             whole(row.shape),
             in_hbm,
@@ -940,7 +984,7 @@
         ],
         out_specs=[
             pl.BlockSpec((2 * FRAME, width), lambda i: (late(i), 0)),
-            whole((units, 16, 128)),
+            in_hbm,
             whole((units2, 16, 128)),
             whole((16, 128)),
         ],
@@ -955,7 +999,6 @@
             pltpu.VMEM((3, ROWS, WIN), f32),
             pltpu.VMEM((3, ROWS, WIN), bf16),
             pltpu.VMEM((frames * ROWS, width), bf16),
-            pltpu.VMEM((width, 3 * width), f32),
             pltpu.VMEM((8, 3 * width), f32),
             pltpu.VMEM((2, 8, width), f32),
             pltpu.VMEM((units, 16, 128), bf16),
@@ -966,22 +1009,24 @@
             pltpu.VMEM((ROWS, 2 * width), bf16),
             pltpu.VMEM((kv_rows, 2 * width), bf16),
             pltpu.VMEM((frames, ROWS, width), bf16),
+            pltpu.VMEM((frames, ROWS, width), bf16),
             pltpu.VMEM((width, 3 * width), bf16),
             pltpu.SemaphoreType.DMA((2,)),
-            pltpu.SemaphoreType.DMA((5,)),
+            pltpu.SemaphoreType.DMA((7,)),
         ]
         + sum_scratch(stages, first)
         + sum_scratch(stages, second)
-        + sum_scratch(stages, units2)
+        + sum_scratch(stages, first2)
+        + sum_scratch(stages, second2)
         + rows_scratch(stages),
         compiler_params=params(0),
-    )(prob, kv, ga, gs, qs, li, x_pad, gres, row, w_qkv, pack)
+    )(prob, kv, ga, gs, qs, li, x_pad, ain, gres, row, w_qkv, pack)
 
     sizes = [(width,), (width,), (width, 3 * width), (2, width), (width, width), (width,), (width,), (width,),
              (width, hidden), (hidden,), (hidden, width), (width,)]
     big = [len(z) == 2 and z[0] > 2 for z in sizes]
     outs = pl.pallas_call(
-        unpack_kernel,
+        functools.partial(unpack_kernel, first2),
         in_specs=[in_hbm, in_hbm, in_vmem, in_vmem],
         out_specs=[in_hbm] + [in_hbm if far else in_vmem for far in big],
         out_shape=[shape((count, width), f32)] + [shape(z, f32) for z in sizes],

time: 181 us -> 171 us (0.945)
  Pallas kernels: 176 us -> 167 us
    pallas_call x1, Pallas kernels: 87.6 us -> 78 us  [per_device(): pl.pallas_call(functools.partial(back_kernel, stages), grid=(frames + 1 +...]
where the time goes in v5:
time: 171 us
  Pallas kernels  167 us (98%)
    pallas_call x1, Pallas kernels, per_device(): pl.pallas_call(forward_kernel, grid=(steps,), in_specs=[pl.BlockSpec(memo...  79.2 us
    pallas_call x1, Pallas kernels, per_device(): pl.pallas_call(functools.partial(back_kernel, stages), grid=(frames + 1 +...  78 us
    pallas_call x1, Pallas kernels, per_device(): pl.pallas_call(functools.partial(unpack_kernel, first2), in_specs=[in_hbm...  9.57 us
  transfers between devices with their start and end apart: 1, of which 1 were waited for; matrix products, arithmetic and copies ran while one was open for 0% of the time, Pallas kernels for 0%

profile of v5, /device:TPU:0, one launch (start us, length us, event | category | flops | bytes accessed | tf_op | source)
XLA Modules:
  0.0 170.9 jit_solution(3518564189932377155)
XLA Ops:
  0.6 1.0 slice_select_fusion
  1.7 0.5 collective-permute-start
  2.2 1.0 collective-permute-done.ghost_ref
  3.2 0.0 copy-start
  3.2 0.7 copy-done
  3.9 79.2 %shard_map.254 = (bf16[16,208,384]{2,1,0:T(8,128)(2,1)}, bf16[16,208,384]{2,1,0:T(8,128)(2,1)}, bf16[3760,768]{1,0:T(8,128)(2,1)}, bf16[16,6,208,640]{3,2,1,0:T(...) custom-call(s32[32]{0:T(128)} %clip_ref.1, ...), custom_call_target="tpu_custom_call" | custom-call | tf_op jit(solution)/shard_map/pallas_call | solution.py:891
  83.1 78.0 %shard_map.255 = (f32[3136,384]{1,0:T(8,128)}, bf16[672,16,128]{2,1,0:T(8,128)(2,1)}, bf16[224,16,128]{2,1,0:T(8,128)(2,1)}, f32[16,128]{1,0:T(8,128)}) custom-call(bf16[16,6,208,640]{3,2,1,0:T(8,128)(2,1)} %get-tuple-element.44.prob_ref, bf16[3760,768]{1,0:T(8,128)(2,1)} %get-tuple-element.45.kv_hbm, bf16[16,208,768]{2,1,0:T(8,128)(2,1)} %get-tuple-element.46.ga_ref, ...), custom_call_target="tpu_custom_call" | custom-call | tf_op jit(solution)/shard_map/pallas_call | solution.py:968
  161.1 9.6 %shard_map.256 = (f32[3136,384]{1,0:T(8,128)}, f32[384]{0:T(512)}, f32[384]{0:T(512)}, f32[384,1152]{1,0:T(8,128)}, f32[2,384]{1,0:T(2,128)}, /*index=5*/f32[384...) custom-call(f32[3136,384]{1,0:T(8,128)} %get-tuple-element.55.in_hbm, ...), custom_call_target="tpu_custom_call" | custom-call | tf_op jit(solution)/shard_map/pallas_call | solution.py:1028
Async XLA Ops:
  1.7 1.5 collective-permute-start
  3.2 0.7 copy-start

commit v6 on v5

--- a/solution.py
+++ b/solution.py
@@ -12,6 +12,7 @@
 FRAME = 196
 ROWS = 208
 WIN = 640
+EXTRA = 16
 EPS = 1e-6
 LOG2E = math.log2(math.e)
 
@@ -219,7 +220,7 @@
 
 def forward_kernel(
     clip_ref,
-    tok_ref,
+    tok_hbm,
     ghost_ref,
     g1_ref,
     s1_ref,
@@ -249,7 +250,7 @@
     x_ref,
     ain_ref,
     kv_ref,
-    cot_ref,
+    raw_ref,
     wout_ref,
     w1_ref,
     w2_ref,
@@ -275,14 +276,15 @@
     copies = [
         pltpu.make_async_copy(src, dst, sems.at[i])
         for i, (src, dst) in enumerate(
-            ((cot_hbm, cot_ref), (wout_hbm, wout_ref), (w1_hbm, w1_ref), (w2_hbm, w2_ref), (x_ref, x_hbm), (kv_ref, kv_hbm),
-             (ain_ref, ain_hbm))
+            ((cot_hbm, raw_ref), (wout_hbm, wout_ref), (w1_hbm, w1_ref), (w2_hbm, w2_ref), (x_ref, x_hbm), (kv_ref, kv_hbm),
+             (ain_ref, ain_hbm), (tok_hbm, raw_ref))
         )
     ]
 
     @pl.when(step == 0)
     def _():
-        for copy in copies[:4]:
+        copies[7].start()
+        for copy in copies[1:4]:
             copy.start()
         vectors = [g1_ref[...], s1_ref[...], None, None, None, bo_ref[...], g2_ref[...], s2_ref[...], bf2_ref[...]]
         for i, v in enumerate(vectors):
@@ -305,7 +307,7 @@
         sb1_ref[...] = jnp.zeros_like(sb1_ref)
         s384_ref[...] = jnp.zeros_like(s384_ref)
         at = lax.broadcasted_iota(jnp.int32, flag_ref.shape, 0)
-        lane = lax.broadcasted_iota(jnp.int32, flag_ref.shape, 1) % 64
+        lane = lax.broadcasted_iota(jnp.int32, flag_ref.shape, 1)
         slot = at // ROWS
         flag_ref[...] = jnp.where(
             lane == 0,
@@ -341,25 +343,26 @@
             q_ref[4 * i : 4 * i + 4] = qkv[:, :width].reshape(4, ROWS, width)
             kv_ref[(4 * i + 1) * ROWS : (4 * i + 5) * ROWS, :] = qkv[:, width:]
 
+        copies[7].wait()
         for i in range(frames // 4):
-            pad(i, tok_ref, x_ref)
+            pad(i, raw_ref, x_ref)
+        copies[0].start()
         normed = ready(0)
         for i in range(frames // 4):
             following = ready(i + 1) if i + 1 < frames // 4 else None
             project(i, normed)
             normed = following
-        for copy in copies[4:]:
+        for copy in copies[4:7]:
             copy.start()
         for copy in copies[:4]:
             copy.wait()
         for i in range(frames // 4):
-            pad(i, cot_ref, cp_ref)
+            pad(i, raw_ref, cp_ref)
 
     low = lax.broadcasted_iota(jnp.int32, (ROWS, 128), 1) < 64
-    wide_low = lax.broadcasted_iota(jnp.int32, (WIN, 128), 1) < 64
-    lane = lax.broadcasted_iota(jnp.int32, (1, 128), 1) % 64
-    ones = jnp.ones((WIN, 128), bf16)
+    lane = lax.broadcasted_iota(jnp.int32, (1, 128), 1)
     scale = LOG2E / math.sqrt(width // HEADS)
+    twins = HEADS // 2
     flags, windows = [], []
     for sub in range(2):
         frame = 2 * step + sub
@@ -372,46 +375,44 @@
         row = jnp.where(lane == 1 + frame % 4, jnp.where(before == own, 0.0, none), row)
         row = jnp.where(lane == 1 + (frame + 2) % 4, jnp.where(after == own, 0.0, none), row)
         row = jnp.where(lane == 1 + (frame + 3) % 4, none, row)
-        flags.append(jnp.broadcast_to(row.astype(bf16), (ROWS, 128)))
+        flags.append(jnp.broadcast_to(row.astype(bf16), (2 * ROWS, 128))[:, :EXTRA])
         windows.append(pl.ds(pl.multiple_of(frame * ROWS, 16), WIN))
 
     def score(t):
-        sub, h = divmod(t, HEADS)
-        cols = slice(h // 2 * 128, h // 2 * 128 + 128)
-        mine, wide = (low, wide_low) if h % 2 == 0 else (~low, ~wide_low)
-        q = jnp.where(mine, q_ref[2 * step + sub, :, cols], flags[sub])
-        k = jnp.where(wide, kv_ref[windows[sub], cols], flag_ref[windows[sub], :])
-        s_ref[t % 3] = mm_nt(q, k)
+        sub, pair = divmod(t, twins)
+        cols = slice(pair * 128, pair * 128 + 128)
+        q = q_ref[2 * step + sub, :, cols]
+        zero = jnp.zeros_like(q)
+        both = jnp.concatenate([jnp.where(low, q, zero), jnp.where(low, zero, q)], axis=0)
+        k = jnp.concatenate([kv_ref[windows[sub], cols], flag_ref[windows[sub], :EXTRA]], axis=1)
+        s_ref[t % 3] = mm_nt(jnp.concatenate([both, flags[sub]], axis=1), k)
+
+    inverses = {}
 
     def soften(t):
-        sub, h = divmod(t, HEADS)
+        sub, pair = divmod(t, twins)
         s = s_ref[t % 3]
         top = jnp.max(s, axis=-1, keepdims=True)
-        prob_ref[sub, h] = jnp.exp2((s - top) * scale).astype(bf16)
-
-    parts = {}
+        e = jnp.exp2((s - top) * scale)
+        inverses[t] = 1.0 / jnp.sum(e, axis=-1, keepdims=True)
+        prob_ref[sub, pair] = e.astype(bf16)
 
     def attend(t):
-        sub, h = divmod(t, HEADS)
-        at = h // 2 * 128
-        wide = wide_low if h % 2 == 0 else ~wide_low
-        v = jnp.where(wide, kv_ref[windows[sub], width + at : width + at + 128], ones)
-        parts[t] = mm(prob_ref[sub, h], v)
-        if h % 2:
-            even, odd = parts.pop(t - 1), parts.pop(t)
-            total = pltpu.roll(jnp.where(low, odd, even), 64, 1)
-            inverse = 1.0 / total
-            rows = slice(sub * ROWS, (sub + 1) * ROWS)
-            o_ref[rows, at : at + 128] = jnp.where(low, even, odd) * inverse
-            li_ref[sub, :, at : at + 128] = inverse
+        sub, pair = divmod(t, twins)
+        at = pair * 128
+        o = mm(prob_ref[sub, pair], kv_ref[windows[sub], width + at : width + at + 128])
+        inverse = jnp.where(low, inverses[t][:ROWS], inverses[t][ROWS:])
+        rows = slice(sub * ROWS, (sub + 1) * ROWS)
+        o_ref[rows, at : at + 128] = jnp.where(low, o[:ROWS], o[ROWS:]) * inverse
+        li_ref[sub, :, at : at + 128] = inverse
 
     score(0)
-    for t in range(2 * HEADS + 1):
-        if t + 1 < 2 * HEADS:
+    for t in range(2 * twins + 1):
+        if t + 1 < 2 * twins:
             score(t + 1)
         if t >= 1:
             attend(t - 1)
-        if t < 2 * HEADS:
+        if t < 2 * twins:
             soften(t)
 
     att = o_ref[...].astype(bf16)
@@ -462,22 +463,24 @@
     gs_ref[...] = (g32 * inverse).astype(bf16).reshape(2, ROWS, width)
     qs_ref[...] = (q_ref[both].reshape(2 * ROWS, width).astype(f32) * inverse).astype(bf16).reshape(2, ROWS, width)
     dots = g32 * o_ref[...]
-    low2 = lax.broadcasted_iota(jnp.int32, (2 * ROWS, 128), 1) < 64
-    for pair in range(HEADS // 2):
-        cols = slice(128 * pair, 128 * pair + 128)
-        d = dots[:, cols]
-        even = jnp.sum(jnp.where(low2, d, 0.0), axis=-1, keepdims=True)
-        odd = jnp.sum(jnp.where(low2, 0.0, d), axis=-1, keepdims=True)
-        less = -jnp.where(low2, odd, even)
-        one = less.astype(bf16)
-        two = (less - one.astype(f32)).astype(bf16)
-        three = (less - one.astype(f32) - two.astype(f32)).astype(bf16)
-        zero = jnp.zeros_like(one)
-        lanes = jnp.broadcast_to(lane, (2 * ROWS, 128))
-        tail = jnp.where(lanes == 0, one, jnp.where(lanes == 1, two, jnp.where(lanes == 2, three, zero)))
-        gp = g[:, cols]
-        ga_ref[:, :, 256 * pair : 256 * pair + 128] = jnp.where(low2, gp, tail).reshape(2, ROWS, 128)
-        ga_ref[:, :, 256 * pair + 128 : 256 * pair + 256] = jnp.where(low2, tail, gp).reshape(2, ROWS, 128)
+    some = lax.broadcasted_iota(jnp.int32, (2 * ROWS, EXTRA), 1)
+    for sub in range(2):
+        for pair in range(twins):
+            rows, cols = slice(sub * ROWS, (sub + 1) * ROWS), slice(128 * pair, 128 * pair + 128)
+            d = dots[rows, cols]
+            even = jnp.sum(jnp.where(low, d, 0.0), axis=-1, keepdims=True)
+            odd = jnp.sum(jnp.where(low, 0.0, d), axis=-1, keepdims=True)
+            less = jnp.broadcast_to(-jnp.concatenate([even, odd], axis=0), (2 * ROWS, EXTRA))
+            one = less.astype(bf16).astype(f32)
+            two = (less - one).astype(bf16).astype(f32)
+            three = less - one - two
+            ga_ref[sub, pair, :, 128 : 128 + EXTRA] = jnp.where(
+                some == 0, one, jnp.where(some == 1, two, jnp.where(some == 2, three, 0.0))
+            ).astype(bf16)
+            gp = g[rows, cols]
+            zero = jnp.zeros_like(gp)
+            ga_ref[sub, pair, :ROWS, :128] = jnp.where(low, gp, zero)
+            ga_ref[sub, pair, ROWS:, :128] = jnp.where(low, zero, gp)
     s384_ref[0] += fold8(up * n2)
     s384_ref[1] += fold8(up)
     s384_ref[2] += fold8(branch.astype(f32))
@@ -497,7 +500,7 @@
         at = pack_matrix(pack_ref, at, gw2_ref[...])
         at = pack_matrix(pack_ref, at, gwo_ref[...])
         pack_rows(pack_ref, at, [colsum(s384_ref[i]) for i in range(4)] + [colsum(sb1_ref[...])])
-        for copy in copies[4:]:
+        for copy in copies[4:7]:
             copy.wait()
 
 
@@ -539,9 +542,15 @@
     return [pltpu.VMEM((s[2], 16, 128), f32) for s in stages] + [pltpu.SemaphoreType.DMA((copies,))] * 2
 
 
-def halves(units, devices):
-    first = -(-units // (2 * devices)) * devices
-    return first, units - first
+def shares(units, devices):
+    blocks = units // devices
+    side = max(1, round(blocks / 7))
+    first = -(-(blocks - side) // 2)
+    return first * devices, (blocks - side - first) * devices, side * devices
+
+
+def turned(stages):
+    return stages[:1] + stages[:0:-1]
 
 
 def back_kernel(stages, prob_ref, kv_hbm, ga_ref, gs_ref, qs_ref, li_ref, x_hbm, ain_hbm, gres_ref, row_ref,
@@ -559,23 +568,25 @@
     devices = 2
     for stage in stages[1:]:
         devices *= stage[2]
-    cut, _ = halves(own_ref.shape[0], devices)
+    first, second, _ = shares(own_ref.shape[0], devices)
+    both = first + second
     tiles = width // 16
     early_cols = 3 * width // 128 // 2 * 128
     cut2 = units_for(early_cols // 128 * tiles, devices)
     sums = []
-    for n, (own, res) in enumerate(
+    for n, (route, own, res) in enumerate(
         (
-            (own_ref.at[:cut], sum_ref.at[:cut]),
-            (own_ref.at[cut:], sum_ref.at[cut:]),
-            (own2_ref.at[:cut2], sum2_ref.at[:cut2]),
-            (own2_ref.at[cut2:], sum2_ref.at[cut2:]),
+            (stages, own_ref.at[:first], sum_ref.at[:first]),
+            (stages, own_ref.at[first:both], sum_ref.at[first:both]),
+            (turned(stages), own_ref.at[both:], sum_ref.at[both:]),
+            (stages, own2_ref.at[:cut2], sum2_ref.at[:cut2]),
+            (stages, own2_ref.at[cut2:], sum2_ref.at[cut2:]),
         )
     ):
         mine = rest[n * (count + 2) : (n + 1) * (count + 2)]
-        sums.append(Sum(stages, own, res, mine[:count], *mine[count:]))
-    one, two, three, four = sums
-    extra = rest[4 * (count + 2) :]
+        sums.append(Sum(route, own, res, mine[:count], *mine[count:]))
+    one, two, side, three, four = sums
+    extra = rest[5 * (count + 2) :]
     rows = Rows(stages, extra[:count], *extra[count:])
     near = 6 * ROWS
     loads = [
@@ -611,6 +622,7 @@
         s384_ref[...] = jnp.zeros_like(s384_ref)
         loads[0].wait()
         one.send(0)
+        side.send(0)
         two.send(0)
         loads[1].wait()
 
@@ -631,17 +643,18 @@
         return [t for i in range(last, 1, -1) for t in ((total.settle, i), (total.spread, i - 1))]
 
     norm_step = frames + 1
-    at(1, (one.take, 0), (two.take, 0), (one.send, 1))
-    at(5, *scatter(one), (two.send, 1))
-    at(8, (one.take, last), (one.spread, last))
-    at(9, *scatter(two))
-    at(11, *gather(one))
-    at(12, (two.take, last), (two.spread, last))
-    at(15, *gather(two), (one.settle, 1), (one.spread, 0))
+    at(1, (one.take, 0), (one.send, 1), (side.take, 0), (side.send, 1), (two.take, 0))
+    at(4, (two.send, 1), *scatter(side))
+    at(6, *scatter(one))
+    at(8, *scatter(two), (side.take, last), (side.spread, last))
+    at(9, (one.take, last), (one.spread, last))
+    at(10, *gather(side))
+    at(11, (two.take, last), (two.spread, last))
+    at(13, *gather(one))
+    at(15, *gather(two), (side.settle, 1), (side.spread, 0))
 
     low = lax.broadcasted_iota(jnp.int32, (ROWS, 128), 1) < 64
-    wide_low = lax.broadcasted_iota(jnp.int32, (WIN, 128), 1) < 64
-    ones = jnp.ones((WIN, 128), bf16)
+    ones = jnp.ones((WIN, EXTRA), bf16)
     edge_rows = pl.ds(pl.multiple_of(jnp.where(tm == 0, frames, 1) * ROWS, 16), ROWS)
     ghost_rows = pl.ds(pl.multiple_of(jnp.where(tm == 0, frames + 1, 0) * ROWS, 16), ROWS)
 
@@ -651,42 +664,37 @@
         seen = pl.ds(pl.multiple_of(step * ROWS, 16), 2 * ROWS)
         fresh = pl.ds(pl.multiple_of((step + 2) * ROWS, 16), ROWS)
 
-        def differ(h):
-            at = width + h // 2 * 128
-            wide = wide_low if h % 2 == 0 else ~wide_low
-            v = jnp.where(wide, kv_ref[window, at : at + 128], ones)
-            d_ref[h % 3] = mm_nt(ga_ref[0, :, 128 * h : 128 * h + 128], v)
-
-        def weigh(h):
-            ds_ref[h % 3] = (prob_ref[0, h].astype(f32) * d_ref[h % 3]).astype(bf16)
-
-        held = {}
-
-        def spend(h):
-            cols = slice(h // 2 * 128, h // 2 * 128 + 128)
-            vcols = slice(width + h // 2 * 128, width + h // 2 * 128 + 128)
-            mine = slice(h % 2 * 64, h % 2 * 64 + 64)
-            ds = ds_ref[h % 3]
-            if h % 2 == 0:
-                held["qt"], held["gt"] = qs_ref[0, :, cols].T, gs_ref[0, :, cols].T
-            held[h] = mm(ds, kv_ref[window, cols]), mm(held["qt"][mine], ds), mm(held["gt"][mine], prob_ref[0, h])
-            if h % 2:
-                even, odd = held.pop(h - 1), held.pop(h)
-                dq = jnp.where(low, even[0], odd[0]) * (li_ref[0, :, cols] * inv_scale)
-                dq_ref[pl.ds(pl.multiple_of(step * ROWS, 16), ROWS), cols] = dq.astype(bf16)
-                for i, into in ((1, cols), (2, vcols)):
-                    grad = jnp.concatenate([even[i], odd[i]], axis=0).T
-                    acc_ref[seen, into] += grad[: 2 * ROWS]
-                    acc_ref[fresh, into] = grad[2 * ROWS : 3 * ROWS]
-
+        def differ(t):
+            at = width + t * 128
+            v = jnp.concatenate([kv_ref[window, at : at + 128], ones], axis=1)
+            d_ref[t % 3] = mm_nt(ga_ref[0, t], v)
+
+        def weigh(t):
+            ds_ref[t % 3] = (prob_ref[0, t].astype(f32) * d_ref[t % 3]).astype(bf16)
+
+        def spend(t):
+            cols = slice(t * 128, t * 128 + 128)
+            vcols = slice(width + t * 128, width + t * 128 + 128)
+            ds = ds_ref[t % 3]
+            dq = mm(ds, kv_ref[window, cols])
+            dq = jnp.where(low, dq[:ROWS], dq[ROWS:]) * (li_ref[0, :, cols] * inv_scale)
+            dq_ref[pl.ds(pl.multiple_of(step * ROWS, 16), ROWS), cols] = dq.astype(bf16)
+            prob = prob_ref[0, t]
+            for left, right, into in ((qs_ref, ds, cols), (gs_ref, prob, vcols)):
+                turned = left[0, :, cols].T
+                grad = jnp.concatenate([mm(turned[:64], right[:ROWS]), mm(turned[64:], right[ROWS:])], axis=0).T
+                acc_ref[seen, into] += grad[: 2 * ROWS]
+                acc_ref[fresh, into] = grad[2 * ROWS : 3 * ROWS]
+
+        twins = HEADS // 2
         differ(0)
-        for h in range(HEADS + 1):
-            if h + 1 < HEADS:
-                differ(h + 1)
-            if h >= 1:
-                spend(h - 1)
-            if h < HEADS:
-                weigh(h)
+        for t in range(twins + 1):
+            if t + 1 < twins:
+                differ(t + 1)
+            if t >= 1:
+                spend(t - 1)
+            if t < twins:
+                weigh(t)
 
     @pl.when(step == frames - 1)
     def _():
@@ -735,13 +743,13 @@
         pad(pack_matrix(own2_ref, cut2, late), own2_ref.shape[0])
         four.send(0)
 
-    at(norm_step + 1, (four.take, 0), (four.send, 1))
-    at(norm_step + 3, (one.settle, 0), (two.settle, 1), (two.spread, 0))
-    at(norm_step + 4, (three.take, 1), (three.send, 2))
-
-    @pl.when(step == norm_step + 5)
-    def _():
-        two.settle(0)
+    at(norm_step + 1, (four.take, 0), (four.send, 1), (one.settle, 1), (one.spread, 0))
+    at(norm_step + 4, (three.take, 1), (three.send, 2), (two.settle, 1), (two.spread, 0))
+
+    @pl.when(step == norm_step + 6)
+    def _():
+        for total in (one, two, side):
+            total.settle(0)
         keep.start()
 
     at(norm_step + 7, (four.take, 1), (four.send, 2))
@@ -893,7 +901,7 @@
         grid=(steps,),
         in_specs=[
             pl.BlockSpec(memory_space=pltpu.SMEM),
-            whole((count, width)),
+            in_hbm,
             whole((ROWS, width)),
             whole((width,)),
             whole((width,)),
@@ -913,10 +921,10 @@
             in_hbm,
             in_hbm,
             in_hbm,
-            pairs((HEADS, ROWS, WIN)),
+            pairs((HEADS // 2, 2 * ROWS, WIN)),
             pl.BlockSpec((4 * FRAME, width), lambda i: (i // 2, 0)),
             pairs((ROWS, width)),
-            pairs((ROWS, 2 * width)),
+            pairs((HEADS // 2, 2 * ROWS, 128 + EXTRA)),
             pairs((ROWS, width)),
             pairs((ROWS, width)),
             pairs((ROWS, width)),
@@ -927,10 +935,10 @@
             shape((frames, ROWS, width), bf16),
             shape((frames, ROWS, width), bf16),
             shape((kv_rows, 2 * width), bf16),
-            shape((frames, HEADS, ROWS, WIN), bf16),
+            shape((frames, HEADS // 2, 2 * ROWS, WIN), bf16),
             shape((count, width), bf16),
             shape((frames, ROWS, width), bf16),
-            shape((frames, ROWS, 2 * width), bf16),
+            shape((frames, HEADS // 2, 2 * ROWS, 128 + EXTRA), bf16),
             shape((frames, ROWS, width), bf16),
             shape((frames, ROWS, width), f32),
             shape((frames, ROWS, width), f32),
@@ -948,7 +956,7 @@
             pltpu.VMEM((frames, ROWS, width), bf16),
             pltpu.VMEM((frames, ROWS, width), bf16),
             pltpu.VMEM((kv_rows, 128), bf16),
-            pltpu.VMEM((3, ROWS, WIN), f32),
+            pltpu.VMEM((3, 2 * ROWS, WIN), f32),
             pltpu.VMEM((2 * ROWS, width), f32),
             pltpu.VMEM((4 * FRAME, width), f32),
             pltpu.VMEM((width, hidden), f32),
@@ -956,22 +964,22 @@
             pltpu.VMEM((width, width), f32),
             pltpu.VMEM((8, hidden), f32),
             pltpu.VMEM((4, 8, width), f32),
-            pltpu.SemaphoreType.DMA((7,)),
+            pltpu.SemaphoreType.DMA((8,)),
         ],
         compiler_params=params(),
     )(frame_clip, tokens, ghost, ln1_gain, ln1_bias, qv_bias, b_out, ln2_gain, ln2_bias, b_fc1, b_fc2, w_qkv, cotangent,
       w_out, w_fc1, w_fc2)
 
-    first, second = halves(units, devices)
+    first, second, side = shares(units, devices)
     early = lambda sh: pl.BlockSpec((1,) + sh, lambda i: (jnp.minimum(i, frames - 1),) + (0,) * len(sh))
     late = lambda i: jnp.maximum(i - frames - 1, 0)
     input_grad, res, res2, sums = pl.pallas_call(
         functools.partial(back_kernel, stages),
         grid=(frames + 1 + steps,),
         in_specs=[
-            early((HEADS, ROWS, WIN)),
-            in_hbm,
-            early((ROWS, 2 * width)),
+            early((HEADS // 2, 2 * ROWS, WIN)),
+            in_hbm,
+            early((HEADS // 2, 2 * ROWS, 128 + EXTRA)),
             early((ROWS, width)),
             early((ROWS, width)),
             early((ROWS, width)),
@@ -996,8 +1004,8 @@
         ],
         scratch_shapes=[
             pltpu.VMEM((kv_rows, 2 * width), f32),
-            pltpu.VMEM((3, ROWS, WIN), f32),
-            pltpu.VMEM((3, ROWS, WIN), bf16),
+            pltpu.VMEM((3, 2 * ROWS, WIN), f32),
+            pltpu.VMEM((3, 2 * ROWS, WIN), bf16),
             pltpu.VMEM((frames * ROWS, width), bf16),
             pltpu.VMEM((8, 3 * width), f32),
             pltpu.VMEM((2, 8, width), f32),
@@ -1016,6 +1024,7 @@
         ]
         + sum_scratch(stages, first)
         + sum_scratch(stages, second)
+        + sum_scratch(turned(stages), side)
         + sum_scratch(stages, first2)
         + sum_scratch(stages, second2)
         + rows_scratch(stages),

time: 171 us -> 168 us (0.982)
  Pallas kernels: 167 us -> 164 us
    pallas_call x1, Pallas kernels: 78 us -> 75.2 us  [per_device(): pl.pallas_call(functools.partial(back_kernel, stages), grid=(frames + 1 +...]
where the time goes in v6:
time: 168 us
  Pallas kernels  164 us (98%)
    pallas_call x1, Pallas kernels, per_device(): pl.pallas_call(forward_kernel, grid=(steps,), in_specs=[pl.BlockSpec(memo...  79.2 us
    pallas_call x1, Pallas kernels, per_device(): pl.pallas_call(functools.partial(back_kernel, stages), grid=(frames + 1 +...  75.2 us
    pallas_call x1, Pallas kernels, per_device(): pl.pallas_call(functools.partial(unpack_kernel, first2), in_specs=[in_hbm...  9.57 us
  transfers between devices with their start and end apart: 1, of which 1 were waited for; matrix products, arithmetic and copies ran while one was open for 0% of the time, Pallas kernels for 0%

profile of v6, /device:TPU:0, one launch (start us, length us, event | category | flops | bytes accessed | tf_op | source)
XLA Modules:
  0.0 168.0 jit_solution(12782629311756402125)
XLA Ops:
  0.6 1.0 slice_select_fusion
  1.7 0.5 collective-permute-start
  2.2 1.0 collective-permute-done.ghost_ref
  3.2 0.0 copy-start
  3.2 0.7 copy-done
  3.9 79.2 %shard_map.254 = (bf16[16,208,384]{2,1,0:T(8,128)(2,1)}, bf16[16,208,384]{2,1,0:T(8,128)(2,1)}, bf16[3760,768]{1,0:T(8,128)(2,1)}, bf16[16,3,416,640]{3,2,1,0:T(...) custom-call(s32[32]{0:T(128)} %clip_ref.1, ...), custom_call_target="tpu_custom_call" | custom-call | tf_op jit(solution)/shard_map/pallas_call | solution.py:899
  83.1 75.2 %shard_map.255 = (f32[3136,384]{1,0:T(8,128)}, bf16[672,16,128]{2,1,0:T(8,128)(2,1)}, bf16[224,16,128]{2,1,0:T(8,128)(2,1)}, f32[16,128]{1,0:T(8,128)}) custom-call(bf16[16,3,416,640]{3,2,1,0:T(8,128)(2,1)} %get-tuple-element.44.prob_ref, bf16[3760,768]{1,0:T(8,128)(2,1)} %get-tuple-element.45.kv_hbm, bf16[16,3,416,144]{3,2,1,0:T(8,128)(2,1)} %get-tuple-element.46.ga_ref, ...), custom_call_target="tpu_custom_call" | custom-call | tf_op jit(solution)/shard_map/pallas_call | solution.py:976
  158.3 9.6 %shard_map.256 = (f32[3136,384]{1,0:T(8,128)}, f32[384]{0:T(512)}, f32[384]{0:T(512)}, f32[384,1152]{1,0:T(8,128)}, f32[2,384]{1,0:T(2,128)}, /*index=5*/f32[384...) custom-call(f32[3136,384]{1,0:T(8,128)} %get-tuple-element.55.in_hbm, ...), custom_call_target="tpu_custom_call" | custom-call | tf_op jit(solution)/shard_map/pallas_call | solution.py:1037
Async XLA Ops:
  1.7 1.5 collective-permute-start
  3.2 0.7 copy-start

commit v7 on v6

--- a/solution.py
+++ b/solution.py
@@ -614,16 +614,18 @@
 
     @pl.when(step == 0)
     def _():
-        for load in loads:
+        for load in loads[:2]:
             load.start()
         greet(stages)
-        acc_ref[: 2 * ROWS] = jnp.zeros((2 * ROWS, 2 * width), f32)
-        sq_ref[...] = jnp.zeros_like(sq_ref)
-        s384_ref[...] = jnp.zeros_like(s384_ref)
         loads[0].wait()
         one.send(0)
         side.send(0)
         two.send(0)
+        for load in loads[2:]:
+            load.start()
+        acc_ref[: 2 * ROWS] = jnp.zeros((2 * ROWS, 2 * width), f32)
+        sq_ref[...] = jnp.zeros_like(sq_ref)
+        s384_ref[...] = jnp.zeros_like(s384_ref)
         loads[1].wait()
 
     @pl.when(step == 1)
@@ -814,8 +816,11 @@
         pltpu.make_async_copy(src, dst, sems.at[3 + i])
         for i, (src, dst) in enumerate(((gqkv, gqkv_hbm), (gwo, gwo_hbm), (gw1, gw1_hbm), (gw2, gw2_hbm)))
     ]
-    for copy in loads + come:
+    for copy in come + loads:
         copy.start()
+    for i in range(pieces):
+        come[i].wait()
+        go[i].start()
     early = 3 * width // 128 // 2
     for c in range(3 * width // 128):
         at = c * tiles if c < early else cut2 + (c - early) * tiles
@@ -827,9 +832,6 @@
         gw1[:, 128 * c : 128 * c + 128] = res_ref[at : at + tiles].reshape(width, 128).astype(f32)
         at += tiles
     stores[2].start()
-    for i in range(pieces):
-        come[i].wait()
-        go[i].start()
     loads[1].wait()
     for c in range(hidden // 128):
         gw2[128 * c : 128 * c + 128, :] = res_ref[at : at + tiles].reshape(width, 128).astype(f32).T

time: 168 us -> 168 us (level)
  no operation moved by 1% of the time
where the time goes in v7:
time: 168 us; the launch traced here: 167 us
  Pallas kernels  163 us (97%)
    pallas_call x1, Pallas kernels, per_device(): pl.pallas_call(forward_kernel, grid=(steps,), in_specs=[pl.BlockSpec(memo...  79.2 us
    pallas_call x1, Pallas kernels, per_device(): pl.pallas_call(functools.partial(back_kernel, stages), grid=(frames + 1 +...  75.1 us
    pallas_call x1, Pallas kernels, per_device(): pl.pallas_call(functools.partial(unpack_kernel, first2), in_specs=[in_hbm...  8.97 us
  transfers between devices with their start and end apart: 1, of which 1 were waited for; matrix products, arithmetic and copies ran while one was open for 0% of the time, Pallas kernels for 0%

profile of v7, /device:TPU:0, one launch (start us, length us, event | category | flops | bytes accessed | tf_op | source)
XLA Modules:
  0.0 167.3 jit_solution(9987603714419202400)
XLA Ops:
  0.6 1.0 slice_select_fusion
  1.7 0.5 collective-permute-start
  2.2 1.0 collective-permute-done.ghost_ref
  3.2 0.0 copy-start
  3.2 0.7 copy-done
  3.9 79.2 %shard_map.254 = (bf16[16,208,384]{2,1,0:T(8,128)(2,1)}, bf16[16,208,384]{2,1,0:T(8,128)(2,1)}, bf16[3760,768]{1,0:T(8,128)(2,1)}, bf16[16,3,416,640]{3,2,1,0:T(...) custom-call(s32[32]{0:T(128)} %clip_ref.1, ...), custom_call_target="tpu_custom_call" | custom-call | tf_op jit(solution)/shard_map/pallas_call | solution.py:901
  83.1 75.1 %shard_map.255 = (f32[3136,384]{1,0:T(8,128)}, bf16[672,16,128]{2,1,0:T(8,128)(2,1)}, bf16[224,16,128]{2,1,0:T(8,128)(2,1)}, f32[16,128]{1,0:T(8,128)}) custom-call(bf16[16,3,416,640]{3,2,1,0:T(8,128)(2,1)} %get-tuple-element.44.prob_ref, bf16[3760,768]{1,0:T(8,128)(2,1)} %get-tuple-element.45.kv_hbm, bf16[16,3,416,144]{3,2,1,0:T(8,128)(2,1)} %get-tuple-element.46.ga_ref, ...), custom_call_target="tpu_custom_call" | custom-call | tf_op jit(solution)/shard_map/pallas_call | solution.py:978
  158.2 9.0 %shard_map.256 = (f32[3136,384]{1,0:T(8,128)}, f32[384]{0:T(512)}, f32[384]{0:T(512)}, f32[384,1152]{1,0:T(8,128)}, f32[2,384]{1,0:T(2,128)}, /*index=5*/f32[384...) custom-call(f32[3136,384]{1,0:T(8,128)} %get-tuple-element.55.in_hbm, ...), custom_call_target="tpu_custom_call" | custom-call | tf_op jit(solution)/shard_map/pallas_call | solution.py:1039
Async XLA Ops:
  1.7 1.5 collective-permute-start
  3.2 0.7 copy-start

commit v8 on v7

--- a/solution.py
+++ b/solution.py
@@ -904,7 +904,7 @@
         in_specs=[
             pl.BlockSpec(memory_space=pltpu.SMEM),
             in_hbm,
-            whole((ROWS, width)),
+            in_vmem,
             whole((width,)),
             whole((width,)),
             whole((2, width)),

time: 168 us -> 168 us (level)
  no operation moved by 1% of the time
where the time goes in v8:
time: 168 us; the launch traced here: 167 us
  Pallas kernels  163 us (97%)
    pallas_call x1, Pallas kernels, per_device(): pl.pallas_call(forward_kernel, grid=(steps,), in_specs=[pl.BlockSpec(memo...  79.2 us
    pallas_call x1, Pallas kernels, per_device(): pl.pallas_call(functools.partial(back_kernel, stages), grid=(frames + 1 +...  75.1 us
    pallas_call x1, Pallas kernels, per_device(): pl.pallas_call(functools.partial(unpack_kernel, first2), in_specs=[in_hbm...  8.97 us
  transfers between devices with their start and end apart: 1, of which 1 were waited for; matrix products, arithmetic and copies ran while one was open for 0% of the time, Pallas kernels for 0%

profile of v8, /device:TPU:0, one launch (start us, length us, event | category | flops | bytes accessed | tf_op | source)
XLA Modules:
  0.0 167.3 jit_solution(9987603714419202400)
XLA Ops:
  0.6 1.0 slice_select_fusion
  1.7 0.5 collective-permute-start
  2.2 1.0 collective-permute-done.ghost_ref
  3.2 0.0 copy-start
  3.2 0.7 copy-done
  3.9 79.2 %shard_map.254 = (bf16[16,208,384]{2,1,0:T(8,128)(2,1)}, bf16[16,208,384]{2,1,0:T(8,128)(2,1)}, bf16[3760,768]{1,0:T(8,128)(2,1)}, bf16[16,3,416,640]{3,2,1,0:T(...) custom-call(s32[32]{0:T(128)} %clip_ref.1, ...), custom_call_target="tpu_custom_call" | custom-call | tf_op jit(solution)/shard_map/pallas_call | solution.py:901
  83.1 75.1 %shard_map.255 = (f32[3136,384]{1,0:T(8,128)}, bf16[672,16,128]{2,1,0:T(8,128)(2,1)}, bf16[224,16,128]{2,1,0:T(8,128)(2,1)}, f32[16,128]{1,0:T(8,128)}) custom-call(bf16[16,3,416,640]{3,2,1,0:T(8,128)(2,1)} %get-tuple-element.44.prob_ref, bf16[3760,768]{1,0:T(8,128)(2,1)} %get-tuple-element.45.kv_hbm, bf16[16,3,416,144]{3,2,1,0:T(8,128)(2,1)} %get-tuple-element.46.ga_ref, ...), custom_call_target="tpu_custom_call" | custom-call | tf_op jit(solution)/shard_map/pallas_call | solution.py:978
  158.2 9.0 %shard_map.256 = (f32[3136,384]{1,0:T(8,128)}, f32[384]{0:T(512)}, f32[384]{0:T(512)}, f32[384,1152]{1,0:T(8,128)}, f32[2,384]{1,0:T(2,128)}, /*index=5*/f32[384...) custom-call(f32[3136,384]{1,0:T(8,128)} %get-tuple-element.55.in_hbm, ...), custom_call_target="tpu_custom_call" | custom-call | tf_op jit(solution)/shard_map/pallas_call | solution.py:1039
Async XLA Ops:
  1.7 1.5 collective-permute-start
  3.2 0.7 copy-start
